TPU v7x, 32 devices: a whole 2x2x4 slice. The times are simulated.
32 devices in a mesh: seq: 16 (over z, x, core), mp: 2 (over y).
Axes of the slice: x: 2, y: 2, z: 4, core: 2. Of those that a mesh axis runs over, the one named last changes fastest.
Arguments:
- acoustic_features: bfloat16 [16384, 1024], P('seq'), may hold values from -6 to 6
- clip_durations: int32 [32], replicated, may hold values from 1 to 3008, as said below
- early_layernorm_scale: float32 [1024], replicated, may hold values from 0.25 to 1.75
- early_widening_matrix: bfloat16 [1024, 4096], P(None, 'mp'), may hold values from -0.1875 to 0.1875
- early_narrowing_matrix: bfloat16 [4096, 1024], P('mp'), may hold values from -0.09375 to 0.09375
- mixer_layernorm_scale: float32 [1024], replicated, may hold values from 0.25 to 1.75
- triple_matrix: bfloat16 [3, 1024, 1024], P(None, None, 'mp'), may hold values from -0.25 to 0.25
- mixer_exit_matrix: bfloat16 [1024, 1024], P('mp'), may hold values from -0.75 to 0.75
- filter_layernorm_scale: float32 [1024], replicated, may hold values from 0.25 to 1.75
- gating_pair_matrix: bfloat16 [2, 1024, 1024], P(None, None, 'mp'), may hold values from -0.1875 to 0.1875
- depthwise_filter: float32 [5, 1024], P(None, 'mp'), may hold values from -6 to 6
- running_stats_factor: float32 [1024], P('mp'), may hold values from 0.25 to 1.75
- running_stats_offset: float32 [1024], P('mp'), may hold values from -3 to 3
- filter_exit_projection: bfloat16 [1024, 1024], P('mp'), may hold values from -0.1875 to 0.1875
- later_layernorm_scale: float32 [1024], replicated, may hold values from 0.25 to 1.75
- later_widening_matrix: bfloat16 [1024, 4096], P(None, 'mp'), may hold values from -0.1875 to 0.1875
- later_narrowing_matrix: bfloat16 [4096, 1024], P('mp'), may hold values from -0.09375 to 0.09375
- last_layernorm_scale: float32 [1024], replicated, may hold values from 0.25 to 1.75
- quantizer_projection: bfloat16 [1024, 1024], P(None, 'mp'), may hold values from -0.1875 to 0.1875
- entry_vectors: bfloat16 [1024, 1024], P('mp'), may hold values from -6 to 6
- smoothing_level: float32 [1], replicated, may hold values from 0.5 to 2
- random_flat_samples: float32 [16384, 1024], P('seq', 'mp'), may hold values from 0.02 to 0.98
- expected_entries: int32 [16384], P('seq'), may hold values from 0 to 1023
- result_adjoint: bfloat16 [16384, 1024], P('seq'), may hold values from -6 to 6
- discrete_adjoint: bfloat16 [16384, 1024], P('seq'), may hold values from -6 to 6
Outputs:
- layer_out: bfloat16 [16384, 1024], P('seq')
- quantized: bfloat16 [16384, 1024], P('seq')
- frame_loss: float32 [16384], P('seq')
- grad_frames: bfloat16 [16384, 1024], P('seq')
- grad_ln_ffn1: float32 [1024], replicated
- grad_up1: float32 [1024, 4096], P(None, 'mp')
- grad_down1: float32 [4096, 1024], P('mp')
- grad_ln_att: float32 [1024], replicated
- grad_qkv: float32 [3, 1024, 1024], P(None, None, 'mp')
- grad_out: float32 [1024, 1024], P('mp')
- grad_ln_conv: float32 [1024], replicated
- grad_glu: float32 [2, 1024, 1024], P(None, None, 'mp')
- grad_kernel: float32 [5, 1024], P(None, 'mp')
- grad_bn_gain: float32 [1024], P('mp')
- grad_bn_bias: float32 [1024], P('mp')
- grad_point: float32 [1024, 1024], P('mp')
- grad_ln_ffn2: float32 [1024], replicated
- grad_up2: float32 [1024, 4096], P(None, 'mp')
- grad_down2: float32 [4096, 1024], P('mp')
- grad_ln_final: float32 [1024], replicated
- grad_w_code: float32 [1024, 1024], P(None, 'mp')
- grad_codebook: float32 [1024, 1024], P('mp')
- grad_temperature: float32 [1], replicated
Inputs may be any that keep to these rules, and one draw needn't show every extreme that they name: `clip_durations`: the lengths sum to 16384; no clip has more than 3008 frames, and at least one clip has exactly 3008.
All inputs are finite; a program needn't handle non-finite values.
Results may differ from a plain program's by a relative error of at most 0.033.
Values may be sent and summed in bfloat16 or wider, within the bound.
A program may use at most 320 MiB of HBM per device.

v0:
```python
import jax
import jax.numpy as jnp
from jax import lax
from jax.sharding import PartitionSpec as P

D = 1024
HEAD = 128
KERNEL = 5


EPSILON = 1e-05
MASKED = -1e30
REACHES = (1, 2, 3, -1, -2, -3)


def shortened(shard):
    return jax.tree.map(lambda a: a.astype(jnp.bfloat16) if a.dtype == jnp.float32 else a, shard)


def merged(shard, axis, combine):
    everything = jax.tree.map(lambda part: lax.all_gather(part, axis), shard)
    initial = jax.tree.map(lambda part: part[0], everything)

    def hop(k, so_far):
        return combine(so_far, jax.tree.map(lambda part: part[k], everything))

    return lax.fori_loop(1, lax.axis_size(axis), hop, initial)


def shifted(shard, axis, by):
    count = lax.axis_size(axis)
    pairs = [(i, i + by) for i in range(count) if 0 <= i + by < count]
    return lax.ppermute(shard, axis, pairs)


def padded(block, sides, width):
    for axis, dim in sides:
        count = lax.axis_size(axis)
        forward = [(i, i + 1) for i in range(count - 1)]
        backward = [(target, source) for source, target in forward]
        low = lax.ppermute(
            lax.slice_in_dim(block, block.shape[dim] - width, None, axis=dim), axis, forward
        )
        high = lax.ppermute(lax.slice_in_dim(block, 0, width, axis=dim), axis, backward)
        block = jnp.concatenate([low, block, high], axis=dim)
    return block


def clip_of(clip_durations, positions):
    clip_ends = jnp.cumsum(clip_durations, dtype=jnp.int32)
    passed = clip_ends[None, :] <= positions[:, None]
    segment = jnp.sum(passed.astype(jnp.int32), 1, dtype=jnp.int32)
    starts = jnp.sum(jnp.where(passed, clip_durations[None, :], 0), 1, dtype=jnp.int32)
    return (segment, positions - starts)


def piece_segments(clip_durations, offset, frame_rows, reach, all_rows):
    index = offset - reach * frame_rows + jnp.arange(frame_rows, dtype=jnp.int32)
    segment, unused_pos = clip_of(clip_durations, index)
    return jnp.where(jnp.logical_and(index >= 0, index < all_rows), segment, -1)


def norm_forward(layer_operands, norm_gain):
    centred = layer_operands - jnp.mean(layer_operands, -1, keepdims=True)
    inverse = lax.rsqrt(jnp.mean(centred * centred, -1, keepdims=True) + EPSILON)
    normed = centred * inverse
    return (normed * norm_gain, normed, inverse)


def norm_backward(upstream, norm_gain, normed, inverse):
    scaled = upstream * norm_gain
    centred_grad = (
        scaled
        - jnp.mean(scaled, -1, keepdims=True)
        - normed * jnp.mean(scaled * normed, -1, keepdims=True)
    )
    return (centred_grad * inverse, jnp.sum(upstream * normed, 0))


def rotary(heads_in, position, direction):
    half_width = heads_in.shape[-1] // 2
    frequency = 10000.0 ** (-jnp.arange(half_width, dtype=jnp.float32) / half_width)
    angles = position.astype(jnp.float32)[:, None] * frequency[None, :]
    cosine = jnp.cos(angles)[:, None, :]
    sine_part = direction * jnp.sin(angles)[:, None, :]
    leading = heads_in[..., :half_width]
    trailing = heads_in[..., half_width:]
    return jnp.concatenate(
        [leading * cosine - trailing * sine_part, leading * sine_part + trailing * cosine], -1
    )


def silu_slope(hidden, sigma):
    return sigma * (1.0 + hidden * (1.0 - sigma))


def model_total(partial_terms):
    return jax.tree.map(
        lambda part: part.astype(jnp.float32), lax.psum(shortened(partial_terms), "mp")
    )


def code_combine(first_part, second_part):
    row_top = jnp.maximum(first_part[0], second_part[0])
    row_total = first_part[1] * jnp.exp(first_part[0] - row_top) + second_part[1] * jnp.exp(
        second_part[0] - row_top
    )
    return (row_top, row_total, first_part[2] + second_part[2])


def code_softmax(logits, picked_part):
    row_top = jnp.max(logits, -1)
    row_total = jnp.sum(jnp.exp(logits - row_top[:, None]), -1)
    row_top, row_total, picked = merged((row_top, row_total, picked_part), "mp", code_combine)
    return (row_top + jnp.log(row_total), picked)


def block_scores(queries, keys_block, query_seg, key_seg):
    scores = jnp.einsum(
        "qhd,khd->hqk", queries, keys_block, preferred_element_type=jnp.float32
    ) * HEAD ** (-0.5)
    return jnp.where(query_seg[None, :, None] == key_seg[None, None, :], scores, MASKED)


def ffn_forward(layer_operands, norm_gain, w_in, w_back):
    normal_out, normed, inverse = norm_forward(layer_operands, norm_gain)
    entered = normal_out.astype(jnp.bfloat16)
    hidden = jnp.dot(entered, w_in, preferred_element_type=jnp.float32)
    sigma = jax.nn.sigmoid(hidden)
    activated = (hidden * sigma).astype(jnp.bfloat16)
    partial_out = jnp.dot(activated, w_back, preferred_element_type=jnp.float32)
    return (partial_out, (normed, inverse, entered, hidden, sigma, activated))


def ffn_backward(upstream, w_in, w_back, saved):
    normed, inverse, entered, hidden, sigma, activated = saved
    grad_branch = (0.5 * upstream).astype(jnp.bfloat16)
    grad_back = jnp.dot(activated.T, grad_branch, preferred_element_type=jnp.float32)
    grad_act = jnp.dot(grad_branch, w_back.T, preferred_element_type=jnp.float32)
    grad_hidden = (grad_act * silu_slope(hidden, sigma)).astype(jnp.bfloat16)
    grad_in = jnp.dot(entered.T, grad_hidden, preferred_element_type=jnp.float32)
    partial_in = jnp.dot(grad_hidden, w_in.T, preferred_element_type=jnp.float32)
    return (partial_in, grad_in, grad_back)


def on_device(
    acoustic_features,
    clip_durations,
    early_layernorm_scale,
    early_widening_matrix,
    early_narrowing_matrix,
    mixer_layernorm_scale,
    triple_matrix,
    mixer_exit_matrix,
    filter_layernorm_scale,
    gating_pair_matrix,
    depthwise_filter,
    running_stats_factor,
    running_stats_offset,
    filter_exit_projection,
    later_layernorm_scale,
    later_widening_matrix,
    later_narrowing_matrix,
    last_layernorm_scale,
    quantizer_projection,
    entry_vectors,
    smoothing_level,
    random_flat_samples,
    expected_entries,
    result_adjoint,
    discrete_adjoint,
):
    frame_rows = acoustic_features.shape[0]
    all_rows = frame_rows * lax.axis_size("seq")
    offset = lax.axis_index("seq") * frame_rows
    local_index = offset + jnp.arange(frame_rows, dtype=jnp.int32)
    local_seg, local_pos = clip_of(clip_durations, local_index)
    layer_operands = acoustic_features.astype(jnp.float32)
    smoothing_coefficient = smoothing_level[0]
    code_count = quantizer_projection.shape[1]
    code_first = lax.axis_index("mp") * code_count
    code_logits = jnp.dot(
        acoustic_features, quantizer_projection, preferred_element_type=jnp.float32
    )
    noisy_entry_scores = code_logits - jnp.log(-jnp.log(random_flat_samples))
    tempered_scores = noisy_entry_scores / smoothing_coefficient
    code_lse, unused_pick = code_softmax(tempered_scores, jnp.zeros((frame_rows,), jnp.float32))
    smooth_assignments = jnp.exp(tempered_scores - code_lse[:, None])
    soft_low = smooth_assignments.astype(jnp.bfloat16)
    quant_part = jnp.dot(soft_low, entry_vectors, preferred_element_type=jnp.float32)
    part_one, saved_one = ffn_forward(
        layer_operands, early_layernorm_scale, early_widening_matrix, early_narrowing_matrix
    )
    ffn_total, quant_total = model_total((part_one, quant_part))
    after_ffn = layer_operands + 0.5 * ffn_total
    att_norm, att_normed, att_inverse = norm_forward(after_ffn, mixer_layernorm_scale)
    att_entered = att_norm.astype(jnp.bfloat16)
    projected = jnp.einsum(
        "td,sde->tse", att_entered, triple_matrix, preferred_element_type=jnp.float32
    )
    local_width = triple_matrix.shape[2]
    head_count = local_width // HEAD
    shaped = projected.reshape(frame_rows, 3, head_count, HEAD)
    query_rot = rotary(shaped[:, 0], local_pos, 1.0).astype(jnp.bfloat16)
    key_rot = rotary(shaped[:, 1], local_pos, 1.0).astype(jnp.bfloat16)
    value_low = shaped[:, 2].astype(jnp.bfloat16)
    kv_own = jnp.stack([key_rot, value_low], 1)
    kv_pieces = [kv_own]
    seg_pieces = [local_seg]
    for reach in REACHES:
        kv_pieces.append(shifted(kv_own, "seq", reach))
        seg_pieces.append(piece_segments(clip_durations, offset, frame_rows, reach, all_rows))
    kv_stack = jnp.stack(kv_pieces, 0)
    seg_stack = jnp.stack(seg_pieces, 0)
    key_stack = kv_stack[:, :, 0]
    value_stack = kv_stack[:, :, 1]

    def guarded(step_fn):

        def run_step(carry_in, block):
            return step_fn(carry_in, block)

        return run_step

    def lse_step(carry_in, block):
        scores = block_scores(query_rot, block[0], local_seg, block[1])
        new_top = jnp.maximum(carry_in[0], jnp.max(scores, -1))
        summed = carry_in[1] * jnp.exp(carry_in[0] - new_top) + jnp.sum(
            jnp.exp(scores - new_top[..., None]), -1
        )
        return ((new_top, summed), None)

    start_top = jnp.full((head_count, frame_rows), MASKED, jnp.float32)
    start_sum = jnp.zeros((head_count, frame_rows), jnp.float32)
    (row_top, row_sum), unused_out = lax.scan(
        guarded(lse_step), (start_top, start_sum), (key_stack, seg_stack)
    )
    row_lse = row_top + jnp.log(row_sum)

    def out_step(carry_in, block):
        scores = block_scores(query_rot, block[0], local_seg, block[2])
        probs = jnp.exp(scores - row_lse[..., None])
        return (
            carry_in
            + jnp.einsum(
                "hqk,khd->qhd",
                probs.astype(jnp.bfloat16),
                block[1],
                preferred_element_type=jnp.float32,
            ),
            None,
        )

    start_mix = jnp.zeros((frame_rows, head_count, HEAD), jnp.float32)
    mixed_out, unused_out = lax.scan(
        guarded(out_step), start_mix, (key_stack, value_stack, seg_stack)
    )
    att_low = mixed_out.reshape(frame_rows, local_width).astype(jnp.bfloat16)
    att_part = jnp.dot(att_low, mixer_exit_matrix, preferred_element_type=jnp.float32)
    after_att = after_ffn + model_total(att_part)
    half_kernel = KERNEL // 2
    conv_norm, conv_normed, conv_inverse = norm_forward(after_att, filter_layernorm_scale)
    conv_entered = conv_norm.astype(jnp.bfloat16)
    glu_pair = jnp.einsum(
        "td,sde->tse", conv_entered, gating_pair_matrix, preferred_element_type=jnp.float32
    )
    glu_value = glu_pair[:, 0]
    glu_gate = jax.nn.sigmoid(glu_pair[:, 1])
    glu_low = (glu_value * glu_gate).astype(jnp.bfloat16)
    glu_padded = padded(glu_low, (("seq", 0),), half_kernel).astype(jnp.float32)
    pad_index = offset - half_kernel + jnp.arange(frame_rows + 2 * half_kernel, dtype=jnp.int32)
    pad_seg, unused_pad = clip_of(clip_durations, pad_index)
    pad_seg = jnp.where(jnp.logical_and(pad_index >= 0, pad_index < all_rows), pad_seg, -1)
    conv_out = jnp.zeros((frame_rows, glu_low.shape[1]), jnp.float32)
    for tap_index in range(KERNEL):
        matches = (pad_seg[tap_index : tap_index + frame_rows] == local_seg)[:, None]
        conv_out = conv_out + depthwise_filter[tap_index][None, :] * jnp.where(
            matches, glu_padded[tap_index : tap_index + frame_rows], 0.0
        )
    first_sum, square_sum = lax.psum((jnp.sum(conv_out, 0), jnp.sum(conv_out * conv_out, 0)), "seq")
    bn_mean = first_sum / all_rows
    bn_inv = lax.rsqrt(square_sum / all_rows - bn_mean * bn_mean + EPSILON)
    bn_hat = (conv_out - bn_mean) * bn_inv
    bn_out = bn_hat * running_stats_factor + running_stats_offset
    bn_sigma = jax.nn.sigmoid(bn_out)
    swish_low = (bn_out * bn_sigma).astype(jnp.bfloat16)
    conv_part = jnp.dot(swish_low, filter_exit_projection, preferred_element_type=jnp.float32)
    after_conv = after_att + model_total(conv_part)
    part_two, saved_two = ffn_forward(
        after_conv, later_layernorm_scale, later_widening_matrix, later_narrowing_matrix
    )
    after_two = after_conv + 0.5 * model_total(part_two)
    final_norm, final_normed, final_inverse = norm_forward(after_two, last_layernorm_scale)
    final_low = final_norm.astype(jnp.bfloat16)
    pred_logits = jnp.dot(final_low, entry_vectors.T, preferred_element_type=jnp.float32) * D ** (
        -0.5
    )
    is_target = (
        expected_entries[:, None] - code_first == jnp.arange(code_count, dtype=jnp.int32)[None, :]
    )
    picked_part = jnp.sum(jnp.where(is_target, pred_logits, 0.0), -1)
    pred_lse, picked = code_softmax(pred_logits, picked_part)
    row_loss = pred_lse - picked
    grad_pred = (jnp.exp(pred_logits - pred_lse[:, None]) - is_target.astype(jnp.float32)).astype(
        jnp.bfloat16
    )
    pred_in_part = jnp.dot(grad_pred, entry_vectors, preferred_element_type=jnp.float32) * D ** (
        -0.5
    )
    grad_book = jnp.dot(grad_pred.T, final_low, preferred_element_type=jnp.float32) * D ** (-0.5)
    grad_soft = jnp.dot(discrete_adjoint, entry_vectors.T, preferred_element_type=jnp.float32)
    row_dot, weighted_a, weighted_b = lax.psum(
        (
            jnp.sum(smooth_assignments * grad_soft, -1),
            jnp.sum(smooth_assignments * grad_soft * noisy_entry_scores, -1),
            jnp.sum(smooth_assignments * noisy_entry_scores, -1),
        ),
        "mp",
    )
    derivative_tempered = smooth_assignments * (grad_soft - row_dot[:, None])
    derivative_entry_scores = (derivative_tempered / smoothing_coefficient).astype(jnp.bfloat16)
    grad_w_code = jnp.dot(
        acoustic_features.T, derivative_entry_scores, preferred_element_type=jnp.float32
    )
    quant_in_part = jnp.dot(
        derivative_entry_scores, quantizer_projection.T, preferred_element_type=jnp.float32
    )
    grad_book = grad_book + jnp.dot(
        soft_low.T, discrete_adjoint, preferred_element_type=jnp.float32
    )
    grad_temper = -jnp.sum(weighted_a - row_dot * weighted_b) / (
        smoothing_coefficient * smoothing_coefficient
    )
    grad_final = result_adjoint.astype(jnp.float32) + model_total(pred_in_part)
    grad_four, grad_ln_final = norm_backward(
        grad_final, last_layernorm_scale, final_normed, final_inverse
    )
    in_part_two, grad_up2, grad_down2 = ffn_backward(
        grad_four, later_widening_matrix, later_narrowing_matrix, saved_two
    )
    norm_two_grad, grad_ln_ffn2 = norm_backward(
        model_total(in_part_two), later_layernorm_scale, saved_two[0], saved_two[1]
    )
    grad_three = grad_four + norm_two_grad
    grad_conv_branch = grad_three.astype(jnp.bfloat16)
    grad_point = jnp.dot(swish_low.T, grad_conv_branch, preferred_element_type=jnp.float32)
    grad_swish = jnp.dot(
        grad_conv_branch, filter_exit_projection.T, preferred_element_type=jnp.float32
    )
    grad_bn = grad_swish * silu_slope(bn_out, bn_sigma)
    grad_bn_bias, grad_bn_gain = lax.psum(
        (jnp.sum(grad_bn, 0), jnp.sum(grad_bn * bn_hat, 0)), "seq"
    )
    grad_conv = (
        running_stats_factor
        * bn_inv
        * (grad_bn - grad_bn_bias / all_rows - bn_hat * grad_bn_gain / all_rows)
    )
    grad_conv_low = grad_conv.astype(jnp.bfloat16)
    grad_conv_pad = padded(grad_conv_low, (("seq", 0),), half_kernel).astype(jnp.float32)
    grad_conv_exact = grad_conv_low.astype(jnp.float32)
    grad_taps = []
    grad_gated = jnp.zeros_like(grad_conv_exact)
    for tap_index in range(KERNEL):
        matches = (pad_seg[tap_index : tap_index + frame_rows] == local_seg)[:, None]
        grad_taps.append(
            jnp.sum(
                grad_conv_exact
                * jnp.where(matches, glu_padded[tap_index : tap_index + frame_rows], 0.0),
                0,
            )
        )
        back_start = 2 * half_kernel - tap_index
        back_match = (pad_seg[back_start : back_start + frame_rows] == local_seg)[:, None]
        grad_gated = grad_gated + depthwise_filter[tap_index][None, :] * jnp.where(
            back_match, grad_conv_pad[back_start : back_start + frame_rows], 0.0
        )
    grad_kernel = jnp.stack(grad_taps, 0)
    grad_value_low = (grad_gated * glu_gate).astype(jnp.bfloat16)
    grad_gate_low = (grad_gated * glu_value * glu_gate * (1.0 - glu_gate)).astype(jnp.bfloat16)
    grad_pair = jnp.stack([grad_value_low, grad_gate_low], 1)
    grad_glu = jnp.einsum(
        "td,tse->sde", conv_entered, grad_pair, preferred_element_type=jnp.float32
    )
    conv_in_part = jnp.einsum(
        "tse,sde->td", grad_pair, gating_pair_matrix, preferred_element_type=jnp.float32
    )
    norm_conv_grad, grad_ln_conv = norm_backward(
        model_total(conv_in_part), filter_layernorm_scale, conv_normed, conv_inverse
    )
    grad_two = grad_three + norm_conv_grad
    grad_att_branch = grad_two.astype(jnp.bfloat16)
    grad_out = jnp.dot(att_low.T, grad_att_branch, preferred_element_type=jnp.float32)
    grad_heads = (
        jnp.dot(grad_att_branch, mixer_exit_matrix.T, preferred_element_type=jnp.float32)
        .astype(jnp.bfloat16)
        .reshape(frame_rows, head_count, HEAD)
    )
    delta_rows = jnp.transpose(jnp.sum(grad_heads.astype(jnp.float32) * mixed_out, -1))

    def grad_step(carry_in, block):
        scores = block_scores(query_rot, block[0], local_seg, block[2])
        probs = jnp.exp(scores - row_lse[..., None])
        grad_val = jnp.einsum(
            "hqk,qhd->khd",
            probs.astype(jnp.bfloat16),
            grad_heads,
            preferred_element_type=jnp.float32,
        )
        grad_prob = jnp.einsum(
            "qhd,khd->hqk", grad_heads, block[1], preferred_element_type=jnp.float32
        )
        grad_score = (probs * (grad_prob - delta_rows[..., None])).astype(jnp.bfloat16)
        carry_out = carry_in + jnp.einsum(
            "hqk,khd->qhd", grad_score, block[0], preferred_element_type=jnp.float32
        ) * HEAD ** (-0.5)
        grad_key_block = jnp.einsum(
            "hqk,qhd->khd", grad_score, query_rot, preferred_element_type=jnp.float32
        ) * HEAD ** (-0.5)
        return (carry_out, (grad_key_block, grad_val))

    grad_query_acc, (grad_key_all, grad_value_all) = lax.scan(
        guarded(grad_step), start_mix, (key_stack, value_stack, seg_stack)
    )
    key_grad = grad_key_all[0]
    value_grad = grad_value_all[0]
    for piece_number, reach in enumerate(REACHES):
        returned = shifted(
            jnp.stack([grad_key_all[piece_number + 1], grad_value_all[piece_number + 1]], 1).astype(
                jnp.bfloat16
            ),
            "seq",
            -reach,
        ).astype(jnp.float32)
        key_grad = key_grad + returned[:, 0]
        value_grad = value_grad + returned[:, 1]
    grad_query_low = rotary(grad_query_acc, local_pos, -1.0).astype(jnp.bfloat16)
    grad_key_low = rotary(key_grad, local_pos, -1.0).astype(jnp.bfloat16)
    grad_value_rows = value_grad.astype(jnp.bfloat16)
    grad_proj = jnp.stack([grad_query_low, grad_key_low, grad_value_rows], 1).reshape(
        frame_rows, 3, local_width
    )
    grad_qkv = jnp.einsum("td,tse->sde", att_entered, grad_proj, preferred_element_type=jnp.float32)
    att_in_part = jnp.einsum(
        "tse,sde->td", grad_proj, triple_matrix, preferred_element_type=jnp.float32
    )
    norm_att_grad, grad_ln_att = norm_backward(
        model_total(att_in_part), mixer_layernorm_scale, att_normed, att_inverse
    )
    grad_one = grad_two + norm_att_grad
    in_part_one, grad_up1, grad_down1 = ffn_backward(
        grad_one, early_widening_matrix, early_narrowing_matrix, saved_one
    )
    norm_in_total, quant_in_total = model_total((in_part_one, quant_in_part))
    norm_one_grad, grad_ln_ffn1 = norm_backward(
        norm_in_total, early_layernorm_scale, saved_one[0], saved_one[1]
    )
    grad_frames = (grad_one + norm_one_grad + quant_in_total).astype(jnp.bfloat16)
    shares = (
        lax.psum_scatter(
            grad_up1.astype(jnp.bfloat16), "seq", scatter_dimension=0, tiled=True
        ).astype(jnp.float32),
        lax.psum_scatter(
            grad_down1.astype(jnp.bfloat16), "seq", scatter_dimension=1, tiled=True
        ).astype(jnp.float32),
        lax.psum_scatter(
            grad_qkv.astype(jnp.bfloat16), "seq", scatter_dimension=1, tiled=True
        ).astype(jnp.float32),
        lax.psum_scatter(
            grad_out.astype(jnp.bfloat16), "seq", scatter_dimension=1, tiled=True
        ).astype(jnp.float32),
        lax.psum_scatter(
            grad_glu.astype(jnp.bfloat16), "seq", scatter_dimension=1, tiled=True
        ).astype(jnp.float32),
        lax.psum_scatter(
            grad_point.astype(jnp.bfloat16), "seq", scatter_dimension=1, tiled=True
        ).astype(jnp.float32),
        lax.psum_scatter(
            grad_up2.astype(jnp.bfloat16), "seq", scatter_dimension=0, tiled=True
        ).astype(jnp.float32),
        lax.psum_scatter(
            grad_down2.astype(jnp.bfloat16), "seq", scatter_dimension=1, tiled=True
        ).astype(jnp.float32),
        lax.psum_scatter(
            grad_w_code.astype(jnp.bfloat16), "seq", scatter_dimension=0, tiled=True
        ).astype(jnp.float32),
        lax.psum_scatter(
            grad_book.astype(jnp.bfloat16), "seq", scatter_dimension=1, tiled=True
        ).astype(jnp.float32),
    )
    summed = (
        lax.all_gather(shares[0].astype(jnp.bfloat16), "seq", axis=0, tiled=True).astype(
            jnp.float32
        ),
        lax.all_gather(shares[1].astype(jnp.bfloat16), "seq", axis=1, tiled=True).astype(
            jnp.float32
        ),
        lax.all_gather(shares[2].astype(jnp.bfloat16), "seq", axis=1, tiled=True).astype(
            jnp.float32
        ),
        lax.all_gather(shares[3].astype(jnp.bfloat16), "seq", axis=1, tiled=True).astype(
            jnp.float32
        ),
        lax.all_gather(shares[4].astype(jnp.bfloat16), "seq", axis=1, tiled=True).astype(
            jnp.float32
        ),
        lax.all_gather(shares[5].astype(jnp.bfloat16), "seq", axis=1, tiled=True).astype(
            jnp.float32
        ),
        lax.all_gather(shares[6].astype(jnp.bfloat16), "seq", axis=0, tiled=True).astype(
            jnp.float32
        ),
        lax.all_gather(shares[7].astype(jnp.bfloat16), "seq", axis=1, tiled=True).astype(
            jnp.float32
        ),
        lax.all_gather(shares[8].astype(jnp.bfloat16), "seq", axis=0, tiled=True).astype(
            jnp.float32
        ),
        lax.all_gather(shares[9].astype(jnp.bfloat16), "seq", axis=1, tiled=True).astype(
            jnp.float32
        ),
    )
    small = lax.psum(
        (
            grad_ln_ffn1,
            grad_ln_att,
            grad_ln_conv,
            grad_ln_ffn2,
            grad_ln_final,
            grad_kernel,
            jnp.reshape(grad_temper, (1,)),
        ),
        "seq",
    )
    return (
        final_low,
        quant_total.astype(jnp.bfloat16),
        row_loss,
        grad_frames,
        small[0],
        summed[0],
        summed[1],
        small[1],
        summed[2],
        summed[3],
        small[2],
        summed[4],
        small[5],
        grad_bn_gain,
        grad_bn_bias,
        summed[5],
        small[3],
        summed[6],
        summed[7],
        small[4],
        summed[8],
        summed[9],
        small[6],
    )


def solution(mesh):
    in_specs = (
        P("seq", None),
        P(),
        P(),
        P(None, "mp"),
        P("mp", None),
        P(),
        P(None, None, "mp"),
        P("mp", None),
        P(),
        P(None, None, "mp"),
        P(None, "mp"),
        P("mp"),
        P("mp"),
        P("mp", None),
        P(),
        P(None, "mp"),
        P("mp", None),
        P(),
        P(None, "mp"),
        P("mp", None),
        P(),
        P("seq", "mp"),
        P("seq"),
        P("seq", None),
        P("seq", None),
    )
    out_specs = (
        P("seq", None),
        P("seq", None),
        P("seq"),
        P("seq", None),
        P(),
        P(None, "mp"),
        P("mp", None),
        P(),
        P(None, None, "mp"),
        P("mp", None),
        P(),
        P(None, None, "mp"),
        P(None, "mp"),
        P("mp"),
        P("mp"),
        P("mp", None),
        P(),
        P(None, "mp"),
        P("mp", None),
        P(),
        P(None, "mp"),
        P("mp", None),
        P(),
    )
    return jax.shard_map(
        on_device, mesh=mesh, in_specs=in_specs, out_specs=out_specs, check_vma=False
    )
```

profile of v0, /device:TPU:0, one launch (start us, length us, event | category | flops | bytes accessed | tf_op | source)
XLA Modules:
  0.0 2529.6 jit_solution(10867986024500506302)
XLA Ops:
  31.5 61.9 %all-reduce.19.cloned.1.call-done = bf16[1024,1024]{1,0:T(8,128)(2,1)} async-done(((bf16[1024,1024]{1,0:T(8,128)(2,1)}), bf16[1024,1024]{1,0:T(8,128)(2,1)}) %all-reduce.19.cloned.1.call-update) | async-done | bytes 2097168 | tf_op jit(solution)/shard_map/psum | solution.py:99
  144.1 97.8 %collective-permute-done.1 = bf16[1024,2,4,128]{3,0,2,1:T(8,128)(2,1)} collective-permute-done((bf16[1024,2,4,128]{3,0,2,1:T(8,128)(2,1)}, bf16[1024,2,4,128]{3,0,2,1:T(8,128)(2,1)}, u32[]{:S(2)}, u32[]{:S(2)}) %collective-permute-start.1) | collective-permute-done | bytes 2097184 | tf_op jit(solution)/shard_map/ppermute | solution.py:33
  245.0 61.7 %collective-permute-done.2 = bf16[1024,2,4,128]{3,0,2,1:T(8,128)(2,1)} collective-permute-done((bf16[1024,2,4,128]{3,0,2,1:T(8,128)(2,1)}, bf16[1024,2,4,128]{3,0,2,1:T(8,128)(2,1)}, u32[]{:S(2)}, u32[]{:S(2)}) %collective-permute-start.2) | collective-permute-done | bytes 2097184 | tf_op jit(solution)/shard_map/ppermute | solution.py:33
  319.2 11.8 slice_bitcast_fusion
  331.0 64.1 %while.11 = (s32[]{:T(128)}, f32[4,1024]{1,0:T(4,128)S(1)}, f32[4,1024]{1,0:T(4,128)S(1)}, s32[1024]{0:T(1024)S(1)}, s32[7,1024]{1,0:T(8,128)S(1)}, /*index=5*/b...) while((s32[]{:T(128)}, f32[4,1024]{1,0:T(4,128)S(1)}, ...), condition=%wide.region_17.18_spmd.clone, body=%wide.region_14.17_spmd.clone.sunk | while | flops 1104171008 | bytes 39026804 | solution.py:235
  395.1 79.7 %while.12 = (s32[]{:T(128)}, f32[1024,4,128]{0,2,1:T(8,128)}, bf16[7,1024,4,128]{3,1,2,0:T(8,128)(2,1)}, s32[1024]{0:T(1024)S(1)}, s32[7,1024]{1,0:T(8,128)S(1)}...) while((s32[]{:T(128)}, f32[1024,4,128]{0,2,1:T(8,128)}, ...), condition=%wide.region_19.20_spmd.clone, body=%wide.region_18.19_spmd.clone.sunk | while | flops 2166358016 | bytes 9471610 | solution.py:255
  480.7 62.8 %all-reduce.21.cloned.1.call-done = bf16[1024,1024]{1,0:T(8,128)(2,1)} async-done(((bf16[1024,1024]{1,0:T(8,128)(2,1)}), bf16[1024,1024]{1,0:T(8,128)(2,1)}) %all-reduce.21.cloned.1.call-update) | async-done | bytes 2097168 | tf_op jit(solution)/shard_map/psum | solution.py:99
  573.9 33.6 %all-reduce.4 = (f32[512]{0:T(512)S(1)}, f32[512]{0:T(512)S(1)}) all-reduce(f32[512]{0:T(512)S(1)} %get-tuple-element.505, f32[512]{0:T(512)S(1)} %get-tuple-element.504), channel_id=1, replica_groups=mesh['seq'=16,'mp'=2] {'seq'}, use_global_device_ids=true, to_apply=%region_27.28 | all-reduce | flops 1024 | bytes 8192 | tf_op jit(solution)/shard_map/psum | solution.py:280
  612.3 59.3 %all-reduce.23.cloned.1.call-done = bf16[1024,1024]{1,0:T(8,128)(2,1)} async-done(((bf16[1024,1024]{1,0:T(8,128)(2,1)}), bf16[1024,1024]{1,0:T(8,128)(2,1)}) %all-reduce.23.cloned.1.call-update) | async-done | bytes 2097168 | tf_op jit(solution)/shard_map/psum | solution.py:99
  692.6 63.0 %all-reduce.25.cloned.1.call-done = bf16[1024,1024]{1,0:T(8,128)(2,1)} async-done(((bf16[1024,1024]{1,0:T(8,128)(2,1)}), bf16[1024,1024]{1,0:T(8,128)(2,1)}) %all-reduce.25.cloned.1.call-update) | async-done | bytes 2097168 | tf_op jit(solution)/shard_map/psum | solution.py:99
  782.0 62.6 %all-reduce.27.cloned.1.call-done = bf16[1024,1024]{1,0:T(8,128)(2,1)} async-done(((bf16[1024,1024]{1,0:T(8,128)(2,1)}), bf16[1024,1024]{1,0:T(8,128)(2,1)}) %all-reduce.27.cloned.1.call-update) | async-done | bytes 2097168 | tf_op jit(solution)/shard_map/psum | solution.py:99
  870.6 63.0 %all-reduce.29.cloned.1.call-done = bf16[1024,1024]{1,0:T(8,128)(2,1)} async-done(((bf16[1024,1024]{1,0:T(8,128)(2,1)}), bf16[1024,1024]{1,0:T(8,128)(2,1)}) %all-reduce.29.cloned.1.call-update) | async-done | bytes 2097168 | tf_op jit(solution)/shard_map/psum | solution.py:99
  945.7 33.1 %all-reduce.3 = (f32[512]{0:T(512)S(1)}, f32[512]{0:T(512)S(1)}) all-reduce(f32[512]{0:T(512)S(1)} %get-tuple-element.501, f32[512]{0:T(512)S(1)} %get-tuple-element.500), channel_id=1, replica_groups=mesh['seq'=16,'mp'=2] {'seq'}, use_global_device_ids=true, to_apply=%region_49.50 | all-reduce | flops 1024 | bytes 8192 | tf_op jit(solution)/shard_map/psum | solution.py:351
  1014.5 60.8 %all-reduce.31.cloned.1.call-done = bf16[1024,1024]{1,0:T(8,128)(2,1)} async-done(((bf16[1024,1024]{1,0:T(8,128)(2,1)}), bf16[1024,1024]{1,0:T(8,128)(2,1)}) %all-reduce.31.cloned.1.call-update) | async-done | bytes 2097168 | tf_op jit(solution)/shard_map/psum | solution.py:99
  1088.5 306.9 %while.13 = (s32[]{:T(128)}, f32[1024,4,128]{0,2,1:T(8,128)}, f32[7,1024,4,128]{3,1,2,0:T(8,128)}, f32[7,1024,4,128]{3,1,2,0:T(8,128)}, bf16[7,1024,4,128]{3,1,2...) while((s32[]{:T(128)}, f32[1024,4,128]{0,2,1:T(8,128)}, ...), condition=%wide.region_55.56_spmd.clone, body=%wide.region_54.55_spmd.clone.sunk | while | flops 5413797888 | bytes 136380688 | solution.py:422
  1285.1 11.3 bitcast_dynamic-update-slice_fusion.15
  1446.8 27.2 %collective-permute-done.11 = bf16[1024,2,4,128]{3,0,2,1:T(8,128)(2,1)} collective-permute-done((bf16[1024,2,4,128]{3,0,2,1:T(8,128)(2,1)S(1)}, bf16[1024,2,4,128]{3,0,2,1:T(8,128)(2,1)}, u32[]{:S(2)}, u32[]{:S(2)}) %collective-permute-start.11) | collective-permute-done | bytes 2097184 | tf_op jit(solution)/shard_map/ppermute | solution.py:33
  1493.4 17.0 collective-permute-done.12
  1514.1 26.2 %collective-permute-done.14 = bf16[1024,2,4,128]{3,0,2,1:T(8,128)(2,1)} collective-permute-done((bf16[1024,2,4,128]{3,0,2,1:T(8,128)(2,1)}, bf16[1024,2,4,128]{3,0,2,1:T(8,128)(2,1)}, u32[]{:S(2)}, u32[]{:S(2)}) %collective-permute-start.14) | collective-permute-done | bytes 2097184 | tf_op jit(solution)/shard_map/ppermute | solution.py:33
  1544.2 63.4 %collective-permute-done.15 = bf16[1024,2,4,128]{3,0,2,1:T(8,128)(2,1)} collective-permute-done((bf16[1024,2,4,128]{3,0,2,1:T(8,128)(2,1)}, bf16[1024,2,4,128]{3,0,2,1:T(8,128)(2,1)}, u32[]{:S(2)}, u32[]{:S(2)}) %collective-permute-start.15) | collective-permute-done | bytes 2097184 | tf_op jit(solution)/shard_map/ppermute | solution.py:33
  1722.1 11.3 convolution_convert_fusion
  1773.9 17.8 reduce-scatter.23.cloned.1.call-done
  1791.7 74.8 %reduce-scatter.17.cloned.1.call-done = bf16[512,64]{0,1:T(8,128)(2,1)} async-done(((bf16[512,1024]{0,1:T(8,128)(2,1)}), bf16[512,64]{0,1:T(8,128)(2,1)}) %reduce-scatter.17.cloned.1.call-update) | async-done | bytes 65552 | tf_op jit(solution)/shard_map/reduce_scatter | solution.py:475
  1866.6 62.1 %reduce-scatter.15.cloned.1.call-done = bf16[512,64]{0,1:T(8,128)(2,1)} async-done(((bf16[512,1024]{0,1:T(8,128)(2,1)}), bf16[512,64]{0,1:T(8,128)(2,1)}) %reduce-scatter.15.cloned.1.call-update) | async-done | bytes 65552 | tf_op jit(solution)/shard_map/reduce_scatter | solution.py:469
  1931.7 75.2 %reduce-scatter.19.cloned.1.call-done = bf16[64,2048]{1,0:T(8,128)(2,1)} async-done(((bf16[1024,2048]{1,0:T(8,128)(2,1)}), bf16[64,2048]{1,0:T(8,128)(2,1)}) %reduce-scatter.19.cloned.1.call-update) | async-done | bytes 262160 | tf_op jit(solution)/shard_map/reduce_scatter | solution.py:478
  2007.0 81.3 %reduce-scatter.21.cloned.1.call-done = bf16[2048,64]{0,1:T(8,128)(2,1)} async-done(((bf16[2048,1024]{0,1:T(8,128)(2,1)}), bf16[2048,64]{0,1:T(8,128)(2,1)}) %reduce-scatter.21.cloned.1.call-update) | async-done | bytes 262160 | tf_op jit(solution)/shard_map/reduce_scatter | solution.py:481
  2104.6 75.3 %reduce-scatter.11.cloned.1.call-done = bf16[64,2048]{1,0:T(8,128)(2,1)} async-done(((bf16[1024,2048]{1,0:T(8,128)(2,1)}), bf16[64,2048]{1,0:T(8,128)(2,1)}) %reduce-scatter.11.cloned.1.call-update) | async-done | bytes 262160 | tf_op jit(solution)/shard_map/reduce_scatter | solution.py:460
  2180.2 76.7 %reduce-scatter.13.cloned.1.call-done = bf16[2048,64]{0,1:T(8,128)(2,1)} async-done(((bf16[2048,1024]{0,1:T(8,128)(2,1)}), bf16[2048,64]{0,1:T(8,128)(2,1)}) %reduce-scatter.13.cloned.1.call-update) | async-done | bytes 262160 | tf_op jit(solution)/shard_map/reduce_scatter | solution.py:463
  2286.8 74.6 %all-reduce.37.cloned.1.call-done = (bf16[1024,1024]{1,0:T(8,128)(2,1)}, bf16[1024,1024]{1,0:T(8,128)(2,1)}, bf16[1024,1024]{1,0:T(8,128)(2,1)}) async-done(((bf16[1024,1024]{1,0:T(8,128)(2,1)}, bf16[1024,1024]{1,0:T(8,128)(2,1)}, bf16[1024,1024]{1,0:T(8,128)(2,1)}), (bf16[1024,1024]{1,0:T(8,128)(2,1)}, bf16[1024,1024]{1,0:T(8,128)(2,1)}, bf16[1024,1024]{1,0:T(8,128)(2,1)})) %all-reduce.37.cloned.1.call-update) | async-done | bytes 6291472 | tf_op jit(solution)/shard_map/psum | solution.py:99
  2365.1 63.4 %all-reduce.2 = (f32[1024]{0:T(1024)}, f32[1024]{0:T(1024)}, f32[1024]{0:T(1024)}, f32[5,512]{1,0:T(8,128)}, f32[1024]{0:T(1024)}, /*index=5*/f32[1024]{0:T(1024)}, f32[1]{0:T(128)}) all-reduce(f32[1024]{0:T(1024)S(1)} %get-tuple-element.485, f32[1024]{0:T(1024)S(1)} %get-tuple-element.483, ...), channel_id=1, replica_groups=mesh['seq'=16,'mp'=2] {'seq'}, use_global_device_ids=true, to_apply=%region_66.67 | all-reduce | flops 7681 | bytes 61448 | tf_op jit(solution)/shard_map/psum | solution.py:523
  2440.0 20.9 all-gather.16.cloned.1.call-done
  2467.5 44.4 %all-gather.18.cloned.1.call-done = bf16[2048,1024]{0,1:T(8,128)(2,1)} async-done(((bf16[2048,64]{0,1:T(8,128)(2,1)}), bf16[2048,1024]{0,1:T(8,128)(2,1)}) %all-gather.18.cloned.1.call-update) | async-done | bytes 4194320 | tf_op jit(solution)/shard_map/all_gather | solution.py:495
  (686 shorter events, 1013.9 us)
Async XLA Ops:
  27.5 516.0 %all-reduce.21.cloned.1.call-start = ((), (), s32[]{:S(2)}) async-start(), calls=%async_computation.9 | async-start | bytes 4194304 | tf_op jit(solution)/shard_map/psum | solution.py:99
  129.5 177.2 %collective-permute-start.2 = (bf16[1024,2,4,128]{3,0,2,1:T(8,128)(2,1)}, bf16[1024,2,4,128]{3,0,2,1:T(8,128)(2,1)}, u32[]{:S(2)}, u32[]{:S(2)}) collective-permute-start(bf16[1024,2,4,128]{3,0,2,1:T(8,128)(2,1)} %get-tuple-element.602), channel_id=1, source_target_pairs={{0,6},{2,8},{4,10},{6,12},{8,14},{10,16},{12,18},{14,20},{16,22},{... | collective-permute-start | bytes 6291464 | tf_op jit(solution)/shard_map/ppermute | solution.py:33
  133.8 176.1 %collective-permute-start.3 = (bf16[1024,2,4,128]{3,0,2,1:T(8,128)(2,1)}, bf16[1024,2,4,128]{3,0,2,1:T(8,128)(2,1)}, u32[]{:S(2)}, u32[]{:S(2)}) collective-permute-start(bf16[1024,2,4,128]{3,0,2,1:T(8,128)(2,1)} %get-tuple-element.602), channel_id=1, source_target_pairs={{2,0},{4,2},{6,4},{8,6},{10,8},{12,10},{14,12},{16,14},{18,16},{20... | collective-permute-start | bytes 6291464 | tf_op jit(solution)/shard_map/ppermute | solution.py:33
  135.2 177.9 %collective-permute-start.4 = (bf16[1024,2,4,128]{3,0,2,1:T(8,128)(2,1)}, bf16[1024,2,4,128]{3,0,2,1:T(8,128)(2,1)}, u32[]{:S(2)}, u32[]{:S(2)}) collective-permute-start(bf16[1024,2,4,128]{3,0,2,1:T(8,128)(2,1)} %get-tuple-element.602), channel_id=1, source_target_pairs={{4,0},{6,2},{8,4},{10,6},{12,8},{14,10},{16,12},{18,14},{20,16},{2... | collective-permute-start | bytes 6291464 | tf_op jit(solution)/shard_map/ppermute | solution.py:33
  136.5 179.7 %collective-permute-start.5 = (bf16[1024,2,4,128]{3,0,2,1:T(8,128)(2,1)}, bf16[1024,2,4,128]{3,0,2,1:T(8,128)(2,1)}, u32[]{:S(2)}, u32[]{:S(2)}) collective-permute-start(bf16[1024,2,4,128]{3,0,2,1:T(8,128)(2,1)} %get-tuple-element.602), channel_id=1, source_target_pairs={{6,0},{8,2},{10,4},{12,6},{14,8},{16,10},{18,12},{20,14},{22,16},{... | collective-permute-start | bytes 6291464 | tf_op jit(solution)/shard_map/ppermute | solution.py:33
  480.3 191.3 %all-reduce.23.cloned.1.call-start = ((), (), s32[]{:S(2)}) async-start(), calls=%async_computation.10 | async-start | bytes 4194304 | tf_op jit(solution)/shard_map/psum | solution.py:99
  612.2 143.4 %all-reduce.25.cloned.1.call-start = ((), (), s32[]{:S(2)}) async-start(), calls=%async_computation.11 | async-start | bytes 4194304 | tf_op jit(solution)/shard_map/psum | solution.py:99
  692.5 152.1 %all-reduce.27.cloned.1.call-start = ((), (), s32[]{:S(2)}) async-start(), calls=%async_computation.12 | async-start | bytes 4194304 | tf_op jit(solution)/shard_map/psum | solution.py:99
  781.6 152.0 %all-reduce.29.cloned.1.call-start = ((), (), s32[]{:S(2)}) async-start(), calls=%async_computation.13 | async-start | bytes 4194304 | tf_op jit(solution)/shard_map/psum | solution.py:99
  870.5 204.8 %all-reduce.31.cloned.1.call-start = ((), (), s32[]{:S(2)}) async-start(), calls=%async_computation.14 | async-start | bytes 4194304 | tf_op jit(solution)/shard_map/psum | solution.py:99
  1014.4 719.1 %all-reduce.33.cloned.1.call-start = ((), (), s32[]{:S(2)}) async-start(), calls=%async_computation.15 | async-start | bytes 4194304 | tf_op jit(solution)/shard_map/psum | solution.py:99
  1440.5 167.1 %collective-permute-start.15 = (bf16[1024,2,4,128]{3,0,2,1:T(8,128)(2,1)}, bf16[1024,2,4,128]{3,0,2,1:T(8,128)(2,1)}, u32[]{:S(2)}, u32[]{:S(2)}) collective-permute-start(bf16[1024,2,4,128]{3,0,2,1:T(8,128)(2,1)} %pad_maximum_fusion.7), channel_id=1, source_target_pairs={{0,6},{2,8},{4,10},{6,12},{8,14},{10,16},{12,18},{14,20},{16,22},{... | collective-permute-start | bytes 6291464 | tf_op jit(solution)/shard_map/ppermute | solution.py:33
  1474.0 137.5 %collective-permute-start.10 = (bf16[1024,2,4,128]{3,0,2,1:T(8,128)(2,1)}, bf16[1024,2,4,128]{3,0,2,1:T(8,128)(2,1)}, u32[]{:S(2)}, u32[]{:S(2)}) collective-permute-start(bf16[1024,2,4,128]{3,0,2,1:T(8,128)(2,1)} %pad_maximum_fusion.2), channel_id=1, source_target_pairs={{2,0},{4,2},{6,4},{8,6},{10,8},{12,10},{14,12},{16,14},{18,16},{20... | collective-permute-start | bytes 6291464 | tf_op jit(solution)/shard_map/ppermute | solution.py:33
  1635.6 137.6 %reduce-scatter.25.cloned.1.call-start = ((), (), s32[]{:S(2)}) async-start(), calls=%async_computation.33 | async-start | bytes 1114112 | tf_op jit(solution)/shard_map/reduce_scatter | solution.py:484
  1670.4 196.1 %reduce-scatter.17.cloned.1.call-start = ((), (), s32[]{:S(2)}) async-start(), calls=%async_computation.24 | async-start | bytes 1114112 | tf_op jit(solution)/shard_map/reduce_scatter | solution.py:475
  1675.8 252.8 %reduce-scatter.15.cloned.1.call-start = ((), (), s32[]{:S(2)}) async-start(), calls=%async_computation.21 | async-start | bytes 1114112 | tf_op jit(solution)/shard_map/reduce_scatter | solution.py:469
  1681.3 248.7 %all-reduce.35.cloned.1.call-start = ((), (), s32[]{:S(2)}) async-start(), calls=%async_computation.34 | async-start | bytes 12582912
  1710.7 296.2 %reduce-scatter.19.cloned.1.call-start = ((), (), s32[]{:S(2)}) async-start(), calls=%async_computation.26 | async-start | bytes 4456448 | tf_op jit(solution)/shard_map/reduce_scatter | solution.py:478
  1721.8 366.4 %reduce-scatter.21.cloned.1.call-start = ((), (), s32[]{:S(2)}) async-start(), calls=%async_computation.28 | async-start | bytes 4456448 | tf_op jit(solution)/shard_map/reduce_scatter | solution.py:481
  1733.4 446.5 %reduce-scatter.11.cloned.1.call-start = ((), (), s32[]{:S(2)}) async-start(), calls=%async_computation.16 | async-start | bytes 4456448 | tf_op jit(solution)/shard_map/reduce_scatter | solution.py:460
  1761.6 495.4 %reduce-scatter.13.cloned.1.call-start = ((), (), s32[]{:S(2)}) async-start(), calls=%async_computation.18 | async-start | bytes 4456448 | tf_op jit(solution)/shard_map/reduce_scatter | solution.py:463
  1773.2 485.2 %all-gather.32.cloned.1.call-start = ((), (), s32[]{:S(2)}) async-start(), calls=%async_computation.30 | async-start | bytes 1114112 | tf_op jit(solution)/shard_map/all_gather | solution.py:516
  1773.8 487.5 %all-gather.34.cloned.1.call-start = ((), (), s32[]{:S(2)}) async-start(), calls=%async_computation.32 | async-start | bytes 1114112 | tf_op jit(solution)/shard_map/all_gather | solution.py:519
  1791.6 472.3 %all-gather.26.cloned.1.call-start = ((), (), s32[]{:S(2)}) async-start(), calls=%async_computation.25 | async-start | bytes 1114112 | tf_op jit(solution)/shard_map/all_gather | solution.py:507
  1866.5 400.0 %all-gather.22.cloned.1.call-start = ((), (), s32[]{:S(2)}) async-start(), calls=%async_computation.22 | async-start | bytes 1114112 | tf_op jit(solution)/shard_map/all_gather | solution.py:501
  1928.7 340.4 %all-gather.24.cloned.1.call-start = ((), (), s32[]{:S(2)}) async-start(), calls=%async_computation.23 | async-start | bytes 2228224 | tf_op jit(solution)/shard_map/all_gather | solution.py:504
  1931.7 341.6 %all-gather.28.cloned.1.call-start = ((), (), s32[]{:S(2)}) async-start(), calls=%async_computation.27 | async-start | bytes 4456448 | tf_op jit(solution)/shard_map/all_gather | solution.py:510
  2006.9 273.0 %all-gather.30.cloned.1.call-start = ((), (), s32[]{:S(2)}) async-start(), calls=%async_computation.29 | async-start | bytes 4456448 | tf_op jit(solution)/shard_map/all_gather | solution.py:513
  2088.3 273.1 %all-reduce.37.cloned.1.call-start = ((), (), s32[]{:S(2)}) async-start(), calls=%async_computation.35 | async-start | bytes 12582912 | tf_op jit(solution)/shard_map/psum | solution.py:99
  2102.7 331.8 %all-gather.20.cloned.1.call-start = ((), (), s32[]{:S(2)}) async-start(), calls=%async_computation.20 | async-start | bytes 3342336 | tf_op jit(solution)/shard_map/all_gather | solution.py:498
  2104.6 356.3 %all-gather.16.cloned.1.call-start = ((), (), s32[]{:S(2)}) async-start(), calls=%async_computation.17 | async-start | bytes 4456448 | tf_op jit(solution)/shard_map/all_gather | solution.py:492
  2179.9 332.0 %all-gather.18.cloned.1.call-start = ((), (), s32[]{:S(2)}) async-start(), calls=%async_computation.19 | async-start | bytes 4456448 | tf_op jit(solution)/shard_map/all_gather | solution.py:495
  (156 other events, 4372.4 us)
Sparse Core Ops, SparseCore 0:
  27.6 65.6 all-reduce.18
  480.4 63.0 all-reduce.20
  612.4 59.2 all-reduce.22
  692.7 62.9 all-reduce.24
  781.7 62.8 all-reduce.26
  870.6 62.9 all-reduce.28
  1014.5 60.7 all-reduce.30
  1635.8 66.5 all-reduce.32
  1710.8 147.7 all-reduce.34
  1860.7 37.5 all-gather.31
  1900.7 37.1 all-gather.33
  1940.0 51.8 all-gather.25
  1994.2 37.3 all-gather.21
  2034.5 57.1 all-gather.23
  2093.7 54.7 all-gather.27
  2150.7 54.8 all-gather.29
  2208.9 152.4 all-reduce.36
  2363.4 45.4 all-gather.19
  2411.3 49.5 all-gather.15
  2462.9 49.0 all-gather.17
Sparse Core Ops, SparseCore 1:
  1663.4 65.9 reduce-scatter.24
  1732.8 58.8 reduce-scatter.22
  1795.5 70.9 reduce-scatter.16
  1870.7 57.9 reduce-scatter.14
  1933.0 73.8 reduce-scatter.18
  2010.8 77.4 reduce-scatter.20
  2092.6 87.3 reduce-scatter.10
  2184.7 72.2 reduce-scatter.12
where the time goes:
time: 2540 us; the launch traced here: 2530 us
  waiting for transfers between devices  1330 us (52%)
  matrix products  583 us (23%)
  other arithmetic  237 us (9%)
  blocking collectives  159 us (6%)
  local copies, waits for them, and re-layouts  153 us (6%)
  starting transfers between devices  43.7 us (2%)
    psum x9, waiting for transfers between devices, model_total(): lax.psum(shortened(partial_terms), 'mp')  508 us
    ppermute x12, waiting for transfers between devices, shifted(): return lax.ppermute(shard, axis, pairs)  293 us
    dot_general x14, matrix products, block_scores(): jnp.einsum('qhd,khd->hqk', queries, keys_block, preferred_element_type=jn...  101 us
    unnamed x267, local copies, waits for them, and re-layouts  92.3 us
    reduce_scatter x1, waiting for transfers between devices, on_device(): lax.psum_scatter(grad_down2.astype(jnp.bfloat16), 'seq', scatter_dimensio...  81.3 us
    dot_general x7, matrix products, grad_step(): jnp.einsum('hqk,qhd->khd', probs.astype(jnp.bfloat16), grad_heads, prefer...  79 us
    dot_general x7, matrix products, grad_step(): jnp.einsum('qhd,khd->hqk', grad_heads, block[1], preferred_element_type=j...  77.5 us
    reduce_scatter x1, waiting for transfers between devices, on_device(): lax.psum_scatter(grad_down1.astype(jnp.bfloat16), 'seq', scatter_dimensio...  76.7 us
  transfers between devices with their start and end apart: 44, of which 25 were waited for; matrix products, arithmetic and copies ran while one was open for 10% of the time, Pallas kernels for 0%

commit v1 on v0

v1 whole, which is shorter than its diff:
```python
import functools
import math

import jax
import jax.numpy as jnp
from jax import lax
from jax.experimental import pallas as pl
from jax.experimental.pallas import tpu as pltpu
from jax.sharding import PartitionSpec as P

D = 1024
HEAD = 128
KERNEL = 5
LONGEST = 3008

EPSILON = 1e-05
MASKED = -1e30
SCALE = HEAD ** (-0.5)
BOTH = ("seq", "mp")
LOW = jnp.bfloat16
WIDE = jnp.float32


def dot(a, b, dims=((1,), (0,))):
    return lax.dot_general(a, b, (dims, ((), ())), preferred_element_type=WIDE)


def dot_nt(a, b):
    return dot(a, b, ((1,), (1,)))


def dot_tn(a, b):
    return dot(a, b, ((0,), (0,)))


def cut(array, start, size, axis=0):
    return lax.dynamic_slice_in_dim(array, start, size, axis)


def mp_shift(shard, by):
    count = lax.axis_size("mp")
    return lax.ppermute(shard, "mp", [(i, (i + by) % count) for i in range(count)])


def seq_xor(shard, mask):
    return lax.ppermute(shard, "seq", [(i, i ^ mask) for i in range(lax.axis_size("seq"))])


def seq_shift(shard, by):
    count = lax.axis_size("seq")
    return lax.ppermute(shard, "seq", [(i, i + by) for i in range(count) if 0 <= i + by < count])


def flat_shift(shard, by):
    count = lax.axis_size("seq") * lax.axis_size("mp")
    return lax.ppermute(shard, BOTH, [(i, i + by) for i in range(count) if 0 <= i + by < count])


def from_mp(shard):
    return [shard] + [mp_shift(shard, -k) for k in range(1, lax.axis_size("mp"))]


def to_mp(parts):
    total = parts[0].astype(WIDE)
    for k in range(1, len(parts)):
        total = total + mp_shift(parts[k].astype(LOW), k).astype(WIDE)
    return total


def mp_place(k):
    return (lax.axis_index("mp") + k) % lax.axis_size("mp")


def joined(pieces, axis=0):
    size = pieces[0].shape[axis]
    shape = list(pieces[0].shape)
    shape[axis] = size * len(pieces)
    whole = jnp.zeros(shape, pieces[0].dtype)
    for k, piece in enumerate(pieces):
        whole = lax.dynamic_update_slice_in_dim(whole, piece, mp_place(k) * size, axis)
    return whole


def fetched(shard, axis):
    core = lax.axis_index("seq") % 2
    half = shard.shape[axis] // 2
    mine = cut(shard, core * half, half, axis)
    parts = from_mp(mine)[1:]
    return [[part, seq_xor(part, 1)] for part in parts]


def whole_of(shard, axis):
    core = lax.axis_index("seq") % 2
    size = shard.shape[axis]
    half = size // 2
    shape = list(shard.shape)
    shape[axis] = size * lax.axis_size("mp")
    whole = jnp.zeros(shape, shard.dtype)
    whole = lax.dynamic_update_slice_in_dim(whole, shard, mp_place(0) * size, axis)
    for k, pair in enumerate(fetched(shard, axis)):
        for j in range(2):
            start = mp_place(k + 1) * size + (core ^ j) * half
            whole = lax.dynamic_update_slice_in_dim(whole, pair[j], start, axis)
    return whole


def halved(part, first_bit):
    place = lax.axis_index("seq")
    for bit in range(first_bit, int(math.log2(lax.axis_size("seq")))):
        half = part.shape[0] // 2
        side = (place >> bit) & 1
        sent = seq_xor(cut(part, (1 - side) * half, half), 1 << bit)
        part = cut(part, side * half, half) + sent
    return part


def summed_grad(pieces, across):
    held = [pair[0].astype(LOW) + seq_xor(pair[1].astype(LOW), 1) for pair in pieces]
    total = held[0]
    for k in range(1, len(held)):
        total = total + mp_shift(held[k], k)
    block = halved(total, 1)
    rows, columns = block.shape
    bits = int(math.log2(lax.axis_size("seq")))
    every = lax.all_gather(block, "seq", axis=0).reshape([2] * bits + [rows, columns])
    order = [bits - 1 - bit for bit in range(1, bits)] + [bits]
    spread = rows << (bits - 1)
    if across:
        every = jnp.transpose(every, order + [bits - 1, bits + 1])
        return every.reshape(spread, 2 * columns).astype(WIDE)
    every = jnp.transpose(every, [bits - 1] + order + [bits + 1])
    return every.reshape(2 * spread, columns).astype(WIDE)


def clip_of(clip_durations, positions):
    clip_ends = jnp.cumsum(clip_durations, dtype=jnp.int32)
    passed = clip_ends[None, :] <= positions[:, None]
    segment = jnp.sum(passed.astype(jnp.int32), 1, dtype=jnp.int32)
    starts = jnp.sum(jnp.where(passed, clip_durations[None, :], 0), 1, dtype=jnp.int32)
    ends = jnp.min(jnp.where(passed, 2**30, clip_ends[None, :]), 1)
    return segment, starts, ends


def norm_forward(rows, gain):
    centred = rows - jnp.mean(rows, -1, keepdims=True)
    inverse = lax.rsqrt(jnp.mean(centred * centred, -1, keepdims=True) + EPSILON)
    normed = centred * inverse
    return (normed * gain).astype(LOW), normed, inverse


def norm_backward(upstream, gain, normed, inverse):
    scaled = upstream * gain
    centred = (
        scaled
        - jnp.mean(scaled, -1, keepdims=True)
        - normed * jnp.mean(scaled * normed, -1, keepdims=True)
    )
    return centred * inverse, jnp.sum(upstream * normed, 0)


def rotary(rows, position, direction):
    half_width = rows.shape[-1] // 2
    frequency = 10000.0 ** (-jnp.arange(half_width, dtype=WIDE) / half_width)
    angles = position.astype(WIDE)[:, None] * frequency[None, :]
    cosine = jnp.cos(angles)
    sine = direction * jnp.sin(angles)
    leading = rows[..., :half_width]
    trailing = rows[..., half_width:]
    return jnp.concatenate([leading * cosine - trailing * sine, leading * sine + trailing * cosine], -1)


def silu_slope(hidden, sigma):
    return sigma * (1.0 + hidden * (1.0 - sigma))


def attend_kernel(lo_ref, hi_ref, q_ref, kv_ref, sq_ref, sk_ref, low_ref, mix_ref, lse_ref, *, depth, parts):
    i = pl.program_id(0)
    rows = q_ref.shape[0] // parts
    queries = [q_ref[j * rows : (j + 1) * rows, :] for j in range(parts)]
    query_seg = [sq_ref[j * rows : (j + 1) * rows, :] for j in range(parts)]

    def step(t, carry):
        span = pl.ds(pl.multiple_of(t * depth, depth), depth)
        keys = kv_ref[span, :HEAD]
        values = kv_ref[span, HEAD:]
        key_seg = sk_ref[t]
        out = []
        for j in range(parts):
            top, total, mixed = carry[j]
            scores = dot_nt(queries[j], keys) * SCALE
            scores = jnp.where(query_seg[j] == key_seg, scores, MASKED)
            new_top = jnp.maximum(top, jnp.max(scores, -1, keepdims=True))
            probs = jnp.exp(scores - new_top)
            fade = jnp.exp(top - new_top)
            total = fade * total + jnp.sum(probs, -1, keepdims=True)
            mixed = fade * mixed + dot(probs.astype(LOW), values)
            out.append((new_top, total, mixed))
        return tuple(out)

    start = (
        jnp.full((rows, 1), MASKED, WIDE),
        jnp.zeros((rows, 1), WIDE),
        jnp.zeros((rows, HEAD), WIDE),
    )
    done = lax.fori_loop(lo_ref[i], hi_ref[i], step, (start,) * parts)
    for j in range(parts):
        top, total, mixed = done[j]
        mixed = mixed / total
        span = slice(j * rows, (j + 1) * rows)
        mix_ref[span, :] = mixed
        low_ref[span, :] = mixed.astype(LOW)
        lse_ref[span, :] = top + jnp.log(total)


def bounds(starts, ends, key_base, rows, depth, key_rows):
    count = key_rows // depth
    lo = jnp.clip((starts[::rows] - key_base) // depth, 0, count)
    hi = jnp.clip((ends[rows - 1 :: rows] - key_base + depth - 1) // depth, 0, count)
    return lo.astype(jnp.int32), hi.astype(jnp.int32)


def whole_block(array):
    return pl.BlockSpec(array.shape, lambda i, *_: (0,) * array.ndim)


def attend(queries, kv, place, rows=512, depth=1024, parts=2):
    starts, ends, query_seg, key_seg, key_base = place
    count, key_rows = queries.shape[0], kv.shape[0]
    lo, hi = bounds(starts, ends, key_base, rows, depth, key_rows)
    key_seg = key_seg.reshape(key_rows // depth, 1, depth)

    def row(width):
        return pl.BlockSpec((rows, width), lambda i, *_: (i, 0))

    return pl.pallas_call(
        functools.partial(attend_kernel, depth=depth, parts=parts),
        grid_spec=pltpu.PrefetchScalarGridSpec(
            num_scalar_prefetch=2,
            grid=(count // rows,),
            in_specs=[row(HEAD), whole_block(kv), row(1), whole_block(key_seg)],
            out_specs=[row(HEAD), row(HEAD), row(1)],
        ),
        out_shape=[
            jax.ShapeDtypeStruct((count, HEAD), LOW),
            jax.ShapeDtypeStruct((count, HEAD), WIDE),
            jax.ShapeDtypeStruct((count, 1), WIDE),
        ],
        compiler_params=pltpu.CompilerParams(vmem_limit_bytes=50 * 2**20),
        cost_estimate=pl.CostEstimate(
            flops=4 * count * LONGEST * HEAD, bytes_accessed=16 * 2**20, transcendentals=count * LONGEST
        ),
        name="attend",
    )(lo, hi, queries, kv, query_seg.reshape(count, 1), key_seg)


def attend_back_kernel(
    lo_ref, hi_ref, q_ref, do_ref, kv_ref, sq_ref, sk_ref, lse_ref, dl_ref, dq_ref, dkv_ref, *, depth
):
    i = pl.program_id(0)

    @pl.when(i == 0)
    def _():
        dkv_ref[...] = jnp.zeros_like(dkv_ref)

    queries = q_ref[...]
    upstream = do_ref[...]
    query_seg, lse, delta = sq_ref[0], lse_ref[0], dl_ref[0]
    dq_ref[...] = jnp.zeros_like(dq_ref)

    def step(t, unused):
        span = pl.ds(pl.multiple_of(t * depth, depth), depth)
        keys = kv_ref[span, :HEAD]
        values = kv_ref[span, HEAD:]
        scores = dot_nt(keys, queries) * SCALE
        probs = jnp.where(sk_ref[span, :] == query_seg, jnp.exp(scores - lse), 0.0)
        grad_probs = dot_nt(values, upstream)
        grad_scores = (probs * (grad_probs - delta)).astype(LOW)
        dkv_ref[span, HEAD:] += dot(probs.astype(LOW), upstream)
        dkv_ref[span, :HEAD] += dot(grad_scores, queries)
        dq_ref[...] += dot_tn(grad_scores, keys)
        return unused

    lax.fori_loop(lo_ref[i], hi_ref[i], step, 0)


def attend_back(queries, upstream, kv, place, lse, delta, rows=512, depth=512):
    starts, ends, query_seg, key_seg, key_base = place
    count, key_rows = queries.shape[0], kv.shape[0]
    lo, hi = bounds(starts, ends, key_base, rows, depth, key_rows)
    key_seg = key_seg.reshape(key_rows, 1)
    row = pl.BlockSpec((rows, HEAD), lambda i, *_: (i, 0))
    lane = pl.BlockSpec((1, 1, rows), lambda i, *_: (i, 0, 0))

    def lanes(vector):
        return vector.reshape(count // rows, 1, rows)

    grad_kv = jax.ShapeDtypeStruct((key_rows, 2 * HEAD), WIDE)
    return pl.pallas_call(
        functools.partial(attend_back_kernel, depth=depth),
        grid_spec=pltpu.PrefetchScalarGridSpec(
            num_scalar_prefetch=2,
            grid=(count // rows,),
            in_specs=[row, row, whole_block(kv), lane, whole_block(key_seg), lane, lane],
            out_specs=[row, whole_block(grad_kv)],
        ),
        out_shape=[jax.ShapeDtypeStruct((count, HEAD), WIDE), grad_kv],
        compiler_params=pltpu.CompilerParams(vmem_limit_bytes=56 * 2**20),
        cost_estimate=pl.CostEstimate(
            flops=10 * count * LONGEST * HEAD, bytes_accessed=32 * 2**20, transcendentals=count * LONGEST
        ),
        name="attend_back",
    )(lo, hi, queries, upstream, kv, lanes(query_seg), key_seg, lanes(lse), lanes(delta))


def on_device(
    acoustic_features,
    clip_durations,
    early_layernorm_scale,
    early_widening_matrix,
    early_narrowing_matrix,
    mixer_layernorm_scale,
    triple_matrix,
    mixer_exit_matrix,
    filter_layernorm_scale,
    gating_pair_matrix,
    depthwise_filter,
    running_stats_factor,
    running_stats_offset,
    filter_exit_projection,
    later_layernorm_scale,
    later_widening_matrix,
    later_narrowing_matrix,
    last_layernorm_scale,
    quantizer_projection,
    entry_vectors,
    smoothing_level,
    random_flat_samples,
    expected_entries,
    result_adjoint,
    discrete_adjoint,
):
    seq_count, mp_count = lax.axis_size("seq"), lax.axis_size("mp")
    seq_at, mp_at = lax.axis_index("seq"), lax.axis_index("mp")
    core = seq_at % 2
    frame_rows = acoustic_features.shape[0]
    all_rows = frame_rows * seq_count
    own = frame_rows // mp_count
    own_base = seq_at * frame_rows + mp_at * own

    def rel_rows(array, k):
        return cut(array, mp_place(k) * own, own)

    def halves_of(array, width, k):
        half = width // 2
        return [cut(array, mp_place(k) * width + (core ^ j) * half, half, 1) for j in range(2)]

    def local_halves(array):
        half = array.shape[1] // 2
        return [cut(array, (core ^ j) * half, half, 1) for j in range(2)]

    exit_all = whole_of(mixer_exit_matrix, 0)
    gating_all = whole_of(gating_pair_matrix, 2)
    point_all = whole_of(filter_exit_projection, 0)
    small_weights = jnp.concatenate(
        [depthwise_filter, running_stats_factor[None], running_stats_offset[None]], 0
    )
    small_all = joined(from_mp(small_weights), 1)
    filter_all, factor_all, offset_all = small_all[:KERNEL], small_all[KERNEL], small_all[KERNEL + 1]
    up_other = fetched(later_widening_matrix, 1)
    down_other = fetched(later_narrowing_matrix, 0)
    book_all = whole_of(entry_vectors, 0)

    first = []
    for k in list(range(1, mp_count)) + [0]:
        rows = rel_rows(acoustic_features, k).astype(WIDE)
        entered, normed, inverse = norm_forward(rows, early_layernorm_scale)
        hidden = dot(entered, early_widening_matrix)
        activated = (hidden * jax.nn.sigmoid(hidden)).astype(LOW)
        part = dot(activated, early_narrowing_matrix)
        first.append((part, entered, hidden, activated, normed, inverse))
    first = [first[-1]] + first[:-1]
    features = rel_rows(acoustic_features, 0).astype(WIDE)
    after_ffn = features + 0.5 * to_mp([f[0] for f in first])

    local_heads = triple_matrix.shape[2] // HEAD
    group_rows = local_heads * frame_rows
    group_at = seq_at // local_heads
    groups = [
        [(z * local_heads + g) * mp_count + m for g in range(local_heads) for m in range(mp_count)]
        for z in range(seq_count // local_heads)
    ]
    att_entered, att_normed, att_inverse = norm_forward(after_ffn, mixer_layernorm_scale)
    att_group = lax.all_gather(att_entered, BOTH, axis_index_groups=groups, axis=0, tiled=True)
    head_matrix = cut(triple_matrix, (seq_at % local_heads) * HEAD, HEAD, 2)
    head_matrix = jnp.transpose(head_matrix, (1, 0, 2)).reshape(D, 3 * HEAD)
    projected = dot(att_group, head_matrix)
    reaches = range(1, -(-(LONGEST - 1) // group_rows) + 1)
    halo = [min(group_rows, -(-(LONGEST - (r - 1) * group_rows) // 1024) * 1024) for r in reaches]
    halo_rows = sum(halo)
    key_base = group_at * group_rows - halo_rows
    key_index = key_base + jnp.arange(group_rows + 2 * halo_rows, dtype=jnp.int32)
    key_seg, key_start, key_end = clip_of(clip_durations, key_index)
    key_seg = jnp.where(jnp.logical_and(key_index >= 0, key_index < all_rows), key_seg, -1)
    middle = slice(halo_rows, halo_rows + group_rows)
    group_pos = key_index[middle] - key_start[middle]
    place = (key_start[middle], key_end[middle], key_seg[middle], key_seg, key_base)
    query_rot = rotary(projected[:, :HEAD], group_pos, 1.0).astype(LOW)
    key_rot = rotary(projected[:, HEAD : 2 * HEAD], group_pos, 1.0).astype(LOW)
    kv_own = jnp.concatenate([key_rot, projected[:, 2 * HEAD :].astype(LOW)], 1)
    lower = [seq_shift(kv_own[group_rows - n :], local_heads * r) for r, n in zip(reaches, halo)]
    upper = [seq_shift(kv_own[:n], -local_heads * r) for r, n in zip(reaches, halo)]
    kv = jnp.concatenate(lower[::-1] + [kv_own] + upper, 0)
    mixed_low, mixed, row_lse = attend(query_rot, kv, place)

    def exchange(array):
        return lax.all_to_all(array, BOTH, 0, 0, axis_index_groups=groups)

    att_parts = exchange(mixed_low.reshape(local_heads * mp_count, own, HEAD))
    att_low = jnp.transpose(
        att_parts.reshape(local_heads, mp_count, own, HEAD), (2, 1, 0, 3)
    ).reshape(own, D)
    after_att = after_ffn + dot(att_low, exit_all)

    half_kernel = KERNEL // 2
    pad_index = own_base - half_kernel + jnp.arange(own + 2 * half_kernel, dtype=jnp.int32)
    pad_seg = clip_of(clip_durations, pad_index)[0]
    pad_seg = jnp.where(jnp.logical_and(pad_index >= 0, pad_index < all_rows), pad_seg, -1)
    own_seg = pad_seg[half_kernel : half_kernel + own]
    masks = [(pad_seg[j : j + own] == own_seg)[:, None] for j in range(KERNEL)]

    def padded(block):
        low = flat_shift(block[own - half_kernel :], 1)
        high = flat_shift(block[:half_kernel], -1)
        return jnp.concatenate([low, block, high], 0).astype(WIDE)

    conv_entered, conv_normed, conv_inverse = norm_forward(after_att, filter_layernorm_scale)
    glu_value = dot(conv_entered, gating_all[0])
    glu_gate = jax.nn.sigmoid(dot(conv_entered, gating_all[1]))
    glu_low = (glu_value * glu_gate).astype(LOW)
    glu_padded = padded(glu_low)
    conv_out = jnp.zeros((own, D), WIDE)
    for j in range(KERNEL):
        conv_out = conv_out + filter_all[j][None, :] * jnp.where(masks[j], glu_padded[j : j + own], 0.0)
    sums = lax.psum(jnp.stack([jnp.sum(conv_out, 0), jnp.sum(conv_out * conv_out, 0)]), BOTH)
    bn_mean = sums[0] / all_rows
    bn_inv = lax.rsqrt(sums[1] / all_rows - bn_mean * bn_mean + EPSILON)
    bn_hat = (conv_out - bn_mean) * bn_inv
    bn_out = bn_hat * factor_all + offset_all
    bn_sigma = jax.nn.sigmoid(bn_out)
    swish_low = (bn_out * bn_sigma).astype(LOW)
    after_conv = after_att + dot(swish_low, point_all)

    late_entered, late_normed, late_inverse = norm_forward(after_conv, later_layernorm_scale)
    ups = [later_widening_matrix] + [part for pair in up_other for part in pair]
    downs = [later_narrowing_matrix] + [part for pair in down_other for part in pair]
    late_hidden, late_act = [], []
    branch = 0.0
    for w_in, w_back in zip(ups, downs):
        hidden = dot(late_entered, w_in)
        activated = (hidden * jax.nn.sigmoid(hidden)).astype(LOW)
        branch = branch + dot(activated, w_back)
        late_hidden.append(hidden)
        late_act.append(activated)
    after_two = after_conv + 0.5 * branch
    final_low, final_normed, final_inverse = norm_forward(after_two, last_layernorm_scale)
    layer_out = joined(from_mp(final_low))

    codes = book_all.shape[0]
    logits = dot_nt(final_low, book_all) * D ** (-0.5)
    is_target = rel_rows(expected_entries, 0)[:, None] == jnp.arange(codes, dtype=jnp.int32)[None, :]
    pred_lse = jax.nn.logsumexp(logits, -1)
    row_loss = pred_lse - jnp.sum(jnp.where(is_target, logits, 0.0), -1)
    frame_loss = joined(from_mp(row_loss))
    grad_pred = (jnp.exp(logits - pred_lse[:, None]) - is_target.astype(WIDE)).astype(LOW)
    grad_final = rel_rows(result_adjoint, 0).astype(WIDE) + dot(grad_pred, book_all) * D ** (-0.5)
    own_codes = entry_vectors.shape[0]
    book_pieces = [
        [dot_tn(part, final_low) * D ** (-0.5) for part in halves_of(grad_pred, own_codes, k)]
        for k in range(mp_count)
    ]

    temper = smoothing_level[0]
    noisy = dot(acoustic_features, quantizer_projection) - jnp.log(-jnp.log(random_flat_samples))
    tempered = noisy / temper
    top = jnp.max(tempered, -1)
    total = jnp.sum(jnp.exp(tempered - top[:, None]), -1)
    stats = from_mp(jnp.stack([top, total]))
    full_top = functools.reduce(jnp.maximum, [s[0] for s in stats])
    full_total = sum(s[1] * jnp.exp(s[0] - full_top) for s in stats)
    assigned = jnp.exp(tempered - (full_top + jnp.log(full_total))[:, None])
    assigned_low = assigned.astype(LOW)
    quant_own = to_mp([dot(rel_rows(assigned_low, k), entry_vectors) for k in range(mp_count)])
    quantized = joined(from_mp(quant_own.astype(LOW)))
    grad_soft = dot_nt(discrete_adjoint, entry_vectors)
    row_dot = sum(from_mp(jnp.sum(assigned * grad_soft, -1)))
    grad_tempered = assigned * (grad_soft - row_dot[:, None])
    grad_temper = -jnp.sum(grad_tempered * noisy) / (temper * temper)
    grad_entry = (grad_tempered / temper).astype(LOW)
    quant_in = to_mp([dot_nt(rel_rows(grad_entry, k), quantizer_projection) for k in range(mp_count)])
    code_grad = summed_grad([[dot_tn(acoustic_features, p) for p in local_halves(grad_entry)]], True)
    soft_halves = [dot_tn(p, discrete_adjoint) for p in local_halves(assigned_low)]
    book_pieces[0] = [a + b for a, b in zip(book_pieces[0], soft_halves)]
    book_grad = summed_grad(book_pieces, False)

    grad_four, grad_ln_final = norm_backward(grad_final, last_layernorm_scale, final_normed, final_inverse)
    late_branch = (0.5 * grad_four).astype(LOW)
    late_in = 0.0
    grad_hidden = []
    for w_in, w_back, hidden in zip(ups, downs, late_hidden):
        grad_act = dot_nt(late_branch, w_back)
        grad_hid = (grad_act * silu_slope(hidden, jax.nn.sigmoid(hidden))).astype(LOW)
        grad_hidden.append(grad_hid)
        late_in = late_in + dot_nt(grad_hid, w_in)

    def pieced(parts):
        flat = local_halves(parts[0]) + parts[1:]
        return [flat[2 * k : 2 * k + 2] for k in range(mp_count)]

    down2_grad = summed_grad([[dot_tn(p, late_branch) for p in pair] for pair in pieced(late_act)], False)
    up2_grad = summed_grad([[dot_tn(late_entered, p) for p in pair] for pair in pieced(grad_hidden)], True)
    late_norm_grad, grad_ln_ffn2 = norm_backward(late_in, later_layernorm_scale, late_normed, late_inverse)
    grad_three = grad_four + late_norm_grad

    conv_branch = grad_three.astype(LOW)
    own_channels = filter_exit_projection.shape[0]
    point_grad = summed_grad(
        [[dot_tn(p, conv_branch) for p in halves_of(swish_low, own_channels, k)] for k in range(mp_count)], False
    )
    grad_swish = dot_nt(conv_branch, point_all)
    grad_bn = grad_swish * silu_slope(bn_out, bn_sigma)
    back_sums = lax.psum(jnp.stack([jnp.sum(grad_bn, 0), jnp.sum(grad_bn * bn_hat, 0)]), BOTH)
    grad_conv = (
        factor_all * bn_inv * (grad_bn - back_sums[0] / all_rows - bn_hat * back_sums[1] / all_rows)
    ).astype(LOW)
    grad_padded = padded(grad_conv)
    grad_exact = grad_conv.astype(WIDE)
    grad_taps = []
    grad_gated = jnp.zeros_like(grad_exact)
    for j in range(KERNEL):
        grad_taps.append(jnp.sum(grad_exact * jnp.where(masks[j], glu_padded[j : j + own], 0.0), 0))
        back = 2 * half_kernel - j
        grad_gated = grad_gated + filter_all[j][None, :] * jnp.where(
            masks[back], grad_padded[back : back + own], 0.0
        )
    grad_value = (grad_gated * glu_gate).astype(LOW)
    grad_gate = (grad_gated * glu_value * glu_gate * (1.0 - glu_gate)).astype(LOW)
    gate_grads = [
        summed_grad(
            [[dot_tn(conv_entered, p) for p in halves_of(g, own_channels, k)] for k in range(mp_count)], True
        )
        for g in (grad_value, grad_gate)
    ]
    conv_in = dot_nt(grad_value, gating_all[0]) + dot_nt(grad_gate, gating_all[1])
    conv_norm_grad, grad_ln_conv = norm_backward(conv_in, filter_layernorm_scale, conv_normed, conv_inverse)
    grad_two = grad_three + conv_norm_grad

    att_branch = grad_two.astype(LOW)
    exit_grad = summed_grad(
        [
            [dot_tn(p, att_branch) for p in halves_of(att_low, local_heads * HEAD, k)]
            for k in range(mp_count)
        ],
        False,
    )
    grad_heads = dot_nt(att_branch, exit_all).astype(LOW)
    grad_heads = jnp.transpose(
        grad_heads.reshape(own, mp_count, local_heads, HEAD), (2, 1, 0, 3)
    ).reshape(local_heads * mp_count, own, HEAD)
    grad_mixed = exchange(grad_heads).reshape(group_rows, HEAD)
    delta = jnp.sum(grad_mixed.astype(WIDE) * mixed, -1)
    grad_query, grad_kv = attend_back(query_rot, grad_mixed, kv, place, row_lse, delta)
    kv_grad = grad_kv[middle]
    edge = halo_rows
    for r, n in zip(reaches, halo):
        edge -= n
        back = seq_shift(grad_kv[edge : edge + n].astype(LOW), -local_heads * r)
        kv_grad = kv_grad.at[group_rows - n :].add(back.astype(WIDE))
    edge = halo_rows + group_rows
    for r, n in zip(reaches, halo):
        back = seq_shift(grad_kv[edge : edge + n].astype(LOW), local_heads * r)
        kv_grad = kv_grad.at[:n].add(back.astype(WIDE))
        edge += n
    grad_proj = jnp.concatenate(
        [
            rotary(grad_query * SCALE, group_pos, -1.0).astype(LOW),
            rotary(kv_grad[:, :HEAD] * SCALE, group_pos, -1.0).astype(LOW),
            kv_grad[:, HEAD:].astype(LOW),
        ],
        1,
    )
    head_grad = halved(dot_tn(att_group, grad_proj).astype(LOW), int(math.log2(local_heads)))
    head_every = lax.all_gather(head_grad, "seq", axis=0)
    bits = int(math.log2(seq_count))
    low_bits = int(math.log2(local_heads))
    head_rows = head_grad.shape[0]
    head_every = head_every.reshape([2] * (bits - low_bits) + [local_heads, head_rows, 3, HEAD])
    outer = bits - low_bits
    head_every = jnp.transpose(
        head_every, [outer + 2] + list(range(outer))[::-1] + [outer + 1, outer, outer + 3]
    )
    qkv_grad = head_every.reshape(3, D, local_heads * HEAD).astype(WIDE)

    blocks = grad_proj.reshape(local_heads, mp_count, own, 3 * HEAD)
    if local_heads > 1:
        split = blocks.reshape(local_heads // 2, 2, mp_count, own, 3 * HEAD)
        sides = [
            dot_nt(cut(split, core ^ j, 1, 1).reshape(-1, 3 * HEAD), head_matrix).astype(LOW) for j in range(2)
        ]
        held = sides[0] + seq_xor(sides[1], 1)
        outer_count = local_heads // 2
    else:
        held = dot_nt(grad_proj, head_matrix).astype(LOW)
        outer_count = 1
    held = held.reshape(outer_count, mp_count, own, D)
    att_in = 0.0
    outer_at = (seq_at % local_heads) // 2 if local_heads > 1 else 0
    for mask in range(outer_count):
        for k in range(mp_count):
            term = lax.dynamic_slice(held, (outer_at ^ mask, mp_place(k), 0, 0), (1, 1, own, D))[0, 0]
            if mask or k:
                pairs = [
                    (s * mp_count + m, (s ^ (2 * mask)) * mp_count + (m + k) % mp_count)
                    for s in range(seq_count)
                    for m in range(mp_count)
                ]
                term = lax.ppermute(term, BOTH, pairs)
            att_in = att_in + term.astype(WIDE)
    att_norm_grad, grad_ln_att = norm_backward(att_in, mixer_layernorm_scale, att_normed, att_inverse)
    grad_one = grad_two + att_norm_grad

    early_branch = from_mp((0.5 * grad_one).astype(LOW))
    early_in, early_grads = [], []
    for k, (_, entered, hidden, activated, _, _) in enumerate(first):
        grad_act = dot_nt(early_branch[k], early_narrowing_matrix)
        early_grads.append((grad_act * silu_slope(hidden, jax.nn.sigmoid(hidden))).astype(LOW))
        early_in.append(dot_nt(early_grads[k], early_widening_matrix))

    def stacked(parts):
        return jnp.concatenate(parts, 0)

    act_all, branch_all = stacked([f[3] for f in first]), stacked(early_branch)
    entered_all, hid_all = stacked([f[1] for f in first]), stacked(early_grads)
    down1_grad = summed_grad([[dot_tn(p, branch_all) for p in local_halves(act_all)]], False)
    up1_grad = summed_grad([[dot_tn(entered_all, p) for p in local_halves(hid_all)]], True)
    early_norm_grad, grad_ln_ffn1 = norm_backward(to_mp(early_in), early_layernorm_scale, first[0][4], first[0][5])
    grad_frames = joined(from_mp((grad_one + early_norm_grad + quant_in).astype(LOW)))

    small = lax.psum(
        jnp.concatenate(
            [grad_ln_ffn1, grad_ln_att, grad_ln_conv, grad_ln_ffn2, grad_ln_final]
            + grad_taps
            + [jnp.full((D,), grad_temper, WIDE)]
        ),
        BOTH,
    ).reshape(-1, D)

    def own_part(array):
        return cut(array, mp_at * own_channels, own_channels, array.ndim - 1)

    return (
        layer_out,
        quantized,
        frame_loss,
        grad_frames,
        small[0],
        up1_grad,
        down1_grad,
        small[1],
        qkv_grad,
        exit_grad,
        small[2],
        jnp.stack(gate_grads),
        own_part(small[5 : 5 + KERNEL]),
        own_part(back_sums[1]),
        own_part(back_sums[0]),
        point_grad,
        small[3],
        up2_grad,
        down2_grad,
        small[4],
        code_grad,
        book_grad,
        small[5 + KERNEL, :1],
    )


def solution(mesh):
    in_specs = (
        P("seq", None),
        P(),
        P(),
        P(None, "mp"),
        P("mp", None),
        P(),
        P(None, None, "mp"),
        P("mp", None),
        P(),
        P(None, None, "mp"),
        P(None, "mp"),
        P("mp"),
        P("mp"),
        P("mp", None),
        P(),
        P(None, "mp"),
        P("mp", None),
        P(),
        P(None, "mp"),
        P("mp", None),
        P(),
        P("seq", "mp"),
        P("seq"),
        P("seq", None),
        P("seq", None),
    )
    out_specs = (
        P("seq", None),
        P("seq", None),
        P("seq"),
        P("seq", None),
        P(),
        P(None, "mp"),
        P("mp", None),
        P(),
        P(None, None, "mp"),
        P("mp", None),
        P(),
        P(None, None, "mp"),
        P(None, "mp"),
        P("mp"),
        P("mp"),
        P("mp", None),
        P(),
        P(None, "mp"),
        P("mp", None),
        P(),
        P(None, "mp"),
        P("mp", None),
        P(),
    )
    return jax.shard_map(
        on_device, mesh=mesh, in_specs=in_specs, out_specs=out_specs, check_vma=False
    )
```

time: 2540 us -> 1490 us (0.59)
  waiting for transfers between devices: 1330 us -> 510 us
  matrix products: 583 us -> 221 us
  starting transfers between devices: 43.7 us -> 170 us
  other arithmetic: 237 us -> 150 us
  Pallas kernels: 0 us -> 64.6 us
  local copies, waits for them, and re-layouts: 153 us -> 200 us
    psum x9 -> x0, waiting for transfers between devices: 508 us -> none  [model_total(): lax.psum(shortened(partial_terms), 'mp')]
    reduce_scatter x8 -> x0, waiting for transfers between devices: 463 us -> none  [the longest x1 81.3 us: on_device(): lax.psum_scatter(grad_down2.astype(jnp.bfloat16), 'seq', scatter_dimensio...]
    dot_general x82 -> x76, matrix products: 583 us -> 221 us  [dot(): return lax.dot_general(a, b, (dims, ((), ())), preferred_element_type=WIDE)]
    ppermute x16 -> x92, waiting for transfers between devices: 295 us -> 510 us  [the longest x56 293 us: seq_xor(): lax.ppermute(shard, 'seq', [(i, i ^ mask) for i in range(lax.axis_size('s...]
    ppermute x16 -> x92, starting transfers between devices: 40.8 us -> 160 us  [the longest x56 103 us: seq_xor(): lax.ppermute(shard, 'seq', [(i, i ^ mask) for i in range(lax.axis_size('s...]
    all_gather x10 -> x12, waiting for transfers between devices: 65.4 us -> 0.54 us  [the longest x1 0.5 us: on_device(): lax.all_gather(att_entered, BOTH, axis_index_groups=groups, axis=0, tiled...]
    pallas_call x0 -> x2, Pallas kernels: none -> 64.6 us  [the longest x1 36.9 us: attend_back(): pl.pallas_call(functools.partial(attend_back_kernel, depth=depth), grid_s...]
    convert_element_type x2 -> x17, local copies, waits for them, and re-layouts: 13.8 us -> 76.4 us  [the longest x8 32.6 us: summed_grad(): return every.reshape(spread, 2 * columns).astype(WIDE)]
  transfers between devices with their start and end apart: 44 -> 106, of which waited for: 25 -> 42; matrix products, arithmetic and copies ran while one was open for 10% -> 35% of each run, Pallas kernels for 0% -> 4%
where the time goes in v1:
time: 1490 us; the launch traced here: 1480 us
  waiting for transfers between devices  510 us (34%)
  matrix products  221 us (15%)
  local copies, waits for them, and re-layouts  200 us (13%)
  starting transfers between devices  170 us (11%)
  other arithmetic  150 us (10%)
  blocking collectives  140 us (9%)
  Pallas kernels  64.6 us (4%)
  between operations  20.4 us (1%)
    ppermute x56, waiting for transfers between devices, seq_xor(): lax.ppermute(shard, 'seq', [(i, i ^ mask) for i in range(lax.axis_size('s...  293 us
    dot_general x76, matrix products, dot(): return lax.dot_general(a, b, (dims, ((), ())), preferred_element_type=WIDE)  221 us
    ppermute x25, waiting for transfers between devices, mp_shift(): lax.ppermute(shard, 'mp', [(i, (i + by) % count) for i in range(count)])  180 us
    ppermute x56, starting transfers between devices, seq_xor(): lax.ppermute(shard, 'seq', [(i, i ^ mask) for i in range(lax.axis_size('s...  103 us
    psum x1, blocking collectives, on_device(): lax.psum(jnp.concatenate([grad_ln_ffn1, grad_ln_att, grad_ln_conv, grad_l...  53.6 us
    unnamed x333, local copies, waits for them, and re-layouts  48.7 us
    psum x1, blocking collectives, on_device(): lax.psum(jnp.stack([jnp.sum(conv_out, 0), jnp.sum(conv_out * conv_out, 0)...  47.2 us
    psum x1, blocking collectives, on_device(): lax.psum(jnp.stack([jnp.sum(grad_bn, 0), jnp.sum(grad_bn * bn_hat, 0)]),...  39.5 us
  transfers between devices with their start and end apart: 106, of which 42 were waited for; matrix products, arithmetic and copies ran while one was open for 35% of the time, Pallas kernels for 4%

profile of v1, /device:TPU:0, one launch (start us, length us, event | category | flops | bytes accessed | tf_op | source)
XLA Modules:
  0.0 1476.4 jit_solution(14369903362717656822)
XLA Ops:
  30.4 18.4 %collective-permute-done = bf16[512,1024]{1,0:T(8,128)(2,1)S(1)} collective-permute-done((bf16[512,1024]{1,0:T(8,128)(2,1)S(1)}, bf16[512,1024]{1,0:T(8,128)(2,1)S(1)}, u32[]{:S(2)}, u32[]{:S(2)}) %collective-permute-start) | collective-permute-done | bytes 1048608 | tf_op jit(solution)/shard_map/ppermute | solution.py:42
  154.8 28.1 %collective-permute-done.84 = bf16[256,256]{0,1:T(8,128)(2,1)S(1)} collective-permute-done((bf16[256,256]{0,1:T(8,128)(2,1)S(1)}, bf16[256,256]{0,1:T(8,128)(2,1)S(1)}, u32[]{:S(2)}, u32[]{:S(2)}) %collective-permute-start.84) | collective-permute-done | bytes 131104 | tf_op jit(solution)/shard_map/ppermute | solution.py:46
  185.2 23.0 %pad_maximum_fusion.kv_ref = bf16[10240,256]{1,0:T(8,128)(2,1)} fusion(bf16[3072,256]{1,0:T(8,128)(2,1)S(1)} %collective-permute-done.2, bf16[4096,128]{1,0:T(8,128)(2,1)S(1)} %slice.515, bf16[4096,64]{1,0:T(8,128)(2,1)S(1)} %get-tuple-element.115, bf16[4096,64]{1,0:T(8,128)(2,1)S(1)} %get-tuple-element.114, bf16[3072,256]{1,0:T(8,128)(2,1)S(1)} %collective-permute-done.1), kind=kLoop, calls=%fused_computation.4 | loop fusion | flops 26214400 | bytes 10485760 | tf_op jit(solution)/shard_map/concatenate | solution.py:412
  208.3 27.7 %attend.1 = (bf16[4096,128]{1,0:T(8,128)(2,1)}, f32[4096,128]{1,0:T(8,128)}, f32[4096,1]{1,0:T(8,128)}) custom-call(s32[8]{0:T(128)S(1)} %get-tuple-element.200.lo_ref, s32[8]{0:T(128)S(1)} %get-tuple-element.168.hi_ref, bf16[4096,128]{1,0:T(8,128)(2,1)S(1)} %pad_maximum_fusion.8.q_ref, bf16[10240,256]{1,0:T(8,128)(2,1)} %pad_maximum_fusion.kv_ref, ...), custom_call_target="tpu_custom_call" | custom-call | flops 6308233216 | bytes 16777216 | tf_op jit(solution)/shard_map/attend/pallas_call | solution.py:235
  239.6 28.1 %collective-permute-start.85 = (bf16[128,256]{0,1:T(8,128)(2,1)S(1)}, bf16[128,256]{0,1:T(8,128)(2,1)S(1)}, u32[]{:S(2)}, u32[]{:S(2)}) collective-permute-start(bf16[128,256]{0,1:T(8,128)(2,1)S(1)} %constant_dynamic-slice_fusion.3), channel_id=1, source_target_pairs={{0,16},{2,18},{4,20},{6,22},{8,24},{10,26},{12,28},{14,30},{16,0},... | collective-permute-start | bytes 196616 | tf_op jit(solution)/shard_map/ppermute | solution.py:46
  304.7 13.3 collective-permute-done.12
  325.6 47.2 %psum.21 = f32[2,1024]{1,0:T(2,128)S(1)} all-reduce(f32[2,1024]{1,0:T(2,128)S(1)} %pad_maximum_fusion.10), channel_id=1, replica_groups=mesh['seq'=16,'mp'=2] {'seq','mp'}, use_global_device_ids=true, to_apply=%region_15.16 | all-reduce | flops 2048 | bytes 16384 | tf_op jit(solution)/shard_map/psum | solution.py:444
  442.1 39.5 %psum.22 = f32[2,1024]{1,0:T(2,128)S(1)} all-reduce(f32[2,1024]{1,0:T(2,128)S(1)} %pad_maximum_fusion.12), channel_id=1, replica_groups=mesh['seq'=16,'mp'=2] {'seq','mp'}, use_global_device_ids=true, to_apply=%region_31.32 | all-reduce | flops 2048 | bytes 16384 | tf_op jit(solution)/shard_map/psum | solution.py:531
  540.4 12.5 collective-permute-done.66
  623.7 36.9 %attend_back.1 = (f32[4096,128]{1,0:T(8,128)}, f32[10240,256]{1,0:T(8,128)}) custom-call(s32[8]{0:T(128)} %get-tuple-element.201.lo_ref, s32[8]{0:T(128)} %get-tuple-element.167.hi_ref, bf16[4096,128]{1,0:T(8,128)(2,1)} %copy-done.2, bf16[4096,128]{1,0:T(8,128)(2,1)} %bitcast.36.do_ref, bf16[10240,256]{1,0:T(8,128)(2,1)} %pad_maximum_fusion.kv_ref, ...), custom_call_target="tpu_custom_call" | custom-call | flops 15770583040 | bytes 33554432 | tf_op jit(solution)/shard_map/attend_back/pallas_call | solution.py:298
  682.2 31.3 %collective-permute-start.62 = (bf16[256,256]{1,0:T(8,128)(2,1)S(1)}, bf16[256,256]{1,0:T(8,128)(2,1)S(1)}, u32[]{:S(2)}, u32[]{:S(2)}) collective-permute-start(bf16[256,256]{1,0:T(8,128)(2,1)S(1)} %constant_dynamic-slice_fusion.19), channel_id=1, source_target_pairs={{0,8},{2,10},{4,12},{6,14},{8,0},{10,2},{12,4},{14,6},{16,24},{18,... | collective-permute-start | bytes 393224 | tf_op jit(solution)/shard_map/ppermute | solution.py:46
  741.1 21.1 %collective-permute-done.57 = bf16[128,256]{1,0:T(8,128)(2,1)S(1)} collective-permute-done((bf16[128,256]{1,0:T(8,128)(2,1)S(1)}, bf16[128,256]{1,0:T(8,128)(2,1)S(1)}, u32[]{:S(2)}, u32[]{:S(2)}) %collective-permute-start.57) | collective-permute-done | bytes 65568 | tf_op jit(solution)/shard_map/ppermute | solution.py:46
  776.3 11.2 fusion.49
  804.0 10.8 collective-permute-done.44
  830.7 44.0 %collective-permute-done.72 = bf16[1024,1024]{1,0:T(8,128)(2,1)S(1)} collective-permute-done((bf16[1024,1024]{1,0:T(8,128)(2,1)S(1)}, bf16[1024,1024]{1,0:T(8,128)(2,1)S(1)}, u32[]{:S(2)}, u32[]{:S(2)}) %collective-permute-start.72) | collective-permute-done | bytes 2097184 | tf_op jit(solution)/shard_map/ppermute | solution.py:42
  878.2 20.8 %collective-permute-done.73 = bf16[512,1024]{1,0:T(8,128)(2,1)S(1)} collective-permute-done((bf16[512,1024]{1,0:T(8,128)(2,1)S(1)}, bf16[512,1024]{1,0:T(8,128)(2,1)S(1)}, u32[]{:S(2)}, u32[]{:S(2)}) %collective-permute-start.73) | collective-permute-done | bytes 1048608 | tf_op jit(solution)/shard_map/ppermute | solution.py:46
  915.8 12.0 collective-permute-done.75
  942.8 46.2 %collective-permute-done.78 = bf16[1024,1024]{1,0:T(8,128)(2,1)S(1)} collective-permute-done((bf16[1024,1024]{1,0:T(8,128)(2,1)S(1)}, bf16[1024,1024]{1,0:T(8,128)(2,1)S(1)}, u32[]{:S(2)}, u32[]{:S(2)}) %collective-permute-start.78) | collective-permute-done | bytes 2097184 | tf_op jit(solution)/shard_map/ppermute | solution.py:42
  989.6 24.3 %collective-permute-done.79 = bf16[512,1024]{1,0:T(8,128)(2,1)} collective-permute-done((bf16[512,1024]{1,0:T(8,128)(2,1)S(1)}, bf16[512,1024]{1,0:T(8,128)(2,1)}, u32[]{:S(2)}, u32[]{:S(2)}) %collective-permute-start.79) | collective-permute-done | bytes 1048608 | tf_op jit(solution)/shard_map/ppermute | solution.py:46
  1028.7 11.3 collective-permute-done.81
  1041.1 9.5 collective-permute-done.30
  1050.6 26.4 %collective-permute-done.29 = bf16[512,1024]{1,0:T(8,128)(2,1)} collective-permute-done((bf16[512,1024]{1,0:T(8,128)(2,1)}, bf16[512,1024]{1,0:T(8,128)(2,1)}, u32[]{:S(2)}, u32[]{:S(2)}) %collective-permute-start.29) | collective-permute-done | bytes 1048608 | tf_op jit(solution)/shard_map/ppermute | solution.py:626
  1088.1 12.8 collective-permute-done.31
  1115.4 24.0 %collective-permute-done.37 = bf16[512,1024]{1,0:T(8,128)(2,1)S(1)} collective-permute-done((bf16[512,1024]{1,0:T(8,128)(2,1)S(1)}, bf16[512,1024]{1,0:T(8,128)(2,1)S(1)}, u32[]{:S(2)}, u32[]{:S(2)}) %collective-permute-start.37) | collective-permute-done | bytes 1048608 | tf_op jit(solution)/shard_map/ppermute | solution.py:46
  1141.9 11.4 collective-permute-done.38
  1155.1 11.7 collective-permute-done.39
  1182.0 32.3 %collective-permute-done.41 = bf16[512,1024]{1,0:T(8,128)(2,1)S(1)} collective-permute-done((bf16[512,1024]{1,0:T(8,128)(2,1)S(1)}, bf16[512,1024]{1,0:T(8,128)(2,1)S(1)}, u32[]{:S(2)}, u32[]{:S(2)}) %collective-permute-start.41) | collective-permute-done | bytes 1048608 | tf_op jit(solution)/shard_map/ppermute | solution.py:46
  1217.2 14.8 %collective-permute-done.42 = bf16[256,1024]{1,0:T(8,128)(2,1)S(1)} collective-permute-done((bf16[256,1024]{1,0:T(8,128)(2,1)S(1)}, bf16[256,1024]{1,0:T(8,128)(2,1)S(1)}, u32[]{:S(2)}, u32[]{:S(2)}) %collective-permute-start.42) | collective-permute-done | bytes 524320 | tf_op jit(solution)/shard_map/ppermute | solution.py:46
  1233.2 12.3 collective-permute-done.43
  1266.3 18.7 %collective-permute-done.22 = f32[512]{0:T(512)S(1)} collective-permute-done((f32[512]{0:T(512)S(1)}, f32[512]{0:T(512)S(1)}, u32[]{:S(2)}, u32[]{:S(2)}) %collective-permute-start.22) | collective-permute-done | bytes 2080 | tf_op jit(solution)/shard_map/ppermute | solution.py:42
  1356.6 53.6 %psum.23 = f32[11264]{0:T(1024)S(1)} all-reduce(f32[11264]{0:T(1024)S(1)} %constant_dynamic-update-slice_fusion.20), channel_id=1, replica_groups=mesh['seq'=16,'mp'=2] {'seq','mp'}, use_global_device_ids=true, to_apply=%region_51.52 | all-reduce | flops 11264 | bytes 90112 | tf_op jit(solution)/shard_map/psum | solution.py:648
  1443.9 9.7 copy.154
  (847 shorter events, 711.2 us)
Async XLA Ops:
  8.0 114.1 %all-gather.24.cloned.1.call-start = ((), (), s32[]{:S(2)}) async-start(), calls=%async_computation.2 | async-start | bytes 9437184 | tf_op jit(solution)/shard_map/all_gather | solution.py:393
  56.6 92.0 %collective-permute-start.3 = (bf16[256,1024]{1,0:T(8,128)(2,1)}, bf16[256,1024]{1,0:T(8,128)(2,1)}, u32[]{:S(2)}, u32[]{:S(2)}) collective-permute-start(bf16[256,1024]{1,0:T(8,128)(2,1)} %constant_dynamic-slice_fusion.42), channel_id=1, source_target_pairs={{0,1},{1,0},{2,3},{3,2},{4,5},{5,4},{6,7},{7,6},{8,9},{9,8},{10,11... | collective-permute-start | bytes 1572872 | tf_op jit(solution)/shard_map/ppermute | solution.py:42
  58.4 83.4 %collective-permute-start.5 = (f32[7,512]{1,0:T(8,128)S(1)}, f32[7,512]{1,0:T(8,128)S(1)}, u32[]{:S(2)}, u32[]{:S(2)}) collective-permute-start(f32[7,512]{1,0:T(8,128)S(1)} %get-tuple-element.111), channel_id=1, source_target_pairs={{0,1},{1,0},{2,3},{3,2},{4,5},{5,4},{6,7},{7,6},{8,9},{9,8},{10,11... | collective-permute-start | bytes 43016 | tf_op jit(solution)/shard_map/ppermute | solution.py:42
  60.6 91.4 %collective-permute-start.10 = (bf16[256,1024]{1,0:T(8,128)(2,1)}, bf16[256,1024]{1,0:T(8,128)(2,1)}, u32[]{:S(2)}, u32[]{:S(2)}) collective-permute-start(bf16[256,1024]{1,0:T(8,128)(2,1)} %constant_dynamic-slice_fusion.40), channel_id=1, source_target_pairs={{0,1},{1,0},{2,3},{3,2},{4,5},{5,4},{6,7},{7,6},{8,9},{9,8},{10,11... | collective-permute-start | bytes 1572872 | tf_op jit(solution)/shard_map/ppermute | solution.py:42
  152.0 152.7 %collective-permute-start.13 = (bf16[1024,1024]{1,0:T(8,128)(2,1)}, bf16[1024,1024]{1,0:T(8,128)(2,1)}, u32[]{:S(2)}, u32[]{:S(2)}) collective-permute-start(bf16[1024,1024]{1,0:T(8,128)(2,1)} %constant_dynamic-slice_fusion.38), channel_id=1, source_target_pairs={{0,1},{1,0},{2,3},{3,2},{4,5},{5,4},{6,7},{7,6},{8,9},{9,8},{10,11... | collective-permute-start | bytes 6291464 | tf_op jit(solution)/shard_map/ppermute | solution.py:42
  182.9 56.7 %collective-permute-start.20 = (bf16[256,1024]{1,0:T(8,128)(2,1)}, bf16[256,1024]{1,0:T(8,128)(2,1)}, u32[]{:S(2)}, u32[]{:S(2)}) collective-permute-start(bf16[256,1024]{1,0:T(8,128)(2,1)} %constant_dynamic-slice_fusion.37), channel_id=1, source_target_pairs={{0,1},{1,0},{2,3},{3,2},{4,5},{5,4},{6,7},{7,6},{8,9},{9,8},{10,11... | collective-permute-start | bytes 1572872 | tf_op jit(solution)/shard_map/ppermute | solution.py:42
  184.6 88.1 %collective-permute-start.4 = (bf16[256,1024]{1,0:T(8,128)(2,1)}, bf16[256,1024]{1,0:T(8,128)(2,1)}, u32[]{:S(2)}, u32[]{:S(2)}) collective-permute-start(bf16[256,1024]{1,0:T(8,128)(2,1)} %collective-permute-done.3), channel_id=1, source_target_pairs={{0,2},{2,0},{4,6},{6,4},{8,10},{10,8},{12,14},{14,12},{16,18},{18,... | collective-permute-start | bytes 1572872 | tf_op jit(solution)/shard_map/ppermute | solution.py:46
  184.7 89.9 %collective-permute-start.11 = (bf16[256,1024]{1,0:T(8,128)(2,1)}, bf16[256,1024]{1,0:T(8,128)(2,1)}, u32[]{:S(2)}, u32[]{:S(2)}) collective-permute-start(bf16[256,1024]{1,0:T(8,128)(2,1)} %collective-permute-done.10), channel_id=1, source_target_pairs={{0,2},{2,0},{4,6},{6,4},{8,10},{10,8},{12,14},{14,12},{16,18},{18,... | collective-permute-start | bytes 1572872 | tf_op jit(solution)/shard_map/ppermute | solution.py:46
  185.1 93.6 %collective-permute-start.7 = (bf16[2,1024,256]{2,1,0:T(8,128)(2,1)}, bf16[2,1024,256]{2,1,0:T(8,128)(2,1)}, u32[]{:S(2)}, u32[]{:S(2)}) collective-permute-start(bf16[2,1024,256]{2,1,0:T(8,128)(2,1)} %collective-permute-done.6), channel_id=1, source_target_pairs={{0,2},{2,0},{4,6},{6,4},{8,10},{10,8},{12,14},{14,12},{16,18},{18,... | collective-permute-start | bytes 3145736 | tf_op jit(solution)/shard_map/ppermute | solution.py:46
  239.5 1013.8 %all-gather.44.cloned.1.call-start = ((), (), s32[]{:S(2)}) async-start(), calls=%async_computation.12 | async-start | bytes 1114112 | tf_op jit(solution)/shard_map/all_gather | solution.py:125
  304.7 90.7 %collective-permute-start.15 = (bf16[1024,1024]{1,0:T(8,128)(2,1)}, bf16[1024,1024]{1,0:T(8,128)(2,1)}, u32[]{:S(2)}, u32[]{:S(2)}) collective-permute-start(bf16[1024,1024]{1,0:T(8,128)(2,1)} %collective-permute-done.13), channel_id=1, source_target_pairs={{0,2},{2,0},{4,6},{6,4},{8,10},{10,8},{12,14},{14,12},{16,18},{18,... | collective-permute-start | bytes 6291464 | tf_op jit(solution)/shard_map/ppermute | solution.py:46
  318.0 64.8 %collective-permute-start.14 = (bf16[1024,1024]{1,0:T(8,128)(2,1)}, bf16[1024,1024]{1,0:T(8,128)(2,1)}, u32[]{:S(2)}, u32[]{:S(2)}) collective-permute-start(bf16[1024,1024]{1,0:T(8,128)(2,1)} %collective-permute-done.12), channel_id=1, source_target_pairs={{0,2},{2,0},{4,6},{6,4},{8,10},{10,8},{12,14},{14,12},{16,18},{18,... | collective-permute-start | bytes 6291464 | tf_op jit(solution)/shard_map/ppermute | solution.py:46
  496.6 328.9 %collective-permute-start.71 = (bf16[1024,1024]{1,0:T(8,128)(2,1)}, bf16[1024,1024]{1,0:T(8,128)(2,1)}, u32[]{:S(2)}, u32[]{:S(2)}) collective-permute-start(bf16[1024,1024]{1,0:T(8,128)(2,1)} %convolution_convert_fusion.3), channel_id=1, source_target_pairs={{0,2},{2,0},{4,6},{6,4},{8,10},{10,8},{12,14},{14,12},{16,18},{18,... | collective-permute-start | bytes 6291464 | tf_op jit(solution)/shard_map/ppermute | solution.py:46
  499.8 76.9 %collective-permute-start.86 = (bf16[256,1024]{1,0:T(8,128)(2,1)}, bf16[256,1024]{1,0:T(8,128)(2,1)}, u32[]{:S(2)}, u32[]{:S(2)}) collective-permute-start(bf16[256,1024]{1,0:T(8,128)(2,1)} %fusion.105), channel_id=1, source_target_pairs={{0,2},{2,0},{4,6},{6,4},{8,10},{10,8},{12,14},{14,12},{16,18},{18,... | collective-permute-start | bytes 1572872 | tf_op jit(solution)/shard_map/ppermute | solution.py:46
  527.3 766.5 %all-gather.38.cloned.1.call-start = ((), (), s32[]{:S(2)}) async-start(), calls=%async_computation.9 | async-start | bytes 1114112 | tf_op jit(solution)/shard_map/all_gather | solution.py:125
  576.6 720.2 %all-gather.46.cloned.1.call-start = ((), (), s32[]{:S(2)}) async-start(), calls=%async_computation.13 | async-start | bytes 1114112 | tf_op jit(solution)/shard_map/all_gather | solution.py:125
  576.7 96.0 %collective-permute-start.58 = (bf16[1024,256]{1,0:T(8,128)(2,1)}, bf16[1024,256]{1,0:T(8,128)(2,1)}, u32[]{:S(2)}, u32[]{:S(2)}) collective-permute-start(bf16[1024,256]{1,0:T(8,128)(2,1)} %convolution_convert_fusion.17), channel_id=1, source_target_pairs={{0,2},{2,0},{4,6},{6,4},{8,10},{10,8},{12,14},{14,12},{16,18},{18,... | collective-permute-start | bytes 1572872 | tf_op jit(solution)/shard_map/ppermute | solution.py:46
  578.4 97.3 %collective-permute-start.52 = (bf16[1024,256]{1,0:T(8,128)(2,1)}, bf16[1024,256]{1,0:T(8,128)(2,1)}, u32[]{:S(2)}, u32[]{:S(2)}) collective-permute-start(bf16[1024,256]{1,0:T(8,128)(2,1)} %convolution_convert_fusion.21), channel_id=1, source_target_pairs={{0,2},{2,0},{4,6},{6,4},{8,10},{10,8},{12,14},{14,12},{16,18},{18,... | collective-permute-start | bytes 1572872 | tf_op jit(solution)/shard_map/ppermute | solution.py:46
  580.3 92.4 %collective-permute-start.60 = (bf16[1024,256]{1,0:T(8,128)(2,1)}, bf16[1024,256]{1,0:T(8,128)(2,1)S(1)}, u32[]{:S(2)}, u32[]{:S(2)}) collective-permute-start(bf16[1024,256]{1,0:T(8,128)(2,1)} %fusion.114), channel_id=1, source_target_pairs={{0,1},{1,0},{2,3},{3,2},{4,5},{5,4},{6,7},{7,6},{8,9},{9,8},{10,11... | collective-permute-start | bytes 1572872 | tf_op jit(solution)/shard_map/ppermute | solution.py:42
  619.0 680.9 %all-gather.32.cloned.1.call-start = ((), (), s32[]{:S(2)}) async-start(), calls=%async_computation.6 | async-start | bytes 1114112 | tf_op jit(solution)/shard_map/all_gather | solution.py:125
  672.6 630.3 %all-gather.36.cloned.1.call-start = ((), (), s32[]{:S(2)}) async-start(), calls=%async_computation.8 | async-start | bytes 1114112 | tf_op jit(solution)/shard_map/all_gather | solution.py:125
  723.6 582.4 %all-gather.34.cloned.1.call-start = ((), (), s32[]{:S(2)}) async-start(), calls=%async_computation.7 | async-start | bytes 1114112 | tf_op jit(solution)/shard_map/all_gather | solution.py:125
  762.9 548.4 %all-gather.30.cloned.1.call-start = ((), (), s32[]{:S(2)}) async-start(), calls=%async_computation.5 | async-start | bytes 3342336 | tf_op jit(solution)/shard_map/all_gather | solution.py:592
  825.5 587.5 %all-gather.40.cloned.1.call-start = ((), (), s32[]{:S(2)}) async-start(), calls=%async_computation.10 | async-start | bytes 4456448 | tf_op jit(solution)/shard_map/all_gather | solution.py:125
  928.6 504.7 %all-gather.42.cloned.1.call-start = ((), (), s32[]{:S(2)}) async-start(), calls=%async_computation.11 | async-start | bytes 4456448 | tf_op jit(solution)/shard_map/all_gather | solution.py:125
  937.8 77.8 %collective-permute-start.27 = (bf16[2048,1024]{1,0:T(8,128)(2,1)}, bf16[2048,1024]{1,0:T(8,128)(2,1)}, u32[]{:S(2)}, u32[]{:S(2)}) collective-permute-start(bf16[2048,1024]{1,0:T(8,128)(2,1)} %convolution_convert_fusion), channel_id=1, source_target_pairs={{0,2},{2,0},{4,6},{6,4},{8,10},{10,8},{12,14},{14,12},{16,18},{18,... | collective-permute-start | bytes 12582920 | tf_op jit(solution)/shard_map/ppermute | solution.py:46
  1023.6 53.4 %collective-permute-start.29 = (bf16[512,1024]{1,0:T(8,128)(2,1)}, bf16[512,1024]{1,0:T(8,128)(2,1)}, u32[]{:S(2)}, u32[]{:S(2)}) collective-permute-start(bf16[512,1024]{1,0:T(8,128)(2,1)} %get-tuple-element.124), channel_id=1, source_target_pairs={{0,4},{1,5},{2,6},{3,7},{4,0},{5,1},{6,2},{7,3},{8,12},{9,13},{10,... | collective-permute-start | bytes 3145736 | tf_op jit(solution)/shard_map/ppermute | solution.py:626
  1040.9 399.8 %all-gather.26.cloned.1.call-start = ((), (), s32[]{:S(2)}) async-start(), calls=%async_computation.3 | async-start | bytes 4456448 | tf_op jit(solution)/shard_map/all_gather | solution.py:125
  1167.5 293.5 %all-gather.28.cloned.1.call-start = ((), (), s32[]{:S(2)}) async-start(), calls=%async_computation.4 | async-start | bytes 4456448 | tf_op jit(solution)/shard_map/all_gather | solution.py:125
  1232.4 52.8 %collective-permute-start.16 = (bf16[512,1024]{1,0:T(8,128)(2,1)S(1)}, bf16[512,1024]{1,0:T(8,128)(2,1)}, u32[]{:S(2)}, u32[]{:S(2)}) collective-permute-start(bf16[512,1024]{1,0:T(8,128)(2,1)S(1)} %copy-done.22), channel_id=1, source_target_pairs={{0,1},{1,0},{2,3},{3,2},{4,5},{5,4},{6,7},{7,6},{8,9},{9,8},{10,11... | collective-permute-start | bytes 3145736 | tf_op jit(solution)/shard_map/ppermute | solution.py:42
  1249.4 98.8 %collective-permute-start.34 = (bf16[512,1024]{1,0:T(8,128)(2,1)}, bf16[512,1024]{1,0:T(8,128)(2,1)}, u32[]{:S(2)}, u32[]{:S(2)}) collective-permute-start(bf16[512,1024]{1,0:T(8,128)(2,1)} %convolution_convert_fusion.6), channel_id=1, source_target_pairs={{0,1},{1,0},{2,3},{3,2},{4,5},{5,4},{6,7},{7,6},{8,9},{9,8},{10,11... | collective-permute-start | bytes 3145736 | tf_op jit(solution)/shard_map/ppermute | solution.py:42
  1354.9 57.1 %collective-permute-start.35 = (bf16[512,1024]{1,0:T(8,128)(2,1)}, bf16[512,1024]{1,0:T(8,128)(2,1)S(1)}, u32[]{:S(2)}, u32[]{:S(2)}) collective-permute-start(bf16[512,1024]{1,0:T(8,128)(2,1)} %get-tuple-element.199), channel_id=1, source_target_pairs={{0,1},{1,0},{2,3},{3,2},{4,5},{5,4},{6,7},{7,6},{8,9},{9,8},{10,11... | collective-permute-start | bytes 3145736 | tf_op jit(solution)/shard_map/ppermute | solution.py:42
  (233 other events, 3254.1 us)
Sparse Core Ops, SparseCore 0:
  54.8 67.2 all-gather.23
Sparse Core Ops, SparseCore 1:
  272.7 37.2 all-gather.43
  576.7 37.3 all-gather.37
  619.0 40.2 all-gather.45
  672.7 66.9 all-gather.31
  741.8 36.7 all-gather.35
  780.8 37.5 all-gather.33
  825.6 45.0 all-gather.29
  928.6 47.5 all-gather.39
  1040.9 52.8 all-gather.41
  1167.6 59.9 all-gather.25
  1246.5 48.2 all-gather.27

commit v2 on v1

v2 whole, which is shorter than its diff:
```python
import functools
import math

import jax
import jax.numpy as jnp
from jax import lax
from jax.experimental import pallas as pl
from jax.experimental.pallas import tpu as pltpu
from jax.sharding import PartitionSpec as P

D = 1024
HEAD = 128
KERNEL = 5
LONGEST = 3008

EPSILON = 1e-05
MASKED = -1e30
SCALE = HEAD ** (-0.5)
SCALE_2 = SCALE * math.log2(math.e)
BOTH = ("seq", "mp")
LOW = jnp.bfloat16
WIDE = jnp.float32


def dot(a, b, dims=((1,), (0,))):
    return lax.dot_general(a, b, (dims, ((), ())), preferred_element_type=WIDE)


def dot_nt(a, b):
    return dot(a, b, ((1,), (1,)))


def dot_tn(a, b):
    return dot(a, b, ((0,), (0,)))


def cut(array, start, size, axis=0):
    return lax.dynamic_slice_in_dim(array, start, size, axis)


def mp_shift(shard, by):
    count = lax.axis_size("mp")
    return lax.ppermute(shard, "mp", [(i, (i + by) % count) for i in range(count)])


def seq_xor(shard, mask):
    return lax.ppermute(shard, "seq", [(i, i ^ mask) for i in range(lax.axis_size("seq"))])


def seq_shift(shard, by):
    count = lax.axis_size("seq")
    return lax.ppermute(shard, "seq", [(i, i + by) for i in range(count) if 0 <= i + by < count])


def flat_shift(shard, by):
    count = lax.axis_size("seq") * lax.axis_size("mp")
    return lax.ppermute(shard, BOTH, [(i, i + by) for i in range(count) if 0 <= i + by < count])


def from_mp(shard):
    return [shard] + [mp_shift(shard, -k) for k in range(1, lax.axis_size("mp"))]


def to_mp(parts):
    total = parts[0].astype(WIDE)
    for k in range(1, len(parts)):
        total = total + mp_shift(parts[k].astype(LOW), k).astype(WIDE)
    return total


def mp_place(k):
    return (lax.axis_index("mp") + k) % lax.axis_size("mp")


def joined(pieces, axis=0):
    size = pieces[0].shape[axis]
    shape = list(pieces[0].shape)
    shape[axis] = size * len(pieces)
    whole = jnp.zeros(shape, pieces[0].dtype)
    for k, piece in enumerate(pieces):
        whole = lax.dynamic_update_slice_in_dim(whole, piece, mp_place(k) * size, axis)
    return whole


def halved(part, bit):
    half = part.shape[1] // 2
    side = (lax.axis_index("seq") >> bit) & 1
    sent = seq_xor(cut(part, (1 - side) * half, half, 1), 1 << bit)
    return cut(part, side * half, half, 1) + sent


def paced(*values):
    return lax.optimization_barrier(values)


def bit_count(number):
    return int(math.log2(number))


def reversed_bits(number, bits):
    out = 0
    for b in range(bits):
        out = out + (((number >> b) & 1) << (bits - 1 - b))
    return out


def laid_kernel(in_ref, out_ref, *, places, turned):
    _, _, rows, width = in_ref.shape
    for s, place in enumerate(places):
        block = in_ref[s, 0].astype(WIDE)
        span = slice(place * rows, (place + 1) * rows)
        if turned:
            out_ref[0, :, span] = block.T
        else:
            out_ref[0, span, :] = block


def laid(every, first, amount, local_heads, turned, width=256):
    count, _, rows, columns = every.shape
    line = count // local_heads
    bits = bit_count(line)
    places = [
        part_of(s % local_heads, local_heads) * line + reversed_bits(s // local_heads, bits) for s in range(count)
    ]
    if count * rows % 128:
        order = sorted(range(count), key=lambda s: places[s])
        whole = jnp.stack([every[s, first : first + amount] for s in order], 1).astype(WIDE)
        whole = whole.reshape(amount, count * rows, columns)
        return jnp.transpose(whole, (0, 2, 1)) if turned else whole
    shape = (columns, count * rows) if turned else (count * rows, columns)
    block = (1, width, count * rows) if turned else (1, count * rows, width)
    return pl.pallas_call(
        functools.partial(laid_kernel, places=places, turned=turned),
        grid=(amount, columns // width),
        in_specs=[pl.BlockSpec((count, 1, rows, width), lambda i, j: (0, first + i, 0, j))],
        out_specs=pl.BlockSpec(block, lambda i, j: (i, j, 0) if turned else (i, 0, j)),
        out_shape=jax.ShapeDtypeStruct((amount,) + shape, WIDE),
        compiler_params=pltpu.CompilerParams(vmem_limit_bytes=32 * 2**20),
        cost_estimate=pl.CostEstimate(
            flops=0, bytes_accessed=6 * amount * shape[0] * shape[1], transcendentals=0
        ),
        name="laid",
    )(every)


def laid_heads_kernel(in_ref, out_ref, *, local_heads, bits):
    rows = in_ref.shape[1]
    for s in range(in_ref.shape[0]):
        block = reversed_bits(s // local_heads, bits)
        head = part_of(s % local_heads, local_heads)
        out_ref[0, block * rows : (block + 1) * rows, head * HEAD : (head + 1) * HEAD] = in_ref[s].astype(WIDE)


def laid_heads(every, local_heads):
    count, rows, _ = every.shape
    shape = (D, local_heads * HEAD)
    return pl.pallas_call(
        functools.partial(
            laid_heads_kernel, local_heads=local_heads, bits=bit_count(count) - bit_count(local_heads)
        ),
        grid=(3,),
        in_specs=[pl.BlockSpec((count, rows, HEAD), lambda i: (0, 0, i))],
        out_specs=pl.BlockSpec((1,) + shape, lambda i: (i, 0, 0)),
        out_shape=jax.ShapeDtypeStruct((3,) + shape, WIDE),
        compiler_params=pltpu.CompilerParams(vmem_limit_bytes=32 * 2**20),
        cost_estimate=pl.CostEstimate(flops=0, bytes_accessed=18 * D * local_heads * HEAD, transcendentals=0),
        name="laid_heads",
    )(every)


def beside_kernel(in_ref, out_ref):
    out_ref[...] = in_ref[0].astype(WIDE)


def beside(halves, down, rows=1024):
    _, height, width = halves.shape
    rows = min(rows, height)
    steps = height // rows
    shape = (2 * height, width) if down else (height, 2 * width)

    def target(j, i):
        return (j * steps + i, 0) if down else (i, j)

    return pl.pallas_call(
        beside_kernel,
        grid=(2, steps),
        in_specs=[pl.BlockSpec((1, rows, width), lambda j, i: (j, i, 0))],
        out_specs=pl.BlockSpec((rows, width), target),
        out_shape=jax.ShapeDtypeStruct(shape, WIDE),
        compiler_params=pltpu.CompilerParams(vmem_limit_bytes=32 * 2**20),
        cost_estimate=pl.CostEstimate(flops=0, bytes_accessed=12 * height * width, transcendentals=0),
        name="beside",
    )(halves)


def remote(source, target, send, recv, device):
    return pltpu.make_async_remote_copy(
        src_ref=source,
        dst_ref=target,
        send_sem=send,
        recv_sem=recv,
        device_id=device,
        device_id_type=pl.DeviceIdType.MESH,
    )


def seq_partner(bit):
    return (lax.axis_index("seq") ^ (1 << bit), lax.axis_index("mp"))


def all_partners(seq_bits, mp_bits):
    mp = lax.axis_index("mp")
    across = [(lax.axis_index("seq"), mp ^ (1 << bit)) for bit in range(mp_bits)]
    return across + [seq_partner(bit) for bit in range(seq_bits)]


def meet(partners):
    barrier = pltpu.get_barrier_semaphore()
    for device in partners:
        pl.semaphore_signal(barrier, inc=1, device_id=device, device_id_type=pl.DeviceIdType.MESH)
    pl.semaphore_wait(barrier, len(partners))


class Small:
    def __init__(self, held, slots, send, recv, partners):
        self.held, self.slots, self.send, self.recv, self.partners = held, slots, send, recv, partners
        self.at = 0

    def copy(self, k):
        return remote(self.held.at[k], self.slots.at[k], self.send.at[k], self.recv.at[k], self.partners[k])

    def advance(self):
        k = self.at
        if k > len(self.partners):
            return
        if k > 0:
            self.copy(k - 1).wait_recv()
            self.held[k] = self.held[k - 1] + self.slots[k - 1]
        if k < len(self.partners):
            self.copy(k).start()
        self.at += 1

    def finish(self, out):
        while self.at <= len(self.partners):
            self.advance()
        for k in range(len(self.partners)):
            self.copy(k).wait_send()
        out[...] = self.held[len(self.partners)]


def small_scratch(shape, steps):
    dma = pltpu.SemaphoreType.DMA
    return [pltpu.VMEM((steps + 1,) + shape, WIDE), pltpu.VMEM((steps,) + shape, WIDE), dma((steps,)), dma((steps,))]


def total_kernel(in_ref, out_ref, held, slots, send, recv, *, seq_bits, mp_bits):
    partners = all_partners(seq_bits, mp_bits)
    meet(partners)
    held[0] = in_ref[...]
    Small(held, slots, send, recv, partners).finish(out_ref)


def total_over_all(values, collective_id):
    seq_bits, mp_bits = bit_count(lax.axis_size("seq")), bit_count(lax.axis_size("mp"))
    flat = values.reshape(-1, HEAD)
    space = pl.BlockSpec(memory_space=pltpu.VMEM)
    out = pl.pallas_call(
        functools.partial(total_kernel, seq_bits=seq_bits, mp_bits=mp_bits),
        in_specs=[space],
        out_specs=space,
        out_shape=jax.ShapeDtypeStruct(flat.shape, WIDE),
        scratch_shapes=small_scratch(flat.shape, seq_bits + mp_bits),
        compiler_params=pltpu.CompilerParams(collective_id=collective_id, has_side_effects=True),
        name="total_over_all",
    )(flat)
    return out.reshape(values.shape)


def seq_total_kernel(small_ref, *refs, count, chunks, seq_bits, mp_bits, share_count):
    shares, refs = refs[:share_count], refs[share_count:]
    mine, other = refs[:count], refs[count : 2 * count]
    small_out, refs = refs[2 * count], refs[2 * count + 1 :]
    shared, refs = refs[:share_count], refs[share_count:]
    outs, scratch = refs[:count], refs[count:]
    (share_local, share_send, share_recv), scratch = scratch[:3], scratch[3:]
    arrived, held = scratch[:count], scratch[count : 2 * count]
    levels = seq_bits - 1
    slots = [scratch[(2 + i) * count : (3 + i) * count] for i in range(levels)]
    core_send, core_recv, back_core_send, back_core_recv, send, recv, back_send, back_recv = scratch[
        (2 + levels) * count : (2 + levels) * count + 8
    ]
    partners = all_partners(seq_bits, mp_bits)
    mp, mp_count = lax.axis_index("mp"), 1 << mp_bits
    along_mp = [(lax.axis_index("seq"), (mp + k) % mp_count) for k in range(1, mp_count)]
    meet(along_mp + partners[mp_bits:])

    def share_rows(i, index):
        rows = shares[i].shape[0]
        return shared[i].at[pl.ds(pl.multiple_of(index * rows, 16), rows)]

    def share_copy(i, k, index):
        return remote(
            shares[i], share_rows(i, index), share_send.at[i, k - 1], share_recv.at[i, k - 1], along_mp[k - 1]
        )

    def share_own(i):
        return pltpu.make_async_copy(shares[i], share_rows(i, mp), share_local.at[i])

    for i in range(share_count):
        share_own(i).start()
        for k in range(1, mp_count):
            share_copy(i, k, mp).start()
    small = Small(*scratch[(2 + levels) * count + 8 :], partners)
    small.held[0] = small_ref[...]
    seq = lax.axis_index("seq")
    core, sibling = seq % 2, seq_partner(0)

    plan = []
    for a in range(count):
        rows = mine[a].shape[0] // chunks[a]
        plan += [(a, c * rows, rows) for c in range(chunks[a])]
    everything = range(len(plan))

    def base(n, level):
        first, rows = plan[n][1:]
        for bit in range(1, level + 1):
            first = first + ((seq >> bit) & 1) * (rows >> bit)
        return first

    def span(n, level, kept):
        side = (seq >> level) & 1
        size = plan[n][2] >> level
        first = base(n, level - 1) + (side if kept else 1 - side) * size
        return pl.ds(pl.multiple_of(first, 16), size)

    def slot(n, level):
        return pl.ds(plan[n][1] >> level, plan[n][2] >> level)

    def whole(n):
        return pl.ds(plan[n][1], plan[n][2])

    def core_copy(n):
        a = plan[n][0]
        return remote(other[a].at[whole(n)], arrived[a].at[whole(n)], core_send.at[n], core_recv.at[n], sibling)

    def copy(n, level):
        a = plan[n][0]
        return remote(
            held[a].at[span(n, level, False)],
            slots[level - 1][a].at[slot(n, level)],
            send.at[n, level - 1],
            recv.at[n, level - 1],
            seq_partner(level),
        )

    def back_copy(n, level, arriving):
        rows = outs[plan[n][0]].at[core, span(n, level, not arriving)]
        return remote(rows, rows, back_send.at[n, level - 1], back_recv.at[n, level - 1], seq_partner(level))

    def back_core_copy(n, arriving):
        rows = outs[plan[n][0]].at[1 - core if arriving else core, whole(n)]
        return remote(rows, rows, back_core_send.at[n], back_core_recv.at[n], sibling)

    def fold(n, level):
        a = plan[n][0]
        copy(n, level).wait_recv()
        kept = span(n, level, True)
        total = held[a][kept, :].astype(WIDE) + slots[level - 1][a][slot(n, level), :].astype(WIDE)
        if level < levels:
            held[a][kept, :] = total.astype(LOW)
            copy(n, level + 1).start()
        else:
            outs[a][core, kept, :] = total.astype(LOW)
            back_copy(n, level, False).start()

    def unfold(n, level):
        back_copy(n, level, True).wait_recv()
        back_copy(n, level - 1, False).start()

    small.advance()
    for n in everything:
        core_copy(n).start()
    for n in everything:
        a = plan[n][0]
        core_copy(n).wait_recv()
        held[a][whole(n), :] = (mine[a][whole(n), :].astype(WIDE) + arrived[a][whole(n), :].astype(WIDE)).astype(LOW)
        copy(n, 1).start()
    small.advance()
    stages = [functools.partial(fold, level=level) for level in range(1, levels + 1)]
    stages += [functools.partial(unfold, level=level) for level in range(levels, 1, -1)]
    for t in range(len(plan) + len(stages) - 1):
        for number in reversed(range(len(stages))):
            if 0 <= t - number < len(plan):
                stages[number](t - number)
        small.advance()
    for n in everything:
        back_copy(n, 1, True).wait_recv()
        back_core_copy(n, False).start()
    for n in everything:
        back_core_copy(n, True).wait_recv()
        core_copy(n).wait_send()
        back_core_copy(n, False).wait_send()
        for level in range(1, levels + 1):
            copy(n, level).wait_send()
            back_copy(n, level, False).wait_send()
    small.finish(small_out)
    for i in range(share_count):
        share_own(i).wait()
        for k in range(1, mp_count):
            share_copy(i, k, (mp + mp_count - k) % mp_count).wait_recv()
            share_copy(i, k, mp).wait_send()


def seq_total(shares, mine, other, small, collective_id):
    seq_bits, mp_bits = bit_count(lax.axis_size("seq")), bit_count(lax.axis_size("mp"))
    levels = seq_bits - 1
    chunks = [min(4, max(1, part.shape[0] // (16 << levels))) for part in mine]
    count, total = len(mine), sum(chunks)
    flat = small.reshape(-1, HEAD)
    space, far = pl.BlockSpec(memory_space=pltpu.VMEM), pl.BlockSpec(memory_space=pl.ANY)
    shapes = [part.shape for part in mine]
    dma = pltpu.SemaphoreType.DMA
    out = pl.pallas_call(
        functools.partial(
            seq_total_kernel,
            count=count,
            chunks=chunks,
            seq_bits=seq_bits,
            mp_bits=mp_bits,
            share_count=len(shares),
        ),
        in_specs=[space] + [far] * len(shares) + [space] * (2 * count),
        out_specs=[space] + [far] * len(shares) + [space] * count,
        out_shape=[jax.ShapeDtypeStruct(flat.shape, WIDE)]
        + [jax.ShapeDtypeStruct((part.shape[0] << mp_bits, part.shape[1]), part.dtype) for part in shares]
        + [jax.ShapeDtypeStruct((2,) + shape, LOW) for shape in shapes],
        scratch_shapes=[dma((len(shares),))]
        + [dma((len(shares), max(1, (1 << mp_bits) - 1)))] * 2
        + [pltpu.VMEM(shape, LOW) for shape in shapes] * 2
        + [pltpu.VMEM((rows >> level, width), LOW) for level in range(1, levels + 1) for rows, width in shapes]
        + [dma((total,))] * 4
        + [dma((total, levels))] * 4
        + small_scratch(flat.shape, seq_bits + mp_bits),
        compiler_params=pltpu.CompilerParams(
            collective_id=collective_id, has_side_effects=True, vmem_limit_bytes=56 * 2**20
        ),
        cost_estimate=pl.CostEstimate(flops=10**11, bytes_accessed=32 * 2**20, transcendentals=0),
        name="seq_total",
    )(flat, *shares, *mine, *other)
    return out[0].reshape(small.shape), out[1 : 1 + len(shares)], out[1 + len(shares) :]


def clip_of(clip_durations, positions):
    clip_ends = jnp.cumsum(clip_durations, dtype=jnp.int32)
    passed = clip_ends[None, :] <= positions[:, None]
    segment = jnp.sum(passed.astype(jnp.int32), 1, dtype=jnp.int32)
    starts = jnp.sum(jnp.where(passed, clip_durations[None, :], 0), 1, dtype=jnp.int32)
    ends = jnp.min(jnp.where(passed, 2**30, clip_ends[None, :]), 1)
    return segment, starts, ends


def norm_forward(rows, gain):
    centred = rows - jnp.mean(rows, -1, keepdims=True)
    inverse = lax.rsqrt(jnp.mean(centred * centred, -1, keepdims=True) + EPSILON)
    normed = centred * inverse
    return (normed * gain).astype(LOW), normed, inverse


def norm_backward(upstream, gain, normed, inverse):
    scaled = upstream * gain
    centred = (
        scaled
        - jnp.mean(scaled, -1, keepdims=True)
        - normed * jnp.mean(scaled * normed, -1, keepdims=True)
    )
    return centred * inverse, jnp.sum(upstream * normed, 0)


def part_of(place, count):
    return (place % 2) * (count // 2) + place // 2


def turn_tables(position):
    half_width = HEAD // 2
    frequency = 10000.0 ** (-jnp.arange(half_width, dtype=WIDE) / half_width)
    angles = position.astype(WIDE)[:, None] * frequency[None, :]
    cosine, sine = jnp.cos(angles), jnp.sin(angles)
    return jnp.concatenate([cosine, cosine], 1), jnp.concatenate([-sine, sine], 1)


def swapped(rows):
    return pltpu.roll(rows, HEAD // 2, 1)


def silu_slope(hidden, sigma):
    return sigma * (1.0 + hidden * (1.0 - sigma))


def project_kernel(in_ref, matrix_ref, cos_ref, sin_ref, q_ref, kv_ref):
    out = dot(in_ref[...], matrix_ref[...])
    cosine, sine = cos_ref[...], sin_ref[...]
    queries, keys = out[:, :HEAD], out[:, HEAD : 2 * HEAD]
    q_ref[...] = (queries * cosine + swapped(queries) * sine).astype(LOW)
    kv_ref[:, :HEAD] = (keys * cosine + swapped(keys) * sine).astype(LOW)
    kv_ref[:, HEAD:] = out[:, 2 * HEAD :].astype(LOW)


def project(entered, matrix, tables, rows=512):
    count = entered.shape[0]

    def row(width):
        return pl.BlockSpec((rows, width), lambda i: (i, 0))

    return pl.pallas_call(
        project_kernel,
        grid=(count // rows,),
        in_specs=[row(D), pl.BlockSpec(matrix.shape, lambda i: (0, 0)), row(HEAD), row(HEAD)],
        out_specs=[row(HEAD), row(2 * HEAD)],
        out_shape=[
            jax.ShapeDtypeStruct((count, HEAD), LOW),
            jax.ShapeDtypeStruct((count, 2 * HEAD), LOW),
        ],
        compiler_params=pltpu.CompilerParams(vmem_limit_bytes=32 * 2**20),
        cost_estimate=pl.CostEstimate(
            flops=6 * count * D * HEAD, bytes_accessed=6 * count * D, transcendentals=0
        ),
        name="project",
    )(entered, matrix, *tables)


def gather_keys(pieces, kv_ref):
    @pl.when(pl.program_id(0) == 0)
    def _():
        at = 0
        for piece in pieces:
            kv_ref[at : at + piece.shape[0], :] = piece[...]
            at += piece.shape[0]


def attend_kernel(lo_ref, hi_ref, q_ref, start_ref, end_ref, *rest, count, depth):
    pieces = rest[:count]
    low_ref, mix_ref, lse_ref, kv_ref = rest[count:]
    gather_keys(pieces, kv_ref)
    i = pl.program_id(0)
    queries = q_ref[...]
    rows = queries.shape[0]
    first, last = start_ref[0], end_ref[0]

    def step(t, carry):
        top, total, mixed = carry
        at = pl.multiple_of(t * depth, depth)
        keys = kv_ref[pl.ds(at, depth), :HEAD]
        values = kv_ref[pl.ds(at, depth), HEAD:]
        index = lax.broadcasted_iota(jnp.int32, (depth, 1), 0) + at
        scores = dot_nt(keys, queries) * SCALE_2
        inside = jnp.logical_and(index >= first, index < last)
        scores = jnp.where(inside, scores, MASKED)
        new_top = jnp.maximum(top, jnp.max(scores, 0, keepdims=True))
        probs = jnp.exp2(scores - new_top)
        fade = jnp.exp2(top - new_top)
        total = fade * total + jnp.sum(probs, 0, keepdims=True)
        mixed = fade * mixed + dot_tn(values, probs.astype(LOW))
        return new_top, total, mixed

    start = (jnp.full((1, rows), MASKED, WIDE), jnp.zeros((1, rows), WIDE), jnp.zeros((HEAD, rows), WIDE))
    top, total, mixed = lax.fori_loop(lo_ref[i], hi_ref[i], step, start)
    mixed = jnp.transpose(mixed / total)
    mix_ref[...] = mixed
    low_ref[...] = mixed.astype(LOW)
    lse_ref[0] = top + jnp.log2(total)


def attend_back_kernel(
    lo_ref, hi_ref, q_ref, do_ref, mix_ref, lse_ref, start_ref, end_ref, cos_ref, sin_ref, *rest, count, depth, parts
):
    pieces = rest[:count]
    dq_ref = rest[count]
    grads = rest[count + 1 : 2 * count + 1]
    kv_ref, dkv_ref = rest[2 * count + 1 :]
    gather_keys(pieces, kv_ref)
    i = pl.program_id(0)

    @pl.when(i == 0)
    def _():
        dkv_ref[...] = jnp.zeros_like(dkv_ref)

    queries, upstream = q_ref[...], do_ref[...]
    lse, first, last = lse_ref[0], start_ref[0], end_ref[0]
    products = jnp.transpose(upstream.astype(WIDE) * mix_ref[...])
    delta = jnp.sum(products, 0, keepdims=True)
    height = depth // parts

    def step(t, grad_query):
        for part in range(parts):
            at = pl.multiple_of(t * depth + part * height, height)
            span = pl.ds(at, height)
            keys = kv_ref[span, :HEAD]
            values = kv_ref[span, HEAD:]
            index = lax.broadcasted_iota(jnp.int32, (height, 1), 0) + at
            inside = jnp.logical_and(index >= first, index < last)
            scores = dot_nt(keys, queries) * SCALE_2
            probs = jnp.where(inside, jnp.exp2(scores - lse), 0.0)
            grad_probs = dot_nt(values, upstream)
            grad_scores = (probs * (grad_probs - delta)).astype(LOW)
            dkv_ref[span, HEAD:] += dot(probs.astype(LOW), upstream)
            dkv_ref[span, :HEAD] += dot(grad_scores, queries)
            grad_query = grad_query + dot_tn(grad_scores, keys)
        return grad_query

    grad_query = lax.fori_loop(lo_ref[i], hi_ref[i], step, jnp.zeros(queries.shape, WIDE)) * SCALE
    dq_ref[...] = (grad_query * cos_ref[...] - swapped(grad_query) * sin_ref[...]).astype(LOW)

    @pl.when(i == pl.num_programs(0) - 1)
    def _():
        at = 0
        for grad in grads:
            span = slice(at, at + grad.shape[0])
            grad[:, :HEAD] = (dkv_ref[span, :HEAD] * SCALE).astype(grad.dtype)
            grad[:, HEAD:] = dkv_ref[span, HEAD:].astype(grad.dtype)
            at += grad.shape[0]


def whole_block(array):
    return pl.BlockSpec(array.shape, lambda i, *_: (0,) * len(array.shape))


def bounds(starts, ends, rows, depth, key_rows):
    count = key_rows // depth
    lo = jnp.clip(starts[::rows] // depth, 0, count)
    hi = jnp.clip((ends[rows - 1 :: rows] + depth - 1) // depth, 0, count)
    return lo.astype(jnp.int32), hi.astype(jnp.int32)


def attention_call(kernel, by_row, by_lane, pieces, spans, out_rows, out_lanes, grads, rows, depth, name, **more):
    count = by_row[0].shape[0]
    key_rows = sum(piece.shape[0] for piece in pieces)
    lo, hi = bounds(*spans, rows, depth, key_rows)
    row = pl.BlockSpec((rows, HEAD), lambda i, *_: (i, 0))
    lane = pl.BlockSpec((1, 1, rows), lambda i, *_: (i, 0, 0))
    lanes = [v.reshape(count // rows, 1, rows) for v in by_lane + list(spans)]
    tail = more.pop("tail", [])
    scratch = [pltpu.VMEM((key_rows, 2 * HEAD), LOW)]
    if grads:
        scratch.append(pltpu.VMEM((key_rows, 2 * HEAD), WIDE))
    return pl.pallas_call(
        functools.partial(kernel, count=len(pieces), depth=depth, **more),
        grid_spec=pltpu.PrefetchScalarGridSpec(
            num_scalar_prefetch=2,
            grid=(count // rows,),
            in_specs=[row] * len(by_row) + [lane] * len(lanes) + [row] * len(tail) + [whole_block(p) for p in pieces],
            out_specs=[row] * len(out_rows) + [lane] * out_lanes + [whole_block(g) for g in grads],
            scratch_shapes=scratch,
        ),
        out_shape=[jax.ShapeDtypeStruct((count, HEAD), kind) for kind in out_rows]
        + [jax.ShapeDtypeStruct((count // rows, 1, rows), WIDE)] * out_lanes
        + grads,
        compiler_params=pltpu.CompilerParams(vmem_limit_bytes=60 * 2**20),
        cost_estimate=pl.CostEstimate(
            flops=(40 if grads else 30) * count * LONGEST * HEAD,
            bytes_accessed=16 * 2**20,
            transcendentals=count * LONGEST,
        ),
        name=name,
    )(lo, hi, *by_row, *lanes, *tail, *pieces)


def attend(queries, pieces, spans, rows=512, depth=1024):
    return attention_call(
        attend_kernel, [queries], [], pieces, spans, [LOW, WIDE], 1, [], rows, depth, "attend"
    )


def attend_back(queries, upstream, mixed, lse, tables, pieces, spans, rows=512, depth=1024):
    middle = len(pieces) // 2
    grads = [
        jax.ShapeDtypeStruct(p.shape, WIDE if j == middle else LOW) for j, p in enumerate(pieces)
    ]
    return attention_call(
        attend_back_kernel,
        [queries, upstream, mixed],
        [lse],
        pieces,
        spans,
        [LOW],
        0,
        grads,
        rows,
        depth,
        "attend_back",
        tail=list(tables),
        parts=2,
    )


def gathered_kernel(dq_ref, own_ref, cos_ref, sin_ref, *rest, places):
    out_ref = rest[-1]
    i = pl.program_id(0)
    grad = own_ref[...]
    for ref, (first, count) in zip(rest, places):
        here = jnp.logical_and(i >= first, i < first + count)
        grad = grad + jnp.where(here, ref[...].astype(WIDE), 0.0)
    keys = grad[:, :HEAD]
    out_ref[:, :HEAD] = dq_ref[...]
    out_ref[:, HEAD : 2 * HEAD] = (keys * cos_ref[...] - swapped(keys) * sin_ref[...]).astype(LOW)
    out_ref[:, 2 * HEAD :] = grad[:, HEAD:].astype(LOW)


def gathered(grad_query, own, tables, arrivals, rows=512):
    count = own.shape[0]
    places = [(first // rows, part.shape[0] // rows) for first, part in arrivals]

    def row(width):
        return pl.BlockSpec((rows, width), lambda i: (i, 0))

    def part(place):
        return pl.BlockSpec((rows, 2 * HEAD), lambda i: (jnp.clip(i - place[0], 0, place[1] - 1), 0))

    return pl.pallas_call(
        functools.partial(gathered_kernel, places=places),
        grid=(count // rows,),
        in_specs=[row(HEAD), row(2 * HEAD), row(HEAD), row(HEAD)] + [part(place) for place in places],
        out_specs=row(3 * HEAD),
        out_shape=jax.ShapeDtypeStruct((count, 3 * HEAD), LOW),
        cost_estimate=pl.CostEstimate(flops=0, bytes_accessed=16 * 2**20, transcendentals=0),
        name="gathered",
    )(grad_query, own, *tables, *[array for _, array in arrivals])


def on_device(
    acoustic_features,
    clip_durations,
    early_layernorm_scale,
    early_widening_matrix,
    early_narrowing_matrix,
    mixer_layernorm_scale,
    triple_matrix,
    mixer_exit_matrix,
    filter_layernorm_scale,
    gating_pair_matrix,
    depthwise_filter,
    running_stats_factor,
    running_stats_offset,
    filter_exit_projection,
    later_layernorm_scale,
    later_widening_matrix,
    later_narrowing_matrix,
    last_layernorm_scale,
    quantizer_projection,
    entry_vectors,
    smoothing_level,
    random_flat_samples,
    expected_entries,
    result_adjoint,
    discrete_adjoint,
):
    seq_count, mp_count = lax.axis_size("seq"), lax.axis_size("mp")
    seq_at, mp_at = lax.axis_index("seq"), lax.axis_index("mp")
    core = seq_at % 2
    frame_rows = acoustic_features.shape[0]
    all_rows = frame_rows * seq_count
    own = frame_rows // mp_count
    own_base = seq_at * frame_rows + mp_at * own

    local_heads = triple_matrix.shape[2] // HEAD
    group_place = seq_at % local_heads
    groups = [
        [(z * local_heads + g) * mp_count + m for g in range(local_heads) for m in range(mp_count)]
        for z in range(seq_count // local_heads)
    ]
    group_size = local_heads * mp_count

    def own_rows(shard):
        size = shard.shape[0] // local_heads
        return cut(shard, part_of(group_place, local_heads) * size, size)

    def own_columns(shard):
        size = shard.shape[1] // local_heads
        return cut(shard, part_of(group_place, local_heads) * size, size, 1).T

    def over_group(part):
        return lax.all_gather(part, BOTH, axis_index_groups=groups, axis=0)

    def grouped(array):
        parts = array.reshape(-1, mp_count, local_heads, array.shape[1] // group_size)
        parts = jnp.stack([parts[:, :, part_of(g, local_heads)] for g in range(local_heads)], 1)
        return parts.reshape(array.shape)

    def ungrouped(array):
        parts = array.reshape(-1, local_heads, mp_count, array.shape[1] // group_size)
        places = sorted(range(local_heads), key=lambda g: part_of(g, local_heads))
        return jnp.stack([parts[:, g] for g in places], 2).reshape(array.shape)

    def group_total(array, over=None):
        return lax.psum_scatter(array, BOTH, scatter_dimension=0, axis_index_groups=over or groups, tiled=True)

    def interleaved(arrays, count):
        parts = [a.astype(LOW).reshape(count, a.shape[0] // count, D) for a in arrays]
        return jnp.concatenate(parts, 1).reshape(-1, D)

    def rel_rows(array, k):
        return cut(array, mp_place(k) * own, own)

    def local_halves(array):
        half = array.shape[1] // 2
        return [cut(array, (core ^ j) * half, half, 1) for j in range(2)]

    head_matrix = cut(triple_matrix, part_of(group_place, local_heads) * HEAD, HEAD, 2)
    head_matrix = jnp.concatenate([head_matrix[i] for i in range(3)], 1)
    small_weights = jnp.concatenate(
        [depthwise_filter, running_stats_factor[None], running_stats_offset[None]], 0
    )
    small_all = grouped(joined(from_mp(small_weights), 1))
    filter_all, factor_all, offset_all = small_all[:KERNEL], small_all[KERNEL], small_all[KERNEL + 1]

    code_parts = jnp.stack([own_columns(quantizer_projection), own_rows(entry_vectors)])
    noise_parts = [rel_rows(random_flat_samples, k) for k in range(mp_count)]
    first_rows, code_parts, noise_parts = paced(acoustic_features, code_parts, noise_parts)
    code_every = over_group(code_parts)
    noise_parts = [noise_parts[0]] + [mp_shift(part, k) for k, part in enumerate(noise_parts) if k]

    first = []
    for k in list(range(1, mp_count)) + [0]:
        rows = rel_rows(first_rows, k).astype(WIDE)
        entered, normed, inverse = norm_forward(rows, early_layernorm_scale)
        hidden = dot(entered, early_widening_matrix)
        activated = (hidden * jax.nn.sigmoid(hidden)).astype(LOW)
        part = dot(activated, early_narrowing_matrix)
        first.append((part, entered, hidden, activated, normed, inverse))
    first = [first[-1]] + first[:-1]
    features = rel_rows(acoustic_features, 0).astype(WIDE)
    after_ffn = features + 0.5 * to_mp([f[0] for f in first])

    quantizer_all, book_all = code_every[:, 0].reshape(-1, D), code_every[:, 1].reshape(-1, D)
    noise = grouped(joined([noise_parts[0]] + noise_parts[:0:-1], 1))
    temper = smoothing_level[0]
    own_features = rel_rows(acoustic_features, 0)
    noisy = dot_nt(own_features, quantizer_all) - jnp.log(-jnp.log(noise))
    tempered = noisy / temper
    assigned = jnp.exp(tempered - jax.nn.logsumexp(tempered, -1)[:, None])
    assigned_low = assigned.astype(LOW)
    quant_low = dot(assigned_low, book_all).astype(LOW)
    own_discrete = rel_rows(discrete_adjoint, 0)
    grad_soft = dot_nt(own_discrete, book_all)
    row_dot = jnp.sum(assigned * grad_soft, -1)
    grad_tempered = assigned * (grad_soft - row_dot[:, None])
    grad_temper = -jnp.sum(grad_tempered * noisy) / (temper * temper)
    grad_entry = (grad_tempered / temper).astype(LOW)
    quant_in = dot(grad_entry, quantizer_all)
    code_grads = dot_tn(assigned_low, own_discrete), dot_tn(grad_entry, own_features)

    group_rows = local_heads * frame_rows
    group_at = seq_at // local_heads
    att_entered, att_normed, att_inverse = norm_forward(after_ffn, mixer_layernorm_scale)
    att_group = over_group(att_entered).reshape(group_rows, D)
    reaches = range(1, -(-(LONGEST - 1) // group_rows) + 1)
    halo = [min(group_rows, -(-(LONGEST - (r - 1) * group_rows) // 1024) * 1024) for r in reaches]
    halo_rows = sum(halo)
    key_base = group_at * group_rows - halo_rows
    group_index = group_at * group_rows + jnp.arange(group_rows, dtype=jnp.int32)
    _, group_start, group_end = clip_of(clip_durations, group_index)
    tables = turn_tables(group_index - group_start)
    spans = (group_start - key_base, group_end - key_base)
    middle_parts = [
        own_rows(mixer_exit_matrix),
        own_columns(gating_pair_matrix[0]),
        own_columns(gating_pair_matrix[1]),
        own_rows(filter_exit_projection),
    ]
    up_part, down_part = own_columns(later_widening_matrix), own_rows(later_narrowing_matrix)
    att_group, tables, code_grads, quant_low, quant_in, grad_temper, sent = paced(
        att_group,
        tables,
        code_grads,
        quant_low,
        quant_in,
        grad_temper,
        (jnp.stack(middle_parts), up_part, down_part, head_matrix),
    )
    middle_every = over_group(sent[0])
    head_matrix = sent[3]
    exit_all, value_all, gate_all, point_all = [middle_every[:, i].reshape(-1, D) for i in range(4)]
    up_all = over_group(sent[1]).reshape(-1, D)
    down_all = over_group(sent[2]).reshape(-1, D)
    query_rot, kv_own = project(att_group, head_matrix, tables)
    lower = [seq_shift(kv_own[group_rows - n :], local_heads * r) for r, n in zip(reaches, halo)]
    upper = [seq_shift(kv_own[:n], -local_heads * r) for r, n in zip(reaches, halo)]
    kv_pieces = lower[::-1] + [kv_own] + upper
    mixed_low, mixed, row_lse = attend(query_rot, kv_pieces, spans)
    mixed_low, head_sent = paced(mixed_low, head_matrix)
    heads_all = over_group(head_sent)

    def exchange(array):
        return lax.all_to_all(array, BOTH, 0, 0, axis_index_groups=groups)

    att_parts = exchange(mixed_low.reshape(group_size, own, HEAD))
    att_low = jnp.transpose(att_parts, (1, 0, 2)).reshape(own, D)
    after_att = after_ffn + dot(att_low, exit_all)

    half_kernel = KERNEL // 2
    pad_index = own_base - half_kernel + jnp.arange(own + 2 * half_kernel, dtype=jnp.int32)
    pad_seg = clip_of(clip_durations, pad_index)[0]
    pad_seg = jnp.where(jnp.logical_and(pad_index >= 0, pad_index < all_rows), pad_seg, -1)
    own_seg = pad_seg[half_kernel : half_kernel + own]
    masks = [(pad_seg[j : j + own] == own_seg)[:, None] for j in range(KERNEL)]

    def padded(block):
        low = flat_shift(block[own - half_kernel :], 1)
        high = flat_shift(block[:half_kernel], -1)
        return jnp.concatenate([low, block, high], 0).astype(WIDE)

    conv_entered, conv_normed, conv_inverse = norm_forward(after_att, filter_layernorm_scale)
    glu_value = dot_nt(conv_entered, value_all)
    glu_gate = jax.nn.sigmoid(dot_nt(conv_entered, gate_all))
    glu_low = (glu_value * glu_gate).astype(LOW)
    glu_padded = padded(glu_low)
    conv_out = jnp.zeros((own, D), WIDE)
    for j in range(KERNEL):
        conv_out = conv_out + filter_all[j][None, :] * jnp.where(masks[j], glu_padded[j : j + own], 0.0)
    sums = total_over_all(jnp.stack([jnp.sum(conv_out, 0), jnp.sum(conv_out * conv_out, 0)]), 1)
    bn_mean = sums[0] / all_rows
    bn_inv = lax.rsqrt(sums[1] / all_rows - bn_mean * bn_mean + EPSILON)
    bn_hat = (conv_out - bn_mean) * bn_inv
    bn_out = bn_hat * factor_all + offset_all
    bn_sigma = jax.nn.sigmoid(bn_out)
    swish_low = (bn_out * bn_sigma).astype(LOW)
    after_conv = after_att + dot(swish_low, point_all)

    late_entered, late_normed, late_inverse = norm_forward(after_conv, later_layernorm_scale)
    late_hidden = dot_nt(late_entered, up_all)
    late_act = (late_hidden * jax.nn.sigmoid(late_hidden)).astype(LOW)
    branch = dot(late_act, down_all)
    after_two = after_conv + 0.5 * branch
    final_low, final_normed, final_inverse = norm_forward(after_two, last_layernorm_scale)

    codes = book_all.shape[0]
    logits = dot_nt(final_low, book_all) * D ** (-0.5)
    code_index = grouped(jnp.arange(codes, dtype=jnp.int32)[None, :])
    is_target = rel_rows(expected_entries, 0)[:, None] == code_index
    pred_lse = jax.nn.logsumexp(logits, -1)
    row_loss = pred_lse - jnp.sum(jnp.where(is_target, logits, 0.0), -1)
    grad_pred = (jnp.exp(logits - pred_lse[:, None]) - is_target.astype(WIDE)).astype(LOW)
    grad_final = rel_rows(result_adjoint, 0).astype(WIDE) + dot(grad_pred, book_all) * D ** (-0.5)
    book_grad = dot_tn(grad_pred, final_low) * D ** (-0.5) + code_grads[0]
    grad_final, loss_shares = paced(grad_final, from_mp(row_loss))
    frame_loss = joined(loss_shares)
    grad_four, grad_ln_final = norm_backward(grad_final, last_layernorm_scale, final_normed, final_inverse)
    late_branch = (0.5 * grad_four).astype(LOW)
    grad_act = dot_nt(late_branch, down_all)
    grad_hidden = (grad_act * silu_slope(late_hidden, jax.nn.sigmoid(late_hidden))).astype(LOW)
    late_in = dot(grad_hidden, up_all)
    down_grad = dot_tn(late_act, late_branch).astype(LOW)
    up_grad = dot_tn(grad_hidden, late_entered).astype(LOW)
    late_norm_grad, grad_ln_ffn2 = norm_backward(late_in, later_layernorm_scale, late_normed, late_inverse)
    grad_three = grad_four + late_norm_grad

    conv_branch = grad_three.astype(LOW)
    grad_swish = dot_nt(conv_branch, point_all)
    grad_bn = grad_swish * silu_slope(bn_out, bn_sigma)
    back_sums = jnp.stack([jnp.sum(grad_bn, 0), jnp.sum(grad_bn * bn_hat, 0)])
    back_sums, up_grad, down_grad, heads_all = paced(back_sums, up_grad, down_grad, heads_all)
    down_total, up_total = group_total(down_grad), group_total(up_grad)
    back_sums = total_over_all(back_sums, 2)
    grad_conv = (
        factor_all * bn_inv * (grad_bn - back_sums[0] / all_rows - bn_hat * back_sums[1] / all_rows)
    ).astype(LOW)
    grad_padded = padded(grad_conv)
    grad_exact = grad_conv.astype(WIDE)
    grad_taps = []
    grad_gated = jnp.zeros_like(grad_exact)
    for j in range(KERNEL):
        grad_taps.append(jnp.sum(grad_exact * jnp.where(masks[j], glu_padded[j : j + own], 0.0), 0))
        back = 2 * half_kernel - j
        grad_gated = grad_gated + filter_all[j][None, :] * jnp.where(
            masks[back], grad_padded[back : back + own], 0.0
        )
    grad_value = (grad_gated * glu_gate).astype(LOW)
    grad_gate = (grad_gated * glu_value * glu_gate * (1.0 - glu_gate)).astype(LOW)
    conv_in = dot(grad_value, value_all) + dot(grad_gate, gate_all)
    conv_norm_grad, grad_ln_conv = norm_backward(conv_in, filter_layernorm_scale, conv_normed, conv_inverse)
    grad_two = grad_three + conv_norm_grad

    att_branch = grad_two.astype(LOW)
    mixer_grads = [
        dot_tn(grad_value, conv_entered),
        dot_tn(grad_gate, conv_entered),
        dot_tn(swish_low, conv_branch),
        dot_tn(att_low, att_branch),
        book_grad,
        code_grads[1],
    ]
    grad_heads = dot_nt(att_branch, exit_all).astype(LOW)
    grad_heads = jnp.transpose(grad_heads.reshape(own, group_size, HEAD), (1, 0, 2))
    grad_mixed = exchange(grad_heads).reshape(group_rows, HEAD)
    mixer_grads = interleaved(mixer_grads, group_size)
    grad_mixed, mixer_grads = paced(grad_mixed, mixer_grads)
    mixer_total = group_total(mixer_grads)
    grad_query, *grad_pieces = attend_back(query_rot, grad_mixed, mixed, row_lse, tables, kv_pieces, spans)
    grad_pieces, up_total, down_total = paced(grad_pieces, up_total, down_total)
    arrivals = []
    reach_count = len(halo)
    for r, n in zip(reaches, halo):
        back = seq_shift(grad_pieces[reach_count - r], -local_heads * r)
        arrivals.append((group_rows - n, back))
        back = seq_shift(grad_pieces[reach_count + r], local_heads * r)
        arrivals.append((0, back))
    grad_proj = gathered(grad_query, grad_pieces[reach_count], tables, arrivals)
    bits, low_bits = bit_count(seq_count), bit_count(local_heads)
    late_total = halved(jnp.stack([up_total, down_total]), low_bits)

    proj_parts = exchange(grad_proj.reshape(group_size, own, 3 * HEAD))
    head_total = halved(dot_tn(att_group, grad_proj).astype(LOW)[None], low_bits)
    proj_parts, late_total = paced(proj_parts, late_total)
    for bit in range(low_bits + 1, bits):
        late_total = halved(late_total, bit)
    att_in = lax.dot_general(
        proj_parts, heads_all, (((0, 2), (0, 2)), ((), ())), preferred_element_type=WIDE
    )
    att_norm_grad, grad_ln_att = norm_backward(att_in, mixer_layernorm_scale, att_normed, att_inverse)
    grad_one = grad_two + att_norm_grad
    grad_one, late_total, mixer_total, head_total = paced(grad_one, late_total, mixer_total, head_total)
    late_every = lax.all_gather(late_total, "seq", axis=0)
    mixed_total = halved(mixer_total.reshape(6, -1, D), low_bits)

    early_branch = from_mp((0.5 * grad_one).astype(LOW))
    early_branch, mixed_total = paced(early_branch, mixed_total)
    for bit in range(low_bits + 1, bits):
        mixed_total, head_total = halved(mixed_total, bit), halved(head_total, bit)
    early_in, early_grads = [], []
    for k, (_, entered, hidden, activated, _, _) in enumerate(first):
        grad_act = dot_nt(early_branch[k], early_narrowing_matrix)
        early_grads.append((grad_act * silu_slope(hidden, jax.nn.sigmoid(hidden))).astype(LOW))
        early_in.append(dot_nt(early_grads[k], early_widening_matrix))

    early_in, head_total, mixed_total = paced(early_in, head_total, mixed_total)
    mixed_every = lax.all_gather(mixed_total, "seq", axis=0)
    head_every = lax.all_gather(head_total[0], "seq", axis=0)
    act_all = jnp.concatenate([f[3] for f in first], 0)
    branch_all = jnp.concatenate(early_branch, 0)
    entered_all = jnp.concatenate([f[1] for f in first], 0)
    hid_all = jnp.concatenate(early_grads, 0)
    up_parts = [dot_tn(entered_all, hid).astype(LOW) for hid in local_halves(hid_all)]
    down_parts = [dot_tn(act, branch_all).astype(LOW) for act in local_halves(act_all)]
    up2_grad, down2_grad = laid(late_every, 0, 1, local_heads, True)[0], laid(late_every, 1, 1, local_heads, False)[0]
    gate_grads = laid(mixed_every, 0, 2, local_heads, True)
    point_grad, exit_grad, book_grad = [laid(mixed_every, i, 1, local_heads, False)[0] for i in (2, 3, 4)]
    code_grad = laid(mixed_every, 5, 1, local_heads, True)[0]
    qkv_grad = laid_heads(head_every, local_heads)
    early_norm_grad, grad_ln_ffn1 = norm_backward(to_mp(early_in), early_layernorm_scale, first[0][4], first[0][5])
    frames_low = (grad_one + early_norm_grad + quant_in).astype(LOW)
    small, (grad_frames, layer_out, quantized), (up1_halves, down1_halves) = seq_total(
        [frames_low, final_low, quant_low],
        [up_parts[0], down_parts[0]],
        [up_parts[1], down_parts[1]],
        jnp.stack(
            [grad_ln_ffn1, grad_ln_att, grad_ln_conv, grad_ln_ffn2, grad_ln_final]
            + grad_taps
            + [jnp.full((D,), grad_temper, WIDE)]
        ),
        3,
    )
    up1_grad, down1_grad = beside(up1_halves, False), beside(down1_halves, True)
    own_channels = filter_exit_projection.shape[0]

    def own_part(array):
        return cut(ungrouped(array), mp_at * own_channels, own_channels, 1)

    bn_grads = own_part(back_sums)

    return (
        layer_out,
        quantized,
        frame_loss,
        grad_frames,
        small[0],
        up1_grad,
        down1_grad,
        small[1],
        qkv_grad,
        exit_grad,
        small[2],
        gate_grads,
        own_part(small[5 : 5 + KERNEL]),
        bn_grads[1],
        bn_grads[0],
        point_grad,
        small[3],
        up2_grad,
        down2_grad,
        small[4],
        code_grad,
        book_grad,
        small[5 + KERNEL, :1],
    )


def solution(mesh):
    in_specs = (
        P("seq", None),
        P(),
        P(),
        P(None, "mp"),
        P("mp", None),
        P(),
        P(None, None, "mp"),
        P("mp", None),
        P(),
        P(None, None, "mp"),
        P(None, "mp"),
        P("mp"),
        P("mp"),
        P("mp", None),
        P(),
        P(None, "mp"),
        P("mp", None),
        P(),
        P(None, "mp"),
        P("mp", None),
        P(),
        P("seq", "mp"),
        P("seq"),
        P("seq", None),
        P("seq", None),
    )
    out_specs = (
        P("seq", None),
        P("seq", None),
        P("seq"),
        P("seq", None),
        P(),
        P(None, "mp"),
        P("mp", None),
        P(),
        P(None, None, "mp"),
        P("mp", None),
        P(),
        P(None, None, "mp"),
        P(None, "mp"),
        P("mp"),
        P("mp"),
        P("mp", None),
        P(),
        P(None, "mp"),
        P("mp", None),
        P(),
        P(None, "mp"),
        P("mp", None),
        P(),
    )
    return jax.shard_map(
        on_device, mesh=mesh, in_specs=in_specs, out_specs=out_specs, check_vma=False
    )
```

time: 1490 us -> 1080 us (0.72)
  Pallas kernels: 64.6 us -> 372 us
  waiting for transfers between devices: 510 us -> 260 us
  blocking collectives: 140 us -> 0 us
  starting transfers between devices: 170 us -> 59.6 us
  other arithmetic: 150 us -> 64.4 us
  local copies, waits for them, and re-layouts: 200 us -> 119 us
  matrix products: 221 us -> 180 us
    pallas_call x2 -> x17, Pallas kernels: 64.6 us -> 372 us  [the longest x1 217 us: seq_total(): pl.pallas_call(functools.partial(seq_total_kernel, count=count, chunks=ch...]
    ppermute x56 -> x6, waiting for transfers between devices: 293 us -> 61.9 us  [seq_xor(): lax.ppermute(shard, 'seq', [(i, i ^ mask) for i in range(lax.axis_size('s...]
    psum x3 -> x0, blocking collectives: 140 us -> none  [the longest x1 53.6 us: on_device(): lax.psum(jnp.concatenate([grad_ln_ffn1, grad_ln_att, grad_ln_conv, grad_l...]
    ppermute x25 -> x6, waiting for transfers between devices: 180 us -> 50.8 us  [mp_shift(): lax.ppermute(shard, 'mp', [(i, (i + by) % count) for i in range(count)])]
    ppermute x56 -> x6, starting transfers between devices: 103 us -> 12.1 us  [seq_xor(): lax.ppermute(shard, 'seq', [(i, i ^ mask) for i in range(lax.axis_size('s...]
    convert_element_type x17 -> x0, local copies, waits for them, and re-layouts: 76.4 us -> none  [the longest x8 32.6 us: summed_grad(): return every.reshape(spread, 2 * columns).astype(WIDE)]
    ppermute x4, waiting for transfers between devices: 0.01 us -> 66.4 us  [seq_shift(): lax.ppermute(shard, 'seq', [(i, i + by) for i in range(count) if 0 <= i +...]
    dot_general x76 -> x40, matrix products: 221 us -> 172 us  [dot(): return lax.dot_general(a, b, (dims, ((), ())), preferred_element_type=WIDE)]
  transfers between devices with their start and end apart: 106 -> 35, of which waited for: 42 -> 19; matrix products, arithmetic and copies ran while one was open for 35% -> 28% of each run, Pallas kernels for 4% -> 34%
where the time goes in v2:
time: 1080 us; the launch traced here: 1070 us
  Pallas kernels  372 us (34%)
  waiting for transfers between devices  260 us (24%)
  matrix products  180 us (17%)
  local copies, waits for them, and re-layouts  119 us (11%)
  other arithmetic  64.4 us (6%)
  starting transfers between devices  59.6 us (6%)
  between operations  17.9 us (2%)
    pallas_call x1, Pallas kernels, seq_total(): pl.pallas_call(functools.partial(seq_total_kernel, count=count, chunks=ch...  217 us
    dot_general x40, matrix products, dot(): return lax.dot_general(a, b, (dims, ((), ())), preferred_element_type=WIDE)  172 us
    ppermute x4, waiting for transfers between devices, seq_shift(): lax.ppermute(shard, 'seq', [(i, i + by) for i in range(count) if 0 <= i +...  66.4 us
    pallas_call x2, Pallas kernels, attention_call(): pl.pallas_call(functools.partial(kernel, count=len(pieces), depth=depth,...  65.5 us
    ppermute x6, waiting for transfers between devices, seq_xor(): lax.ppermute(shard, 'seq', [(i, i ^ mask) for i in range(lax.axis_size('s...  61.9 us
    unnamed x286, local copies, waits for them, and re-layouts  52.9 us
    ppermute x6, waiting for transfers between devices, mp_shift(): lax.ppermute(shard, 'mp', [(i, (i + by) % count) for i in range(count)])  50.8 us
    pallas_call x2, Pallas kernels, total_over_all(): pl.pallas_call(functools.partial(total_kernel, seq_bits=seq_bits, mp_bits...  39.4 us
  transfers between devices with their start and end apart: 35, of which 19 were waited for; matrix products, arithmetic and copies ran while one was open for 28% of the time, Pallas kernels for 34%

profile of v2, /device:TPU:0, one launch (start us, length us, event | category | flops | bytes accessed | tf_op | source)
XLA Modules:
  0.0 1072.8 jit_solution(3214238430788007707)
XLA Ops:
  35.6 30.5 %collective-permute-done = bf16[512,1024]{1,0:T(8,128)(2,1)S(1)} collective-permute-done((bf16[512,1024]{1,0:T(8,128)(2,1)S(1)}, bf16[512,1024]{1,0:T(8,128)(2,1)S(1)}, u32[]{:S(2)}, u32[]{:S(2)}) %collective-permute-start) | collective-permute-done | bytes 1048608 | tf_op jit(solution)/shard_map/ppermute | solution.py:43
  81.4 9.8 fusion.76
  159.0 6.3 project.1
  174.6 28.8 %collective-permute-done.2.rest_0_ = bf16[3072,256]{1,0:T(8,128)(2,1)} collective-permute-done((bf16[3072,256]{1,0:T(8,128)(2,1)}, bf16[3072,256]{1,0:T(8,128)(2,1)}, u32[]{:S(2)}, u32[]{:S(2)}) %collective-permute-start.2) | collective-permute-done | bytes 1572896 | tf_op jit(solution)/shard_map/ppermute | solution.py:52
  208.5 26.9 %attend.1 = (bf16[4096,128]{1,0:T(8,128)(2,1)}, f32[4096,128]{1,0:T(8,128)}, f32[8,1,512]{2,1,0:T(1,128)}) custom-call(s32[8]{0:T(128)} %get-tuple-element.278.lo_ref, s32[8]{0:T(128)} %get-tuple-element.277.hi_ref, bf16[4096,128]{1,0:T(8,128)(2,1)} %copy-done.12, s32[8,1,512]{2,1,0:T(1,128)} %bitcast.337, s32[8,1,512]{2,1,0:T(1,128)} %bitcast.339, ...), custom_call_target="tpu_custom_call" | custom-call | flops 47311749120 | bytes 16777216 | tf_op jit(solution)/shard_map/attend/pallas_call | solution.py:645
  241.6 6.1 fusion.113
  247.8 19.6 %all-to-all-done = bf16[8,512,128]{1,2,0:T(8,128)(2,1)S(1)} async-done(((bf16[8,512,128]{1,2,0:T(8,128)(2,1)}), bf16[8,512,128]{1,2,0:T(8,128)(2,1)S(1)}, u32[]{:S(2)}, u32[]{:S(2)}) %all-to-all-start) | async-done | bytes 1048608 | tf_op jit(solution)/shard_map/all_to_all | solution.py:893
  289.0 25.0 %total_over_all.2 = f32[16,128]{1,0:T(8,128)} custom-call(f32[16,128]{1,0:T(8,128)} %reshape.462.in_ref), custom_call_target="tpu_custom_call" | custom-call | tf_op jit(solution)/shard_map/total_over_all/pallas_call | solution.py:267
  320.9 12.1 %fusion.104 = f32[512,4096]{1,0:T(8,128)} fusion(bf16[4096,1024]{0,1:T(8,128)(2,1)} %all-gather.26.cloned.1.call-done, f32[512,1024]{1,0:T(8,128)} %copy-done.36, f32[1024]{0:T(1024)S(1)} %copy-done.112, f32[512]{0:T(512)S(1)} %add_rsqrt_fusion.1, f32[512]{0:T(512)S(1)} %broadcast_multiply_fusion.11), kind=kOutput, calls=%fused_computation.326 | convolution fusion | flops 4297064448 | bytes 18882560 | tf_op jit(solution)/shard_map/dot_general | solution.py:26
  333.1 11.3 %fusion.126 = (f32[512]{0:T(512)S(1)}, f32[512,1024]{1,0:T(8,128)S(1)}) fusion(f32[512,1024]{1,0:T(8,128)} %copy-done.36, bf16[4096,1024]{1,0:T(8,128)(2,1)} %all-gather.28.cloned.1.call-done, f32[512,4096]{1,0:T(8,128)} %fusion.104), kind=kOutput, calls=%fused_computation.345 | convolution fusion | flops 4307025408 | bytes 20973568 | tf_op jit(solution)/shard_map/dot_general | solution.py:26
  355.0 13.4 %multiply_convert_fusion = bf16[512,4096]{1,0:T(8,128)(2,1)} fusion(f32[512,4096]{1,0:T(8,128)} %fusion.104, bf16[4096,1024]{1,0:T(8,128)(2,1)} %all-gather.28.cloned.1.call-done, f32[512,1024]{1,0:T(8,128)S(1)} %subtract_multiply_fusion), kind=kOutput, calls=%fused_computation | convolution fusion | flops 4314890240 | bytes 23068672 | tf_op jit(solution)/shard_map/dot_general | solution.py:26
  368.4 8.0 multiply_reduce_fusion.1
  382.0 7.3 convolution_convert_fusion.1
  389.3 12.2 %convolution_convert_fusion = bf16[4096,1024]{1,0:T(8,128)(2,1)} fusion(f32[512,1024]{1,0:T(8,128)} %copy-done.38, f32[512,4096]{1,0:T(8,128)} %fusion.104), kind=kOutput, calls=%fused_computation.3 | convolution fusion | flops 4310695936 | bytes 18874368 | tf_op jit(solution)/shard_map/dot_general | solution.py:26
  408.6 14.4 %total_over_all.3 = f32[16,128]{1,0:T(8,128)} custom-call(f32[16,128]{1,0:T(8,128)} %reshape.465.in_ref), custom_call_target="tpu_custom_call" | custom-call | tf_op jit(solution)/shard_map/total_over_all/pallas_call | solution.py:267
  423.6 8.4 fusion.27
  482.0 38.6 %attend_back.1 = (bf16[4096,128]{1,0:T(8,128)(2,1)}, bf16[3072,256]{1,0:T(8,128)(2,1)}, f32[4096,256]{1,0:T(8,128)}, bf16[3072,256]{1,0:T(8,128)(2,1)}) custom-call(s32[8]{0:T(128)} %get-tuple-element.278.lo_ref, s32[8]{0:T(128)} %get-tuple-element.277.hi_ref, bf16[4096,128]{1,0:T(8,128)(2,1)} %copy-done.12, bf16[4096,128]{1,0:T(8,128)(2,1)} %bitcast.63.do_ref, ...), custom_call_target="tpu_custom_call" | custom-call | flops 63082332160 | bytes 16777216 | tf_op jit(solution)/shard_map/attend_back/pallas_call | solution.py:645
  520.7 38.4 %reduce-scatter.6.cloned.1.call-done = bf16[512,1024]{1,0:T(8,128)(2,1)} async-done(((bf16[4096,1024]{1,0:T(8,128)(2,1)}), bf16[512,1024]{1,0:T(8,128)(2,1)}) %reduce-scatter.6.cloned.1.call-update) | async-done | bytes 1048592 | tf_op jit(solution)/shard_map/reduce_scatter | solution.py:794
  566.1 31.2 %collective-permute-done.10.rest_0_ = bf16[3072,256]{1,0:T(8,128)(2,1)S(1)} collective-permute-done((bf16[3072,256]{1,0:T(8,128)(2,1)}, bf16[3072,256]{1,0:T(8,128)(2,1)S(1)}, u32[]{:S(2)}, u32[]{:S(2)}) %collective-permute-start.10) | collective-permute-done | bytes 1572896 | tf_op jit(solution)/shard_map/ppermute | solution.py:52
  598.6 9.0 gathered.1
  614.6 8.9 convolution_convert_fusion.9
  624.6 14.1 %collective-permute-done.12 = bf16[2,256,1024]{2,1,0:T(8,128)(2,1)} collective-permute-done((bf16[2,256,1024]{2,1,0:T(8,128)(2,1)S(1)}, bf16[2,256,1024]{2,1,0:T(8,128)(2,1)}, u32[]{:S(2)}, u32[]{:S(2)}) %collective-permute-start.12) | collective-permute-done | bytes 1048608 | tf_op jit(solution)/shard_map/ppermute | solution.py:47
  640.3 6.5 collective-permute-done.14
  647.9 13.0 %all-to-all-done.2 = bf16[8,512,384]{2,1,0:T(8,128)(2,1)} async-done(((bf16[8,512,384]{2,1,0:T(8,128)(2,1)}), bf16[8,512,384]{2,1,0:T(8,128)(2,1)}, u32[]{:S(2)}, u32[]{:S(2)}) %all-to-all-start.2) | async-done | bytes 3145760 | tf_op jit(solution)/shard_map/all_to_all | solution.py:893
  663.5 7.2 fusion.50
  671.5 15.6 %collective-permute-done.13 = bf16[2,128,1024]{2,1,0:T(8,128)(2,1)S(1)} collective-permute-done((bf16[2,128,1024]{2,1,0:T(8,128)(2,1)S(1)}, bf16[2,128,1024]{2,1,0:T(8,128)(2,1)S(1)}, u32[]{:S(2)}, u32[]{:S(2)}) %collective-permute-start.13) | collective-permute-done | bytes 524320 | tf_op jit(solution)/shard_map/ppermute | solution.py:47
  695.8 16.3 %collective-permute-done.17 = bf16[1,256,384]{2,1,0:T(8,128)(2,1)S(1)} collective-permute-done((bf16[1,256,384]{2,1,0:T(8,128)(2,1)S(1)}, bf16[1,256,384]{2,1,0:T(8,128)(2,1)S(1)}, u32[]{:S(2)}, u32[]{:S(2)}) %collective-permute-start.17) | collective-permute-done | bytes 196640 | tf_op jit(solution)/shard_map/ppermute | solution.py:47
  716.0 6.6 multiply_convert_fusion.3
  737.4 8.9 collective-permute-done.18
  771.4 14.4 %collective-permute-done.19 = bf16[512,1024]{1,0:T(8,128)(2,1)S(1)} collective-permute-done((bf16[512,1024]{1,0:T(8,128)(2,1)S(1)}, bf16[512,1024]{1,0:T(8,128)(2,1)S(1)}, u32[]{:S(2)}, u32[]{:S(2)}) %collective-permute-start.19) | collective-permute-done | bytes 1048608 | tf_op jit(solution)/shard_map/ppermute | solution.py:43
  792.5 217.0 %seq_total.1 = (f32[88,128]{1,0:T(8,128)}, bf16[1024,1024]{1,0:T(8,128)(2,1)}, bf16[1024,1024]{1,0:T(8,128)(2,1)}, bf16[1024,1024]{1,0:T(8,128)(2,1)}, bf16[2,10...) custom-call(f32[88,128]{1,0:T(8,128)} %reshape.477.small_ref, bf16[512,1024]{1,0:T(8,128)(2,1)} %fusion.18.refs_0_, ...), custom_call_target="tpu_custom_call" | custom-call | flops 99999997952 | bytes 33554432 | tf_op jit(solution)/shard_map/seq_total/pallas_call | solution.py:423
  1034.2 6.2 laid.8
  (547 shorter events, 362.5 us)
Async XLA Ops:
  7.2 121.2 %all-gather.22.cloned.1.call-start = ((), (), s32[]{:S(2)}) async-start(), calls=%async_computation.11 | async-start | bytes 4718592 | tf_op jit(solution)/shard_map/all_gather | solution.py:781
  13.5 137.6 %all-gather.20.cloned.1.call-start = ((), (), s32[]{:S(2)}) async-start(), calls=%async_computation.10 | async-start | bytes 9437184 | tf_op jit(solution)/shard_map/all_gather | solution.py:781
  27.8 38.3 %collective-permute-start = (bf16[512,1024]{1,0:T(8,128)(2,1)S(1)}, bf16[512,1024]{1,0:T(8,128)(2,1)S(1)}, u32[]{:S(2)}, u32[]{:S(2)}) collective-permute-start(bf16[512,1024]{1,0:T(8,128)(2,1)S(1)} %convolution_convert_fusion.8), channel_id=1, source_target_pairs={{0,1},{1,0},{2,3},{3,2},{4,5},{5,4},{6,7},{7,6},{8,9},{9,8},{10,11... | collective-permute-start | bytes 3145736 | tf_op jit(solution)/shard_map/ppermute | solution.py:43
  71.9 169.7 %all-gather.24.cloned.1.call-start = ((), (), s32[]{:S(2)}) async-start(), calls=%async_computation.12 | async-start | bytes 9437184 | tf_op jit(solution)/shard_map/all_gather | solution.py:781
  72.2 36.5 %collective-permute-start.1 = (f32[512,512]{1,0:T(8,128)}, f32[512,512]{1,0:T(8,128)}, u32[]{:S(2)}, u32[]{:S(2)}) collective-permute-start(f32[512,512]{1,0:T(8,128)} %get-tuple-element.86), channel_id=1, source_target_pairs={{0,1},{1,0},{2,3},{3,2},{4,5},{5,4},{6,7},{7,6},{8,9},{9,8},{10,11... | collective-permute-start | bytes 3145736 | tf_op jit(solution)/shard_map/ppermute | solution.py:43
  152.4 168.5 %all-gather.26.cloned.1.call-start = ((), (), s32[]{:S(2)}) async-start(), calls=%async_computation.13 | async-start | bytes 9437184 | tf_op jit(solution)/shard_map/all_gather | solution.py:781
  153.0 180.1 %all-gather.28.cloned.1.call-start = ((), (), s32[]{:S(2)}) async-start(), calls=%async_computation.14 | async-start | bytes 9437184 | tf_op jit(solution)/shard_map/all_gather | solution.py:781
  167.4 36.0 %collective-permute-start.2 = (bf16[3072,256]{1,0:T(8,128)(2,1)}, bf16[3072,256]{1,0:T(8,128)(2,1)}, u32[]{:S(2)}, u32[]{:S(2)}) collective-permute-start(bf16[3072,256]{1,0:T(8,128)(2,1)} %get-tuple-element.199), channel_id=1, source_target_pairs={{0,8},{2,10},{4,12},{6,14},{8,16},{10,18},{12,20},{14,22},{16,24},... | collective-permute-start | bytes 4718600 | tf_op jit(solution)/shard_map/ppermute | solution.py:52
  171.3 37.2 %collective-permute-start.3 = (bf16[3072,256]{1,0:T(8,128)(2,1)S(1)}, bf16[3072,256]{1,0:T(8,128)(2,1)}, u32[]{:S(2)}, u32[]{:S(2)}) collective-permute-start(bf16[3072,256]{1,0:T(8,128)(2,1)S(1)} %get-tuple-element.198), channel_id=1, source_target_pairs={{8,0},{10,2},{12,4},{14,6},{16,8},{18,10},{20,12},{22,14},{24,16},... | collective-permute-start | bytes 4718600 | tf_op jit(solution)/shard_map/ppermute | solution.py:52
  172.6 68.9 %collective-permute-start.4 = (f32[7,512]{1,0:T(8,128)S(1)}, f32[7,512]{1,0:T(8,128)S(1)}, u32[]{:S(2)}, u32[]{:S(2)}) collective-permute-start(f32[7,512]{1,0:T(8,128)S(1)} %get-tuple-element.182), channel_id=1, source_target_pairs={{0,1},{1,0},{2,3},{3,2},{4,5},{5,4},{6,7},{7,6},{8,9},{9,8},{10,11... | collective-permute-start | bytes 43016 | tf_op jit(solution)/shard_map/ppermute | solution.py:43
  237.9 29.5 %all-to-all-start = ((bf16[8,512,128]{1,2,0:T(8,128)(2,1)}), bf16[8,512,128]{1,2,0:T(8,128)(2,1)S(1)}, u32[]{:S(2)}, u32[]{:S(2)}) async-start(bf16[8,512,128]{1,2,0:T(8,128)(2,1)} %copy.231), calls=%async_computation | async-start | bytes 2097152 | tf_op jit(solution)/shard_map/all_to_all | solution.py:893
  241.4 160.2 %all-gather.30.cloned.1.call-start = ((), (), s32[]{:S(2)}) async-start(), calls=%async_computation.15 | async-start | bytes 7077888 | tf_op jit(solution)/shard_map/all_gather | solution.py:781
  283.4 237.3 %reduce-scatter.4.cloned.1.call-start = ((), (), s32[]{:S(2)}) async-start(), calls=%async_computation.6 | async-start | bytes 9437184 | tf_op jit(solution)/shard_map/reduce_scatter | solution.py:794
  401.6 157.5 %reduce-scatter.6.cloned.1.call-start = ((), (), s32[]{:S(2)}) async-start(), calls=%async_computation.7 | async-start | bytes 9437184 | tf_op jit(solution)/shard_map/reduce_scatter | solution.py:794
  432.1 8.9 collective-permute-start.9
  433.4 7.6 collective-permute-start.8
  455.5 26.5 %all-to-all-start.1 = ((bf16[8,512,128]{2,1,0:T(8,128)(2,1)}), bf16[8,512,128]{2,1,0:T(8,128)(2,1)}, u32[]{:S(2)}, u32[]{:S(2)}) async-start(bf16[8,512,128]{2,1,0:T(8,128)(2,1)} %bitcast.254), calls=%async_computation.1 | async-start | bytes 2097152 | tf_op jit(solution)/shard_map/all_to_all | solution.py:893
  459.8 228.3 %reduce-scatter.8.cloned.1.call-start = ((), (), s32[]{:S(2)}) async-start(), calls=%async_computation.8 | async-start | bytes 14155776 | tf_op jit(solution)/shard_map/reduce_scatter | solution.py:794
  559.1 38.2 %collective-permute-start.10 = (bf16[3072,256]{1,0:T(8,128)(2,1)}, bf16[3072,256]{1,0:T(8,128)(2,1)S(1)}, u32[]{:S(2)}, u32[]{:S(2)}) collective-permute-start(bf16[3072,256]{1,0:T(8,128)(2,1)} %get-tuple-element.113), channel_id=1, source_target_pairs={{8,0},{10,2},{12,4},{14,6},{16,8},{18,10},{20,12},{22,14},{24,16},... | collective-permute-start | bytes 4718600 | tf_op jit(solution)/shard_map/ppermute | solution.py:52
  560.4 38.2 %collective-permute-start.11 = (bf16[3072,256]{1,0:T(8,128)(2,1)}, bf16[3072,256]{1,0:T(8,128)(2,1)}, u32[]{:S(2)}, u32[]{:S(2)}) collective-permute-start(bf16[3072,256]{1,0:T(8,128)(2,1)} %get-tuple-element.114), channel_id=1, source_target_pairs={{0,8},{2,10},{4,12},{6,14},{8,16},{10,18},{12,20},{14,22},{16,24},... | collective-permute-start | bytes 4718600 | tf_op jit(solution)/shard_map/ppermute | solution.py:52
  607.6 53.4 %all-to-all-start.2 = ((bf16[8,512,384]{2,1,0:T(8,128)(2,1)}), bf16[8,512,384]{2,1,0:T(8,128)(2,1)}, u32[]{:S(2)}, u32[]{:S(2)}) async-start(bf16[8,512,384]{2,1,0:T(8,128)(2,1)} %bitcast.270), calls=%async_computation.4 | async-start | bytes 6291456 | tf_op jit(solution)/shard_map/all_to_all | solution.py:893
  612.3 411.7 %all-gather.18.cloned.1.call-start = ((), (), s32[]{:S(2)}) async-start(), calls=%async_computation.9 | async-start | bytes 3342336 | tf_op jit(solution)/shard_map/all_gather | solution.py:1036
  612.5 26.2 %collective-permute-start.12 = (bf16[2,256,1024]{2,1,0:T(8,128)(2,1)S(1)}, bf16[2,256,1024]{2,1,0:T(8,128)(2,1)}, u32[]{:S(2)}, u32[]{:S(2)}) collective-permute-start(bf16[2,256,1024]{2,1,0:T(8,128)(2,1)S(1)} %fusion.66), channel_id=1, source_target_pairs={{0,8},{2,10},{4,12},{6,14},{8,0},{10,2},{12,4},{14,6},{16,24},{18,... | collective-permute-start | bytes 3145736 | tf_op jit(solution)/shard_map/ppermute | solution.py:47
  624.5 22.3 %collective-permute-start.14 = (bf16[1,512,384]{2,1,0:T(8,128)(2,1)S(1)}, bf16[1,512,384]{2,1,0:T(8,128)(2,1)}, u32[]{:S(2)}, u32[]{:S(2)}) collective-permute-start(bf16[1,512,384]{2,1,0:T(8,128)(2,1)S(1)} %dynamic-slice_bitcast_fusion.1), channel_id=1, source_target_pairs={{0,8},{2,10},{4,12},{6,14},{8,0},{10,2},{12,4},{14,6},{16,24},{18,... | collective-permute-start | bytes 1179656 | tf_op jit(solution)/shard_map/ppermute | solution.py:47
  661.0 26.1 %collective-permute-start.13 = (bf16[2,128,1024]{2,1,0:T(8,128)(2,1)S(1)}, bf16[2,128,1024]{2,1,0:T(8,128)(2,1)S(1)}, u32[]{:S(2)}, u32[]{:S(2)}) collective-permute-start(bf16[2,128,1024]{2,1,0:T(8,128)(2,1)S(1)} %constant_dynamic-slice_fusion.5), channel_id=1, source_target_pairs={{0,16},{2,18},{4,20},{6,22},{8,24},{10,26},{12,28},{14,30},{16,0},... | collective-permute-start | bytes 1572872 | tf_op jit(solution)/shard_map/ppermute | solution.py:47
  690.2 23.2 %collective-permute-start.16 = (bf16[6,64,1024]{2,1,0:T(8,128)(2,1)}, bf16[6,64,1024]{2,1,0:T(8,128)(2,1)}, u32[]{:S(2)}, u32[]{:S(2)}) collective-permute-start(bf16[6,64,1024]{2,1,0:T(8,128)(2,1)} %constant_dynamic-slice_fusion.4), channel_id=1, source_target_pairs={{0,8},{2,10},{4,12},{6,14},{8,0},{10,2},{12,4},{14,6},{16,24},{18,... | collective-permute-start | bytes 2359304 | tf_op jit(solution)/shard_map/ppermute | solution.py:47
  691.0 25.0 %collective-permute-start.15 = (bf16[512,1024]{1,0:T(8,128)(2,1)S(1)}, bf16[512,1024]{1,0:T(8,128)(2,1)}, u32[]{:S(2)}, u32[]{:S(2)}) collective-permute-start(bf16[512,1024]{1,0:T(8,128)(2,1)S(1)} %multiply_convert_fusion.6), channel_id=1, source_target_pairs={{0,1},{1,0},{2,3},{3,2},{4,5},{5,4},{6,7},{7,6},{8,9},{9,8},{10,11... | collective-permute-start | bytes 3145736 | tf_op jit(solution)/shard_map/ppermute | solution.py:43
  692.4 19.7 %collective-permute-start.17 = (bf16[1,256,384]{2,1,0:T(8,128)(2,1)S(1)}, bf16[1,256,384]{2,1,0:T(8,128)(2,1)S(1)}, u32[]{:S(2)}, u32[]{:S(2)}) collective-permute-start(bf16[1,256,384]{2,1,0:T(8,128)(2,1)S(1)} %constant_dynamic-slice_fusion.3), channel_id=1, source_target_pairs={{0,16},{2,18},{4,20},{6,22},{8,24},{10,26},{12,28},{14,30},{16,0},... | collective-permute-start | bytes 589832 | tf_op jit(solution)/shard_map/ppermute | solution.py:47
  726.3 20.0 %collective-permute-start.18 = (bf16[6,32,1024]{2,1,0:T(8,128)(2,1)S(1)}, bf16[6,32,1024]{2,1,0:T(8,128)(2,1)S(1)}, u32[]{:S(2)}, u32[]{:S(2)}) collective-permute-start(bf16[6,32,1024]{2,1,0:T(8,128)(2,1)S(1)} %constant_dynamic-slice_fusion.2), channel_id=1, source_target_pairs={{0,16},{2,18},{4,20},{6,22},{8,24},{10,26},{12,28},{14,30},{16,0},... | collective-permute-start | bytes 1179656 | tf_op jit(solution)/shard_map/ppermute | solution.py:47
  747.2 282.2 %all-gather.32.cloned.1.call-start = ((), (), s32[]{:S(2)}) async-start(), calls=%async_computation.16 | async-start | bytes 6684672 | tf_op jit(solution)/shard_map/all_gather | solution.py:1035
  748.0 299.7 %all-gather.34.cloned.1.call-start = ((), (), s32[]{:S(2)}) async-start(), calls=%async_computation.17 | async-start | bytes 8912896 | tf_op jit(solution)/shard_map/all_gather | solution.py:1021
  762.6 23.2 %collective-permute-start.19 = (bf16[512,1024]{1,0:T(8,128)(2,1)S(1)}, bf16[512,1024]{1,0:T(8,128)(2,1)S(1)}, u32[]{:S(2)}, u32[]{:S(2)}) collective-permute-start(bf16[512,1024]{1,0:T(8,128)(2,1)S(1)} %copy-done.125), channel_id=1, source_target_pairs={{0,1},{1,0},{2,3},{3,2},{4,5},{5,4},{6,7},{7,6},{8,9},{9,8},{10,11... | collective-permute-start | bytes 3145736 | tf_op jit(solution)/shard_map/ppermute | solution.py:43
  (141 other events, 1341.2 us)
Sparse Core Ops, SparseCore 0:
  13.6 51.0 all-gather.21
  72.1 66.3 all-gather.19
  152.5 54.2 all-gather.23
  208.5 67.1 all-gather.25
  277.5 52.6 all-gather.27
  331.9 45.5 all-gather.29
  401.7 81.5 reduce-scatter.3
  487.7 71.3 reduce-scatter.5
  562.6 120.3 reduce-scatter.7
  747.3 44.6 all-gather.17
  794.9 82.6 all-gather.31
  880.2 113.6 all-gather.33

commit v3 on v2

--- a/solution.py
+++ b/solution.py
@@ -82,13 +82,6 @@
     return whole
 
 
-def halved(part, bit):
-    half = part.shape[1] // 2
-    side = (lax.axis_index("seq") >> bit) & 1
-    sent = seq_xor(cut(part, (1 - side) * half, half, 1), 1 << bit)
-    return cut(part, side * half, half, 1) + sent
-
-
 def paced(*values):
     return lax.optimization_barrier(values)
 
@@ -97,17 +90,10 @@
     return int(math.log2(number))
 
 
-def reversed_bits(number, bits):
-    out = 0
-    for b in range(bits):
-        out = out + (((number >> b) & 1) << (bits - 1 - b))
-    return out
-
-
 def laid_kernel(in_ref, out_ref, *, places, turned):
-    _, _, rows, width = in_ref.shape
+    rows = in_ref.shape[1]
     for s, place in enumerate(places):
-        block = in_ref[s, 0].astype(WIDE)
+        block = in_ref[s].astype(WIDE)
         span = slice(place * rows, (place + 1) * rows)
         if turned:
             out_ref[0, :, span] = block.T
@@ -115,24 +101,22 @@
             out_ref[0, span, :] = block
 
 
-def laid(every, first, amount, local_heads, turned, width=256):
-    count, _, rows, columns = every.shape
+def laid(every, first, rows, amount, local_heads, turned):
+    count, _, columns = every.shape
     line = count // local_heads
-    bits = bit_count(line)
-    places = [
-        part_of(s % local_heads, local_heads) * line + reversed_bits(s // local_heads, bits) for s in range(count)
-    ]
-    if count * rows % 128:
+    places = [part_of(s % local_heads, local_heads) * line + s // local_heads for s in range(count)]
+    if rows % 16 or count * rows % 128:
         order = sorted(range(count), key=lambda s: places[s])
-        whole = jnp.stack([every[s, first : first + amount] for s in order], 1).astype(WIDE)
-        whole = whole.reshape(amount, count * rows, columns)
+        whole = every[:, first : first + amount * rows].reshape(count, amount, rows, columns)
+        whole = jnp.stack([whole[s] for s in order], 1).astype(WIDE).reshape(amount, count * rows, columns)
         return jnp.transpose(whole, (0, 2, 1)) if turned else whole
     shape = (columns, count * rows) if turned else (count * rows, columns)
+    width = min(columns, 2**19 // (count * rows))
     block = (1, width, count * rows) if turned else (1, count * rows, width)
     return pl.pallas_call(
         functools.partial(laid_kernel, places=places, turned=turned),
         grid=(amount, columns // width),
-        in_specs=[pl.BlockSpec((count, 1, rows, width), lambda i, j: (0, first + i, 0, j))],
+        in_specs=[pl.BlockSpec((count, rows, width), lambda i, j: (0, first // rows + i, j))],
         out_specs=pl.BlockSpec(block, lambda i, j: (i, j, 0) if turned else (i, 0, j)),
         out_shape=jax.ShapeDtypeStruct((amount,) + shape, WIDE),
         compiler_params=pltpu.CompilerParams(vmem_limit_bytes=32 * 2**20),
@@ -143,29 +127,49 @@
     )(every)
 
 
-def laid_heads_kernel(in_ref, out_ref, *, local_heads, bits):
-    rows = in_ref.shape[1]
-    for s in range(in_ref.shape[0]):
-        block = reversed_bits(s // local_heads, bits)
-        head = part_of(s % local_heads, local_heads)
-        out_ref[0, block * rows : (block + 1) * rows, head * HEAD : (head + 1) * HEAD] = in_ref[s].astype(WIDE)
-
-
-def laid_heads(every, local_heads):
-    count, rows, _ = every.shape
-    shape = (D, local_heads * HEAD)
-    return pl.pallas_call(
-        functools.partial(
-            laid_heads_kernel, local_heads=local_heads, bits=bit_count(count) - bit_count(local_heads)
+def products_kernel(*refs, plan, line):
+    out_ref = refs[-1]
+    at = ref = 0
+    for terms in plan:
+        sum_of = None
+        for scale in terms:
+            term = dot_tn(refs[ref][...], refs[ref + 1][...])
+            term = term if scale is None else term * scale
+            sum_of = term if sum_of is None else sum_of + term
+            ref += 2
+        rows = sum_of.shape[0] // line
+        for z in range(line):
+            to = z * (out_ref.shape[1] // line) + at
+            out_ref[0, to : to + rows, :] = sum_of[z * rows : (z + 1) * rows].astype(LOW)
+        at += rows
+
+
+def products(matrices, count, line):
+    frames = matrices[0][0][0].shape[0]
+    plan = [[term[2] for term in terms] for terms in matrices]
+    operands, specs, height = [], [], 0
+    for terms in matrices:
+        width = terms[0][0].shape[1] // count
+        height += width
+        for left, right, _ in terms:
+            operands += [left, right]
+            specs += [
+                pl.BlockSpec((frames, width), lambda i: (0, i)),
+                pl.BlockSpec(right.shape, lambda i: (0, 0)),
+            ]
+    out = pl.pallas_call(
+        functools.partial(products_kernel, plan=plan, line=line),
+        grid=(count,),
+        in_specs=specs,
+        out_specs=pl.BlockSpec((1, height, D), lambda i: (i, 0, 0)),
+        out_shape=jax.ShapeDtypeStruct((count, height, D), LOW),
+        compiler_params=pltpu.CompilerParams(vmem_limit_bytes=50 * 2**20),
+        cost_estimate=pl.CostEstimate(
+            flops=2 * frames * height * count * D, bytes_accessed=2 * height * count * D, transcendentals=0
         ),
-        grid=(3,),
-        in_specs=[pl.BlockSpec((count, rows, HEAD), lambda i: (0, 0, i))],
-        out_specs=pl.BlockSpec((1,) + shape, lambda i: (i, 0, 0)),
-        out_shape=jax.ShapeDtypeStruct((3,) + shape, WIDE),
-        compiler_params=pltpu.CompilerParams(vmem_limit_bytes=32 * 2**20),
-        cost_estimate=pl.CostEstimate(flops=0, bytes_accessed=18 * D * local_heads * HEAD, transcendentals=0),
-        name="laid_heads",
-    )(every)
+        name="products",
+    )(*operands)
+    return out.reshape(count * height, D)
 
 
 def beside_kernel(in_ref, out_ref):
@@ -306,10 +310,6 @@
     def share_own(i):
         return pltpu.make_async_copy(shares[i], share_rows(i, mp), share_local.at[i])
 
-    for i in range(share_count):
-        share_own(i).start()
-        for k in range(1, mp_count):
-            share_copy(i, k, mp).start()
     small = Small(*scratch[(2 + levels) * count + 8 :], partners)
     small.held[0] = small_ref[...]
     seq = lax.axis_index("seq")
@@ -380,15 +380,24 @@
     small.advance()
     for n in everything:
         core_copy(n).start()
-    for n in everything:
+    def enter(n):
         a = plan[n][0]
         core_copy(n).wait_recv()
         held[a][whole(n), :] = (mine[a][whole(n), :].astype(WIDE) + arrived[a][whole(n), :].astype(WIDE)).astype(LOW)
         copy(n, 1).start()
+
+    for n in range(2):
+        enter(n)
     small.advance()
+    for i in range(share_count):
+        share_own(i).start()
+        for k in range(1, mp_count):
+            share_copy(i, k, mp).start()
     stages = [functools.partial(fold, level=level) for level in range(1, levels + 1)]
     stages += [functools.partial(unfold, level=level) for level in range(levels, 1, -1)]
     for t in range(len(plan) + len(stages) - 1):
+        if t + 2 < len(plan):
+            enter(t + 2)
         for number in reversed(range(len(stages))):
             if 0 <= t - number < len(plan):
                 stages[number](t - number)
@@ -768,6 +777,10 @@
         for z in range(seq_count // local_heads)
     ]
     group_size = local_heads * mp_count
+    line = seq_count // local_heads
+    lines = [
+        [(z * local_heads + g) * mp_count + m for z in range(line)] for g in range(local_heads) for m in range(mp_count)
+    ]
 
     def own_rows(shard):
         size = shard.shape[0] // local_heads
@@ -793,10 +806,6 @@
     def group_total(array, over=None):
         return lax.psum_scatter(array, BOTH, scatter_dimension=0, axis_index_groups=over or groups, tiled=True)
 
-    def interleaved(arrays, count):
-        parts = [a.astype(LOW).reshape(count, a.shape[0] // count, D) for a in arrays]
-        return jnp.concatenate(parts, 1).reshape(-1, D)
-
     def rel_rows(array, k):
         return cut(array, mp_place(k) * own, own)
 
@@ -804,8 +813,6 @@
         half = array.shape[1] // 2
         return [cut(array, (core ^ j) * half, half, 1) for j in range(2)]
 
-    head_matrix = cut(triple_matrix, part_of(group_place, local_heads) * HEAD, HEAD, 2)
-    head_matrix = jnp.concatenate([head_matrix[i] for i in range(3)], 1)
     small_weights = jnp.concatenate(
         [depthwise_filter, running_stats_factor[None], running_stats_offset[None]], 0
     )
@@ -813,10 +820,11 @@
     filter_all, factor_all, offset_all = small_all[:KERNEL], small_all[KERNEL], small_all[KERNEL + 1]
 
     code_parts = jnp.stack([own_columns(quantizer_projection), own_rows(entry_vectors)])
-    noise_parts = [rel_rows(random_flat_samples, k) for k in range(mp_count)]
+    noise_parts = [-jnp.log(-jnp.log(rel_rows(random_flat_samples, k))) for k in range(mp_count)]
+    noise_parts = noise_parts[:1] + [part.astype(LOW) for part in noise_parts[1:]]
     first_rows, code_parts, noise_parts = paced(acoustic_features, code_parts, noise_parts)
     code_every = over_group(code_parts)
-    noise_parts = [noise_parts[0]] + [mp_shift(part, k) for k, part in enumerate(noise_parts) if k]
+    noise_parts = noise_parts[:1] + [mp_shift(part, k).astype(WIDE) for k, part in enumerate(noise_parts) if k]
 
     first = []
     for k in list(range(1, mp_count)) + [0]:
@@ -824,17 +832,34 @@
         entered, normed, inverse = norm_forward(rows, early_layernorm_scale)
         hidden = dot(entered, early_widening_matrix)
         activated = (hidden * jax.nn.sigmoid(hidden)).astype(LOW)
-        part = dot(activated, early_narrowing_matrix)
+        part = dot(activated, early_narrowing_matrix).astype(LOW)
         first.append((part, entered, hidden, activated, normed, inverse))
     first = [first[-1]] + first[:-1]
     features = rel_rows(acoustic_features, 0).astype(WIDE)
+    group_rows = local_heads * frame_rows
+    group_at = seq_at // local_heads
+    group_index = group_at * group_rows + jnp.arange(group_rows, dtype=jnp.int32)
+    _, group_start, group_end = clip_of(clip_durations, group_index)
+    tables = turn_tables(group_index - group_start)
+    head_matrix = cut(triple_matrix, part_of(group_place, local_heads) * HEAD, HEAD, 2)
+    head_matrix = jnp.concatenate([head_matrix[i] for i in range(3)], 1)
+    middle_parts = [
+        own_rows(mixer_exit_matrix),
+        own_columns(gating_pair_matrix[0]),
+        own_columns(gating_pair_matrix[1]),
+        own_rows(filter_exit_projection),
+    ]
+    up_part, down_part = own_columns(later_widening_matrix), own_rows(later_narrowing_matrix)
     after_ffn = features + 0.5 * to_mp([f[0] for f in first])
+    after_ffn, tables, sent = paced(
+        after_ffn, tables, (jnp.stack(middle_parts), up_part, down_part, head_matrix)
+    )
 
     quantizer_all, book_all = code_every[:, 0].reshape(-1, D), code_every[:, 1].reshape(-1, D)
     noise = grouped(joined([noise_parts[0]] + noise_parts[:0:-1], 1))
     temper = smoothing_level[0]
     own_features = rel_rows(acoustic_features, 0)
-    noisy = dot_nt(own_features, quantizer_all) - jnp.log(-jnp.log(noise))
+    noisy = dot_nt(own_features, quantizer_all) + noise
     tempered = noisy / temper
     assigned = jnp.exp(tempered - jax.nn.logsumexp(tempered, -1)[:, None])
     assigned_low = assigned.astype(LOW)
@@ -846,36 +871,15 @@
     grad_temper = -jnp.sum(grad_tempered * noisy) / (temper * temper)
     grad_entry = (grad_tempered / temper).astype(LOW)
     quant_in = dot(grad_entry, quantizer_all)
-    code_grads = dot_tn(assigned_low, own_discrete), dot_tn(grad_entry, own_features)
-
-    group_rows = local_heads * frame_rows
-    group_at = seq_at // local_heads
+
     att_entered, att_normed, att_inverse = norm_forward(after_ffn, mixer_layernorm_scale)
     att_group = over_group(att_entered).reshape(group_rows, D)
     reaches = range(1, -(-(LONGEST - 1) // group_rows) + 1)
     halo = [min(group_rows, -(-(LONGEST - (r - 1) * group_rows) // 1024) * 1024) for r in reaches]
     halo_rows = sum(halo)
     key_base = group_at * group_rows - halo_rows
-    group_index = group_at * group_rows + jnp.arange(group_rows, dtype=jnp.int32)
-    _, group_start, group_end = clip_of(clip_durations, group_index)
-    tables = turn_tables(group_index - group_start)
     spans = (group_start - key_base, group_end - key_base)
-    middle_parts = [
-        own_rows(mixer_exit_matrix),
-        own_columns(gating_pair_matrix[0]),
-        own_columns(gating_pair_matrix[1]),
-        own_rows(filter_exit_projection),
-    ]
-    up_part, down_part = own_columns(later_widening_matrix), own_rows(later_narrowing_matrix)
-    att_group, tables, code_grads, quant_low, quant_in, grad_temper, sent = paced(
-        att_group,
-        tables,
-        code_grads,
-        quant_low,
-        quant_in,
-        grad_temper,
-        (jnp.stack(middle_parts), up_part, down_part, head_matrix),
-    )
+    att_group, assigned_low, quant_low, sent = paced(att_group, assigned_low, quant_low, sent)
     middle_every = over_group(sent[0])
     head_matrix = sent[3]
     exit_all, value_all, gate_all, point_all = [middle_every[:, i].reshape(-1, D) for i in range(4)]
@@ -886,7 +890,9 @@
     upper = [seq_shift(kv_own[:n], -local_heads * r) for r, n in zip(reaches, halo)]
     kv_pieces = lower[::-1] + [kv_own] + upper
     mixed_low, mixed, row_lse = attend(query_rot, kv_pieces, spans)
-    mixed_low, head_sent = paced(mixed_low, head_matrix)
+    mixed_low, head_sent, grad_entry, quant_in, grad_temper = paced(
+        mixed_low, head_matrix, grad_entry, quant_in, grad_temper
+    )
     heads_all = over_group(head_sent)
 
     def exchange(array):
@@ -940,7 +946,6 @@
     row_loss = pred_lse - jnp.sum(jnp.where(is_target, logits, 0.0), -1)
     grad_pred = (jnp.exp(logits - pred_lse[:, None]) - is_target.astype(WIDE)).astype(LOW)
     grad_final = rel_rows(result_adjoint, 0).astype(WIDE) + dot(grad_pred, book_all) * D ** (-0.5)
-    book_grad = dot_tn(grad_pred, final_low) * D ** (-0.5) + code_grads[0]
     grad_final, loss_shares = paced(grad_final, from_mp(row_loss))
     frame_loss = joined(loss_shares)
     grad_four, grad_ln_final = norm_backward(grad_final, last_layernorm_scale, final_normed, final_inverse)
@@ -948,8 +953,7 @@
     grad_act = dot_nt(late_branch, down_all)
     grad_hidden = (grad_act * silu_slope(late_hidden, jax.nn.sigmoid(late_hidden))).astype(LOW)
     late_in = dot(grad_hidden, up_all)
-    down_grad = dot_tn(late_act, late_branch).astype(LOW)
-    up_grad = dot_tn(grad_hidden, late_entered).astype(LOW)
+    late_grads = products([[(grad_hidden, late_entered, None)], [(late_act, late_branch, None)]], group_size, line)
     late_norm_grad, grad_ln_ffn2 = norm_backward(late_in, later_layernorm_scale, late_normed, late_inverse)
     grad_three = grad_four + late_norm_grad
 
@@ -957,8 +961,8 @@
     grad_swish = dot_nt(conv_branch, point_all)
     grad_bn = grad_swish * silu_slope(bn_out, bn_sigma)
     back_sums = jnp.stack([jnp.sum(grad_bn, 0), jnp.sum(grad_bn * bn_hat, 0)])
-    back_sums, up_grad, down_grad, heads_all = paced(back_sums, up_grad, down_grad, heads_all)
-    down_total, up_total = group_total(down_grad), group_total(up_grad)
+    back_sums, late_grads, heads_all = paced(back_sums, late_grads, heads_all)
+    late_part = group_total(late_grads)
     back_sums = total_over_all(back_sums, 2)
     grad_conv = (
         factor_all * bn_inv * (grad_bn - back_sums[0] / all_rows - bn_hat * back_sums[1] / all_rows)
@@ -980,22 +984,25 @@
     grad_two = grad_three + conv_norm_grad
 
     att_branch = grad_two.astype(LOW)
-    mixer_grads = [
-        dot_tn(grad_value, conv_entered),
-        dot_tn(grad_gate, conv_entered),
-        dot_tn(swish_low, conv_branch),
-        dot_tn(att_low, att_branch),
-        book_grad,
-        code_grads[1],
-    ]
+    mixer_grads = products(
+        [
+            [(grad_value, conv_entered, None)],
+            [(grad_gate, conv_entered, None)],
+            [(swish_low, conv_branch, None)],
+            [(att_low, att_branch, None)],
+            [(grad_pred, final_low, D ** (-0.5)), (assigned_low, own_discrete, None)],
+            [(grad_entry, own_features, None)],
+        ],
+        group_size,
+        line,
+    )
     grad_heads = dot_nt(att_branch, exit_all).astype(LOW)
     grad_heads = jnp.transpose(grad_heads.reshape(own, group_size, HEAD), (1, 0, 2))
     grad_mixed = exchange(grad_heads).reshape(group_rows, HEAD)
-    mixer_grads = interleaved(mixer_grads, group_size)
     grad_mixed, mixer_grads = paced(grad_mixed, mixer_grads)
     mixer_total = group_total(mixer_grads)
     grad_query, *grad_pieces = attend_back(query_rot, grad_mixed, mixed, row_lse, tables, kv_pieces, spans)
-    grad_pieces, up_total, down_total = paced(grad_pieces, up_total, down_total)
+    grad_pieces, late_part = paced(grad_pieces, late_part)
     arrivals = []
     reach_count = len(halo)
     for r, n in zip(reaches, halo):
@@ -1004,49 +1011,37 @@
         back = seq_shift(grad_pieces[reach_count + r], local_heads * r)
         arrivals.append((0, back))
     grad_proj = gathered(grad_query, grad_pieces[reach_count], tables, arrivals)
-    bits, low_bits = bit_count(seq_count), bit_count(local_heads)
-    late_total = halved(jnp.stack([up_total, down_total]), low_bits)
 
     proj_parts = exchange(grad_proj.reshape(group_size, own, 3 * HEAD))
-    head_total = halved(dot_tn(att_group, grad_proj).astype(LOW)[None], low_bits)
-    proj_parts, late_total = paced(proj_parts, late_total)
-    for bit in range(low_bits + 1, bits):
-        late_total = halved(late_total, bit)
+    head_grads = dot_tn(grad_proj, att_group).astype(LOW)
+    proj_parts, head_grads = paced(proj_parts, head_grads)
+    head_grads = jnp.transpose(head_grads.reshape(3, line, HEAD // line, D), (1, 0, 2, 3)).reshape(line, -1, D)
     att_in = lax.dot_general(
         proj_parts, heads_all, (((0, 2), (0, 2)), ((), ())), preferred_element_type=WIDE
     )
     att_norm_grad, grad_ln_att = norm_backward(att_in, mixer_layernorm_scale, att_normed, att_inverse)
     grad_one = grad_two + att_norm_grad
-    grad_one, late_total, mixer_total, head_total = paced(grad_one, late_total, mixer_total, head_total)
-    late_every = lax.all_gather(late_total, "seq", axis=0)
-    mixed_total = halved(mixer_total.reshape(6, -1, D), low_bits)
+    grad_one, late_part, mixer_total, head_grads = paced(grad_one, late_part, mixer_total, head_grads)
+    every_total = [part.reshape(line, -1, D) for part in (late_part, mixer_total, head_grads)]
+    every_total = group_total(jnp.concatenate(every_total, 1).reshape(-1, D), lines)
 
     early_branch = from_mp((0.5 * grad_one).astype(LOW))
-    early_branch, mixed_total = paced(early_branch, mixed_total)
-    for bit in range(low_bits + 1, bits):
-        mixed_total, head_total = halved(mixed_total, bit), halved(head_total, bit)
     early_in, early_grads = [], []
     for k, (_, entered, hidden, activated, _, _) in enumerate(first):
         grad_act = dot_nt(early_branch[k], early_narrowing_matrix)
         early_grads.append((grad_act * silu_slope(hidden, jax.nn.sigmoid(hidden))).astype(LOW))
         early_in.append(dot_nt(early_grads[k], early_widening_matrix))
 
-    early_in, head_total, mixed_total = paced(early_in, head_total, mixed_total)
-    mixed_every = lax.all_gather(mixed_total, "seq", axis=0)
-    head_every = lax.all_gather(head_total[0], "seq", axis=0)
     act_all = jnp.concatenate([f[3] for f in first], 0)
     branch_all = jnp.concatenate(early_branch, 0)
     entered_all = jnp.concatenate([f[1] for f in first], 0)
     hid_all = jnp.concatenate(early_grads, 0)
     up_parts = [dot_tn(entered_all, hid).astype(LOW) for hid in local_halves(hid_all)]
     down_parts = [dot_tn(act, branch_all).astype(LOW) for act in local_halves(act_all)]
-    up2_grad, down2_grad = laid(late_every, 0, 1, local_heads, True)[0], laid(late_every, 1, 1, local_heads, False)[0]
-    gate_grads = laid(mixed_every, 0, 2, local_heads, True)
-    point_grad, exit_grad, book_grad = [laid(mixed_every, i, 1, local_heads, False)[0] for i in (2, 3, 4)]
-    code_grad = laid(mixed_every, 5, 1, local_heads, True)[0]
-    qkv_grad = laid_heads(head_every, local_heads)
     early_norm_grad, grad_ln_ffn1 = norm_backward(to_mp(early_in), early_layernorm_scale, first[0][4], first[0][5])
     frames_low = (grad_one + early_norm_grad + quant_in).astype(LOW)
+    frames_low, every_total = paced(frames_low, every_total)
+    every = lax.all_gather(every_total, "seq", axis=0)
     small, (grad_frames, layer_out, quantized), (up1_halves, down1_halves) = seq_total(
         [frames_low, final_low, quant_low],
         [up_parts[0], down_parts[0]],
@@ -1058,6 +1053,17 @@
         ),
         3,
     )
+    late_rows = late_part.shape[0] // line // 2
+    mixer_rows = mixer_total.shape[0] // line // 6
+    up2_grad = laid(every, 0, late_rows, 1, local_heads, True)[0]
+    down2_grad = laid(every, late_rows, late_rows, 1, local_heads, False)[0]
+
+    def mixer_laid(at, amount, turned):
+        return laid(every, 2 * late_rows + at * mixer_rows, mixer_rows, amount, local_heads, turned)
+
+    gate_grads = mixer_laid(0, 2, True)
+    point_grad, exit_grad, book_grad = [mixer_laid(at, 1, False)[0] for at in (2, 3, 4)]
+    code_grad, qkv_grad = mixer_laid(5, 1, True)[0], mixer_laid(6, 3, True)
     up1_grad, down1_grad = beside(up1_halves, False), beside(down1_halves, True)
     own_channels = filter_exit_projection.shape[0]
 

time: 1080 us -> 996 us (0.922)
  waiting for transfers between devices: 260 us -> 215 us
  matrix products: 180 us -> 142 us
  local copies, waits for them, and re-layouts: 119 us -> 88.4 us
  Pallas kernels: 372 us -> 395 us
    ppermute x6 -> x0, waiting for transfers between devices: 61.9 us -> none  [seq_xor(): lax.ppermute(shard, 'seq', [(i, i ^ mask) for i in range(lax.axis_size('s...]
    pallas_call x1, Pallas kernels: 217 us -> 171 us  [seq_total(): pl.pallas_call(functools.partial(seq_total_kernel, count=count, chunks=ch...]
    pallas_call x2, Pallas kernels: 65.5 us -> 109 us  [attention_call(): pl.pallas_call(functools.partial(kernel, count=len(pieces), depth=depth,...]
    dot_general x40 -> x31, matrix products: 172 us -> 135 us  [dot(): return lax.dot_general(a, b, (dims, ((), ())), preferred_element_type=WIDE)]
    pallas_call x1 -> x2, Pallas kernels: 3.51 us -> 30.6 us  [products(): pl.pallas_call(functools.partial(products_kernel, plan=plan, line=line),...]
    all_to_all x3, waiting for transfers between devices: 37.8 us -> 60.2 us  [exchange(): return lax.all_to_all(array, BOTH, 0, 0, axis_index_groups=groups)]
    reduce_scatter x3, waiting for transfers between devices: 38.4 us -> 16.3 us  [group_total(): lax.psum_scatter(array, BOTH, scatter_dimension=0, axis_index_groups=over...]
    unnamed x286 -> x240, local copies, waits for them, and re-layouts: 52.9 us -> 35.5 us
  transfers between devices with their start and end apart: 35 -> 27, of which waited for: 19 -> 15; matrix products, arithmetic and copies ran while one was open for 28% -> 26% of each run, Pallas kernels for 34% -> 37%
where the time goes in v3:
time: 996 us; the launch traced here: 984 us
  Pallas kernels  395 us (40%)
  waiting for transfers between devices  215 us (22%)
  matrix products  142 us (14%)
  local copies, waits for them, and re-layouts  88.4 us (9%)
  other arithmetic  73 us (7%)
  starting transfers between devices  53.2 us (5%)
  between operations  17.5 us (2%)
    pallas_call x1, Pallas kernels, seq_total(): pl.pallas_call(functools.partial(seq_total_kernel, count=count, chunks=ch...  171 us
    dot_general x31, matrix products, dot(): return lax.dot_general(a, b, (dims, ((), ())), preferred_element_type=WIDE)  135 us
    pallas_call x2, Pallas kernels, attention_call(): pl.pallas_call(functools.partial(kernel, count=len(pieces), depth=depth,...  109 us
    ppermute x4, waiting for transfers between devices, seq_shift(): lax.ppermute(shard, 'seq', [(i, i + by) for i in range(count) if 0 <= i +...  63.3 us
    all_to_all x3, waiting for transfers between devices, exchange(): return lax.all_to_all(array, BOTH, 0, 0, axis_index_groups=groups)  60.2 us
    ppermute x6, waiting for transfers between devices, mp_shift(): lax.ppermute(shard, 'mp', [(i, (i + by) % count) for i in range(count)])  58.5 us
    unnamed x240, local copies, waits for them, and re-layouts  35.5 us
    pallas_call x2, Pallas kernels, total_over_all(): pl.pallas_call(functools.partial(total_kernel, seq_bits=seq_bits, mp_bits...  32.4 us
  transfers between devices with their start and end apart: 27, of which 15 were waited for; matrix products, arithmetic and copies ran while one was open for 26% of the time, Pallas kernels for 37%

profile of v3, /device:TPU:0, one launch (start us, length us, event | category | flops | bytes accessed | tf_op | source)
XLA Modules:
  0.0 984.4 jit_solution(17398560083501238645)
XLA Ops:
  44.3 7.9 fusion.64
  55.6 7.5 multiply_convert_fusion.5
  81.6 12.5 %collective-permute-done.1 = bf16[512,512]{1,0:T(8,128)(2,1)S(1)} collective-permute-done((bf16[512,512]{1,0:T(8,128)(2,1)S(1)}, bf16[512,512]{1,0:T(8,128)(2,1)S(1)}, u32[]{:S(2)}, u32[]{:S(2)}) %collective-permute-start.1) | collective-permute-done | bytes 524320 | tf_op jit(solution)/shard_map/ppermute | solution.py:43
  120.3 13.5 %all-gather.15.cloned.1.call-done.in_ref = bf16[4096,1024]{1,0:T(8,128)(2,1)} async-done(((bf16[512,1024]{1,0:T(8,128)(2,1)}), bf16[4096,1024]{1,0:T(8,128)(2,1)}) %all-gather.15.cloned.1.call-update) | async-done | bytes 8388624 | tf_op jit(solution)/shard_map/all_gather | solution.py:794
  142.9 6.3 project.1
  163.8 25.5 %collective-permute-done.2.rest_0_ = bf16[3072,256]{1,0:T(8,128)(2,1)} collective-permute-done((bf16[3072,256]{1,0:T(8,128)(2,1)}, bf16[3072,256]{1,0:T(8,128)(2,1)}, u32[]{:S(2)}, u32[]{:S(2)}) %collective-permute-start.2) | collective-permute-done | bytes 1572896 | tf_op jit(solution)/shard_map/ppermute | solution.py:52
  194.6 44.8 %attend.1 = (bf16[4096,128]{1,0:T(8,128)(2,1)}, f32[4096,128]{1,0:T(8,128)}, f32[8,1,512]{2,1,0:T(1,128)}) custom-call(s32[8]{0:T(128)} %get-tuple-element.282.lo_ref, s32[8]{0:T(128)} %get-tuple-element.281.hi_ref, bf16[4096,128]{1,0:T(8,128)(2,1)} %copy-done.10, s32[8,1,512]{2,1,0:T(1,128)} %bitcast.336, s32[8,1,512]{2,1,0:T(1,128)} %bitcast.338, ...), custom_call_target="tpu_custom_call" | custom-call | flops 47311749120 | bytes 16777216 | tf_op jit(solution)/shard_map/attend/pallas_call | solution.py:654
  243.2 6.1 fusion.87
  249.3 8.1 all-to-all-done
  278.9 18.4 %total_over_all.2 = f32[16,128]{1,0:T(8,128)} custom-call(f32[16,128]{1,0:T(8,128)} %reshape.457.in_ref), custom_call_target="tpu_custom_call" | custom-call | tf_op jit(solution)/shard_map/total_over_all/pallas_call | solution.py:271
  306.5 11.1 %multiply_convert_fusion.1 = (bf16[512,4096]{1,0:T(8,128)(2,1)}, f32[512,4096]{1,0:T(8,128)}) fusion(bf16[512,1024]{1,0:T(8,128)(2,1)S(1)} %multiply_convert_fusion.12.refs_1_, bf16[4096,1024]{0,1:T(8,128)(2,1)} %all-gather.21.cloned.1.call-done), kind=kOutput, calls=%fused_computation.1 | convolution fusion | flops 4305453056 | bytes 22020096 | tf_op jit(solution)/shard_map/dot_general | solution.py:26
  317.7 9.7 fusion.100
  338.9 9.6 multiply_convert_fusion.refs_0_
  348.5 9.7 multiply_reduce_fusion.1
  364.7 15.0 %products.2 = bf16[8,1024,1024]{2,1,0:T(8,128)(2,1)} custom-call(bf16[512,4096]{1,0:T(8,128)(2,1)} %multiply_convert_fusion.refs_0_, bf16[512,1024]{1,0:T(8,128)(2,1)S(1)} %multiply_convert_fusion.12.refs_1_, bf16[512,4096]{1,0:T(8,128)(2,1)} %get-tuple-element.270.refs_2_, bf16[512,1024]{1,0:T(8,128)(2,1)S(1)} %get-tuple-element.178.refs_3_), custom_call_target="tpu_custom_call" | custom-call | flops 8589934592 | bytes 16777216 | tf_op jit(solution)/shard_map/products/pallas_call | solution.py:160
  380.3 14.0 %total_over_all.3 = f32[16,128]{1,0:T(8,128)} custom-call(f32[16,128]{1,0:T(8,128)} %reshape.461.in_ref), custom_call_target="tpu_custom_call" | custom-call | tf_op jit(solution)/shard_map/total_over_all/pallas_call | solution.py:271
  395.0 10.3 %fusion.27 = (f32[1024]{0:T(1024)}, f32[1024]{0:T(1024)}, f32[1024]{0:T(1024)}, f32[1024]{0:T(1024)}, f32[1024]{0:T(1024)}, /*index=5*/bf16[512,1024]{1,0:T(8,128)(2,1)S(1)}) fusion(f32[516,1024]{1,0:T(8,128)} %copy-done.11, pred[512]{0:T(512)(128)(4,1)S(1)} %get-tuple-element.255, pred[512]{0:T(512)(128)(4,1)S(1)} %get-tuple-element.254, ...), kind=kLoop, calls=%fused_computation.58 | loop fusion | flops 12053504 | bytes 15771648 | tf_op jit(solution)/shard_map/reduce_sum | solution.py:975
  433.1 15.5 %products.3 = bf16[8,768,1024]{2,1,0:T(8,128)(2,1)} custom-call(bf16[512,1024]{1,0:T(8,128)(2,1)S(1)} %multiply_convert_fusion.8.refs_0_, bf16[512,1024]{1,0:T(8,128)(2,1)S(1)} %multiply_convert_fusion.15.refs_1_.refs_3_, bf16[512,1024]{1,0:T(8,128)(2,1)S(1)} %get-tuple-element.174.refs_2_, bf16[512,1024]{1,0:T(8,128)(2,1)S(1)} %multiply_convert_fusion.15.refs_1_.refs_3_, ...), custom_call_target="tpu_custom_call" | custom-call | flops 6442450944 | bytes 12582912 | tf_op jit(solution)/shard_map/products/pallas_call | solution.py:160
  448.6 8.1 all-to-all-done.1
  456.7 63.8 %attend_back.1 = (bf16[4096,128]{1,0:T(8,128)(2,1)}, bf16[3072,256]{1,0:T(8,128)(2,1)}, f32[4096,256]{1,0:T(8,128)}, bf16[3072,256]{1,0:T(8,128)(2,1)}) custom-call(s32[8]{0:T(128)} %get-tuple-element.282.lo_ref, s32[8]{0:T(128)} %get-tuple-element.281.hi_ref, bf16[4096,128]{1,0:T(8,128)(2,1)} %copy-done.10, bf16[4096,128]{1,0:T(8,128)(2,1)} %bitcast.62.do_ref, ...), custom_call_target="tpu_custom_call" | custom-call | flops 63082332160 | bytes 16777216 | tf_op jit(solution)/shard_map/attend_back/pallas_call | solution.py:654
  521.8 10.9 %collective-permute-start.11 = (bf16[3072,256]{1,0:T(8,128)(2,1)}, bf16[3072,256]{1,0:T(8,128)(2,1)}, u32[]{:S(2)}, u32[]{:S(2)}) collective-permute-start(bf16[3072,256]{1,0:T(8,128)(2,1)} %get-tuple-element.116), channel_id=1, source_target_pairs={{0,8},{2,10},{4,12},{6,14},{8,16},{10,18},{12,20},{14,22},{16,24},... | collective-permute-start | bytes 4718600 | tf_op jit(solution)/shard_map/ppermute | solution.py:52
  532.8 31.2 %collective-permute-done.10.rest_0_ = bf16[3072,256]{1,0:T(8,128)(2,1)S(1)} collective-permute-done((bf16[3072,256]{1,0:T(8,128)(2,1)}, bf16[3072,256]{1,0:T(8,128)(2,1)S(1)}, u32[]{:S(2)}, u32[]{:S(2)}) %collective-permute-start.10) | collective-permute-done | bytes 1572896 | tf_op jit(solution)/shard_map/ppermute | solution.py:52
  565.3 8.6 gathered.1
  578.5 9.8 convolution_convert_fusion.5
  588.3 43.9 %all-to-all-done.2 = bf16[8,512,384]{2,1,0:T(8,128)(2,1)} async-done(((bf16[8,512,384]{2,1,0:T(8,128)(2,1)}), bf16[8,512,384]{2,1,0:T(8,128)(2,1)}, u32[]{:S(2)}, u32[]{:S(2)}) %all-to-all-start.2) | async-done | bytes 3145760 | tf_op jit(solution)/shard_map/all_to_all | solution.py:899
  633.5 7.2 fusion.48
  649.9 23.3 %collective-permute-done.12 = bf16[512,1024]{1,0:T(8,128)(2,1)S(1)} collective-permute-done((bf16[512,1024]{1,0:T(8,128)(2,1)S(1)}, bf16[512,1024]{1,0:T(8,128)(2,1)S(1)}, u32[]{:S(2)}, u32[]{:S(2)}) %collective-permute-start.12) | collective-permute-done | bytes 1048608 | tf_op jit(solution)/shard_map/ppermute | solution.py:43
  673.1 7.0 multiply_convert_fusion.2
  688.5 19.3 %collective-permute-done.13 = bf16[512,1024]{1,0:T(8,128)(2,1)S(1)} collective-permute-done((bf16[512,1024]{1,0:T(8,128)(2,1)S(1)}, bf16[512,1024]{1,0:T(8,128)(2,1)S(1)}, u32[]{:S(2)}, u32[]{:S(2)}) %collective-permute-start.13) | collective-permute-done | bytes 1048608 | tf_op jit(solution)/shard_map/ppermute | solution.py:43
  712.9 16.2 %reduce-scatter.8.cloned.1.call-done = bf16[544,1024]{1,0:T(8,128)(2,1)} async-done(((bf16[2176,1024]{1,0:T(8,128)(2,1)}), bf16[544,1024]{1,0:T(8,128)(2,1)}) %reduce-scatter.8.cloned.1.call-update) | async-done | bytes 1114128 | tf_op jit(solution)/shard_map/reduce_scatter | solution.py:807
  749.5 170.8 %seq_total.1 = (f32[88,128]{1,0:T(8,128)}, bf16[1024,1024]{1,0:T(8,128)(2,1)}, bf16[1024,1024]{1,0:T(8,128)(2,1)}, bf16[1024,1024]{1,0:T(8,128)(2,1)}, bf16[2,10...) custom-call(f32[88,128]{1,0:T(8,128)} %reshape.468.small_ref, bf16[512,1024]{1,0:T(8,128)(2,1)} %fusion.18.refs_0_, ...), custom_call_target="tpu_custom_call" | custom-call | flops 99999997952 | bytes 33554432 | tf_op jit(solution)/shard_map/seq_total/pallas_call | solution.py:432
  940.4 8.0 laid.8
  (467 shorter events, 293.1 us)
Async XLA Ops:
  7.2 70.7 %copy-start = (bf16[1024,1024]{1,0:T(8,128)(2,1)S(1)}, bf16[1024,1024]{1,0:T(8,128)(2,1)}, u32[]{:S(2)}) copy-start(bf16[1024,1024]{1,0:T(8,128)(2,1)} %param.49) | copy-start | bytes 6291460
  7.2 99.0 %all-gather.17.cloned.1.call-start = ((), (), s32[]{:S(2)}) async-start(), calls=%async_computation.10 | async-start | bytes 4718592 | tf_op jit(solution)/shard_map/all_gather | solution.py:794
  13.7 120.2 %all-gather.15.cloned.1.call-start = ((), (), s32[]{:S(2)}) async-start(), calls=%async_computation.9 | async-start | bytes 9437184 | tf_op jit(solution)/shard_map/all_gather | solution.py:794
  27.3 39.1 %collective-permute-start = (bf16[512,1024]{1,0:T(8,128)(2,1)}, bf16[512,1024]{1,0:T(8,128)(2,1)}, u32[]{:S(2)}, u32[]{:S(2)}) collective-permute-start(bf16[512,1024]{1,0:T(8,128)(2,1)} %convolution_convert_fusion.3), channel_id=1, source_target_pairs={{0,1},{1,0},{2,3},{3,2},{4,5},{5,4},{6,7},{7,6},{8,9},{9,8},{10,11... | collective-permute-start | bytes 3145736 | tf_op jit(solution)/shard_map/ppermute | solution.py:43
  44.3 93.4 %copy-start.79 = (s32[4096]{0:T(1024)}, s32[4096]{0:T(1024)S(1)}, u32[]{:S(2)}) copy-start(s32[4096]{0:T(1024)S(1)} %get-tuple-element.236) | copy-start | bytes 49156
  55.5 82.4 %copy-start.6 = (bf16[1024,384]{1,0:T(8,128)(2,1)}, bf16[1024,384]{1,0:T(8,128)(2,1)S(1)}, u32[]{:S(2)}) copy-start(bf16[1024,384]{1,0:T(8,128)(2,1)S(1)} %pad_maximum_fusion.11.matrix_ref) | copy-start | bytes 2359300
  76.8 166.4 %all-gather.19.cloned.1.call-start = ((), (), s32[]{:S(2)}) async-start(), calls=%async_computation.11 | async-start | bytes 9437184 | tf_op jit(solution)/shard_map/all_gather | solution.py:794
  76.9 17.3 %collective-permute-start.1 = (bf16[512,512]{1,0:T(8,128)(2,1)S(1)}, bf16[512,512]{1,0:T(8,128)(2,1)S(1)}, u32[]{:S(2)}, u32[]{:S(2)}) collective-permute-start(bf16[512,512]{1,0:T(8,128)(2,1)S(1)} %copy-done.62), channel_id=1, source_target_pairs={{0,1},{1,0},{2,3},{3,2},{4,5},{5,4},{6,7},{7,6},{8,9},{9,8},{10,11... | collective-permute-start | bytes 1572872 | tf_op jit(solution)/shard_map/ppermute | solution.py:43
  135.2 171.3 %all-gather.21.cloned.1.call-start = ((), (), s32[]{:S(2)}) async-start(), calls=%async_computation.12 | async-start | bytes 9437184 | tf_op jit(solution)/shard_map/all_gather | solution.py:794
  135.8 181.9 %all-gather.23.cloned.1.call-start = ((), (), s32[]{:S(2)}) async-start(), calls=%async_computation.13 | async-start | bytes 9437184 | tf_op jit(solution)/shard_map/all_gather | solution.py:794
  136.4 106.6 %collective-permute-start.4 = (f32[7,512]{1,0:T(8,128)S(1)}, f32[7,512]{1,0:T(8,128)S(1)}, u32[]{:S(2)}, u32[]{:S(2)}) collective-permute-start(f32[7,512]{1,0:T(8,128)S(1)} %get-tuple-element.184), channel_id=1, source_target_pairs={{0,1},{1,0},{2,3},{3,2},{4,5},{5,4},{6,7},{7,6},{8,9},{9,8},{10,11... | collective-permute-start | bytes 43016 | tf_op jit(solution)/shard_map/ppermute | solution.py:43
  151.9 37.4 %collective-permute-start.2 = (bf16[3072,256]{1,0:T(8,128)(2,1)}, bf16[3072,256]{1,0:T(8,128)(2,1)}, u32[]{:S(2)}, u32[]{:S(2)}) collective-permute-start(bf16[3072,256]{1,0:T(8,128)(2,1)} %get-tuple-element.200), channel_id=1, source_target_pairs={{0,8},{2,10},{4,12},{6,14},{8,16},{10,18},{12,20},{14,22},{16,24},... | collective-permute-start | bytes 4718600 | tf_op jit(solution)/shard_map/ppermute | solution.py:52
  156.5 38.2 %collective-permute-start.3 = (bf16[3072,256]{1,0:T(8,128)(2,1)}, bf16[3072,256]{1,0:T(8,128)(2,1)}, u32[]{:S(2)}, u32[]{:S(2)}) collective-permute-start(bf16[3072,256]{1,0:T(8,128)(2,1)} %get-tuple-element.199), channel_id=1, source_target_pairs={{8,0},{10,2},{12,4},{14,6},{16,8},{18,10},{20,12},{22,14},{24,16},... | collective-permute-start | bytes 4718600 | tf_op jit(solution)/shard_map/ppermute | solution.py:52
  239.4 18.0 %all-to-all-start = ((bf16[8,512,128]{2,1,0:T(8,128)(2,1)}), bf16[8,512,128]{2,1,0:T(8,128)(2,1)S(1)}, u32[]{:S(2)}, u32[]{:S(2)}) async-start(bf16[8,512,128]{2,1,0:T(8,128)(2,1)} %bitcast.306), calls=%async_computation | async-start | bytes 2097152 | tf_op jit(solution)/shard_map/all_to_all | solution.py:899
  243.0 136.7 %all-gather.25.cloned.1.call-start = ((), (), s32[]{:S(2)}) async-start(), calls=%async_computation.14 | async-start | bytes 7077888 | tf_op jit(solution)/shard_map/all_gather | solution.py:794
  267.4 6.0 collective-permute-start.6
  268.7 5.9 collective-permute-start.5
  273.3 247.2 %reduce-scatter.4.cloned.1.call-start = ((), (), s32[]{:S(2)}) async-start(), calls=%async_computation.6 | async-start | bytes 18874368 | tf_op jit(solution)/shard_map/reduce_scatter | solution.py:807
  331.6 4.5 collective-permute-start.7
  405.3 6.0 collective-permute-start.9
  406.8 5.9 collective-permute-start.8
  426.4 30.3 %all-to-all-start.1 = ((bf16[8,512,128]{2,1,0:T(8,128)(2,1)}), bf16[8,512,128]{2,1,0:T(8,128)(2,1)}, u32[]{:S(2)}, u32[]{:S(2)}) async-start(bf16[8,512,128]{2,1,0:T(8,128)(2,1)} %bitcast.282), calls=%async_computation.1 | async-start | bytes 2097152 | tf_op jit(solution)/shard_map/all_to_all | solution.py:899
  430.7 212.0 %reduce-scatter.6.cloned.1.call-start = ((), (), s32[]{:S(2)}) async-start(), calls=%async_computation.7 | async-start | bytes 14155776 | tf_op jit(solution)/shard_map/reduce_scatter | solution.py:807
  520.5 43.5 %collective-permute-start.10 = (bf16[3072,256]{1,0:T(8,128)(2,1)}, bf16[3072,256]{1,0:T(8,128)(2,1)S(1)}, u32[]{:S(2)}, u32[]{:S(2)}) collective-permute-start(bf16[3072,256]{1,0:T(8,128)(2,1)} %get-tuple-element.115), channel_id=1, source_target_pairs={{8,0},{10,2},{12,4},{14,6},{16,8},{18,10},{20,12},{22,14},{24,16},... | collective-permute-start | bytes 4718600 | tf_op jit(solution)/shard_map/ppermute | solution.py:52
  521.8 43.5 %collective-permute-start.11 = (bf16[3072,256]{1,0:T(8,128)(2,1)}, bf16[3072,256]{1,0:T(8,128)(2,1)}, u32[]{:S(2)}, u32[]{:S(2)}) collective-permute-start(bf16[3072,256]{1,0:T(8,128)(2,1)} %get-tuple-element.116), channel_id=1, source_target_pairs={{0,8},{2,10},{4,12},{6,14},{8,16},{10,18},{12,20},{14,22},{16,24},... | collective-permute-start | bytes 4718600 | tf_op jit(solution)/shard_map/ppermute | solution.py:52
  573.9 58.3 %all-to-all-start.2 = ((bf16[8,512,384]{2,1,0:T(8,128)(2,1)}), bf16[8,512,384]{2,1,0:T(8,128)(2,1)}, u32[]{:S(2)}, u32[]{:S(2)}) async-start(bf16[8,512,384]{2,1,0:T(8,128)(2,1)} %bitcast.275), calls=%async_computation.3 | async-start | bytes 6291456 | tf_op jit(solution)/shard_map/all_to_all | solution.py:899
  578.4 55.0 %copy-start.17 = (f32[512,1024]{1,0:T(8,128)S(1)}, f32[512,1024]{1,0:T(8,128)}, u32[]{:S(2)}) copy-start(f32[512,1024]{1,0:T(8,128)} %multiply_add_fusion.7) | copy-start | bytes 6291460
  578.4 55.0 %copy-start.68 = (f32[512]{0:T(512)S(1)}, f32[512]{0:T(512)}, u32[]{:S(2)}) copy-start(f32[512]{0:T(512)} %copy-done.67) | copy-start | bytes 6148
  578.4 150.7 %reduce-scatter.8.cloned.1.call-start = ((), (), s32[]{:S(2)}) async-start(), calls=%async_computation.8 | async-start | bytes 5570560 | tf_op jit(solution)/shard_map/reduce_scatter | solution.py:807
  646.5 287.8 %all-gather.27.cloned.1.call-start = ((), (), s32[]{:S(2)}) async-start(), calls=%async_computation.15 | async-start | bytes 18939904 | tf_op jit(solution)/shard_map/all_gather | solution.py:1044
  648.3 24.8 %collective-permute-start.12 = (bf16[512,1024]{1,0:T(8,128)(2,1)S(1)}, bf16[512,1024]{1,0:T(8,128)(2,1)S(1)}, u32[]{:S(2)}, u32[]{:S(2)}) collective-permute-start(bf16[512,1024]{1,0:T(8,128)(2,1)S(1)} %multiply_convert_fusion.6), channel_id=1, source_target_pairs={{0,1},{1,0},{2,3},{3,2},{4,5},{5,4},{6,7},{7,6},{8,9},{9,8},{10,11... | collective-permute-start | bytes 3145736 | tf_op jit(solution)/shard_map/ppermute | solution.py:43
  683.9 24.0 %collective-permute-start.13 = (bf16[512,1024]{1,0:T(8,128)(2,1)S(1)}, bf16[512,1024]{1,0:T(8,128)(2,1)S(1)}, u32[]{:S(2)}, u32[]{:S(2)}) collective-permute-start(bf16[512,1024]{1,0:T(8,128)(2,1)S(1)} %convolution_convert_fusion.2), channel_id=1, source_target_pairs={{0,1},{1,0},{2,3},{3,2},{4,5},{5,4},{6,7},{7,6},{8,9},{9,8},{10,11... | collective-permute-start | bytes 3145736 | tf_op jit(solution)/shard_map/ppermute | solution.py:43
  (113 other events, 718.3 us)
Sparse Core Ops, SparseCore 0:
  13.8 51.4 all-gather.16
  76.9 56.8 all-gather.14
  136.3 54.3 all-gather.18
  193.0 55.9 all-gather.20
  250.8 65.6 all-gather.22
  318.2 45.5 all-gather.24
  379.8 125.8 reduce-scatter.3
  509.3 124.4 reduce-scatter.5
  646.6 82.4 reduce-scatter.7
  730.6 157.5 all-gather.26

commit v4 on v3

--- a/solution.py
+++ b/solution.py
@@ -90,23 +90,22 @@
     return int(math.log2(number))
 
 
-def laid_kernel(in_ref, out_ref, *, places, turned):
-    rows = in_ref.shape[1]
-    for s, place in enumerate(places):
-        block = in_ref[s].astype(WIDE)
-        span = slice(place * rows, (place + 1) * rows)
+def laid_kernel(in_ref, out_ref, *, local_heads, turned):
+    count, rows, _ = in_ref.shape
+    height = count * rows // local_heads
+    for g in range(local_heads):
+        block = jnp.concatenate([in_ref[s] for s in range(g, count, local_heads)], 0).astype(WIDE)
+        part = part_of(g, local_heads)
         if turned:
-            out_ref[0, :, span] = block.T
+            out_ref[0, :, part * height : (part + 1) * height] = block.T
         else:
-            out_ref[0, span, :] = block
+            out_ref[0, part * height : (part + 1) * height, :] = block
 
 
 def laid(every, first, rows, amount, local_heads, turned):
     count, _, columns = every.shape
-    line = count // local_heads
-    places = [part_of(s % local_heads, local_heads) * line + s // local_heads for s in range(count)]
     if rows % 16 or count * rows % 128:
-        order = sorted(range(count), key=lambda s: places[s])
+        order = sorted(range(count), key=lambda s: (part_of(s % local_heads, local_heads), s // local_heads))
         whole = every[:, first : first + amount * rows].reshape(count, amount, rows, columns)
         whole = jnp.stack([whole[s] for s in order], 1).astype(WIDE).reshape(amount, count * rows, columns)
         return jnp.transpose(whole, (0, 2, 1)) if turned else whole
@@ -114,7 +113,7 @@
     width = min(columns, 2**19 // (count * rows))
     block = (1, width, count * rows) if turned else (1, count * rows, width)
     return pl.pallas_call(
-        functools.partial(laid_kernel, places=places, turned=turned),
+        functools.partial(laid_kernel, local_heads=local_heads, turned=turned),
         grid=(amount, columns // width),
         in_specs=[pl.BlockSpec((count, rows, width), lambda i, j: (0, first // rows + i, j))],
         out_specs=pl.BlockSpec(block, lambda i, j: (i, j, 0) if turned else (i, 0, j)),
@@ -546,7 +545,7 @@
             at += piece.shape[0]
 
 
-def attend_kernel(lo_ref, hi_ref, q_ref, start_ref, end_ref, *rest, count, depth):
+def attend_kernel(lo_ref, inner_ref, outer_ref, hi_ref, q_ref, start_ref, end_ref, *rest, count, depth):
     pieces = rest[:count]
     low_ref, mix_ref, lse_ref, kv_ref = rest[count:]
     gather_keys(pieces, kv_ref)
@@ -555,15 +554,16 @@
     rows = queries.shape[0]
     first, last = start_ref[0], end_ref[0]
 
-    def step(t, carry):
+    def step(masked, t, carry):
         top, total, mixed = carry
         at = pl.multiple_of(t * depth, depth)
         keys = kv_ref[pl.ds(at, depth), :HEAD]
         values = kv_ref[pl.ds(at, depth), HEAD:]
-        index = lax.broadcasted_iota(jnp.int32, (depth, 1), 0) + at
         scores = dot_nt(keys, queries) * SCALE_2
-        inside = jnp.logical_and(index >= first, index < last)
-        scores = jnp.where(inside, scores, MASKED)
+        if masked:
+            index = lax.broadcasted_iota(jnp.int32, (depth, 1), 0) + at
+            inside = jnp.logical_and(index >= first, index < last)
+            scores = jnp.where(inside, scores, MASKED)
         new_top = jnp.maximum(top, jnp.max(scores, 0, keepdims=True))
         probs = jnp.exp2(scores - new_top)
         fade = jnp.exp2(top - new_top)
@@ -572,7 +572,7 @@
         return new_top, total, mixed
 
     start = (jnp.full((1, rows), MASKED, WIDE), jnp.zeros((1, rows), WIDE), jnp.zeros((HEAD, rows), WIDE))
-    top, total, mixed = lax.fori_loop(lo_ref[i], hi_ref[i], step, start)
+    top, total, mixed = over_blocks(step, start, lo_ref[i], inner_ref[i], outer_ref[i], hi_ref[i])
     mixed = jnp.transpose(mixed / total)
     mix_ref[...] = mixed
     low_ref[...] = mixed.astype(LOW)
@@ -580,7 +580,7 @@
 
 
 def attend_back_kernel(
-    lo_ref, hi_ref, q_ref, do_ref, mix_ref, lse_ref, start_ref, end_ref, cos_ref, sin_ref, *rest, count, depth, parts
+    lo_ref, inner_ref, outer_ref, hi_ref, q_ref, do_ref, mix_ref, lse_ref, start_ref, end_ref, cos_ref, sin_ref, *rest, count, depth, parts
 ):
     pieces = rest[:count]
     dq_ref = rest[count]
@@ -599,16 +599,18 @@
     delta = jnp.sum(products, 0, keepdims=True)
     height = depth // parts
 
-    def step(t, grad_query):
+    def step(masked, t, grad_query):
         for part in range(parts):
             at = pl.multiple_of(t * depth + part * height, height)
             span = pl.ds(at, height)
             keys = kv_ref[span, :HEAD]
             values = kv_ref[span, HEAD:]
-            index = lax.broadcasted_iota(jnp.int32, (height, 1), 0) + at
-            inside = jnp.logical_and(index >= first, index < last)
             scores = dot_nt(keys, queries) * SCALE_2
-            probs = jnp.where(inside, jnp.exp2(scores - lse), 0.0)
+            probs = jnp.exp2(scores - lse)
+            if masked:
+                index = lax.broadcasted_iota(jnp.int32, (height, 1), 0) + at
+                inside = jnp.logical_and(index >= first, index < last)
+                probs = jnp.where(inside, probs, 0.0)
             grad_probs = dot_nt(values, upstream)
             grad_scores = (probs * (grad_probs - delta)).astype(LOW)
             dkv_ref[span, HEAD:] += dot(probs.astype(LOW), upstream)
@@ -616,7 +618,8 @@
             grad_query = grad_query + dot_tn(grad_scores, keys)
         return grad_query
 
-    grad_query = lax.fori_loop(lo_ref[i], hi_ref[i], step, jnp.zeros(queries.shape, WIDE)) * SCALE
+    nothing = jnp.zeros(queries.shape, WIDE)
+    grad_query = over_blocks(step, nothing, lo_ref[i], inner_ref[i], outer_ref[i], hi_ref[i]) * SCALE
     dq_ref[...] = (grad_query * cos_ref[...] - swapped(grad_query) * sin_ref[...]).astype(LOW)
 
     @pl.when(i == pl.num_programs(0) - 1)
@@ -633,17 +636,25 @@
     return pl.BlockSpec(array.shape, lambda i, *_: (0,) * len(array.shape))
 
 
+def over_blocks(step, carry, lo, inner, outer, hi):
+    carry = lax.fori_loop(lo, inner, functools.partial(step, True), carry)
+    carry = lax.fori_loop(inner, outer, functools.partial(step, False), carry)
+    return lax.fori_loop(outer, hi, functools.partial(step, True), carry)
+
+
 def bounds(starts, ends, rows, depth, key_rows):
     count = key_rows // depth
     lo = jnp.clip(starts[::rows] // depth, 0, count)
     hi = jnp.clip((ends[rows - 1 :: rows] + depth - 1) // depth, 0, count)
-    return lo.astype(jnp.int32), hi.astype(jnp.int32)
+    inner = jnp.clip((starts[rows - 1 :: rows] + depth - 1) // depth, lo, hi)
+    outer = jnp.clip(ends[::rows] // depth, inner, hi)
+    return [b.astype(jnp.int32) for b in (lo, inner, outer, hi)]
 
 
 def attention_call(kernel, by_row, by_lane, pieces, spans, out_rows, out_lanes, grads, rows, depth, name, **more):
     count = by_row[0].shape[0]
     key_rows = sum(piece.shape[0] for piece in pieces)
-    lo, hi = bounds(*spans, rows, depth, key_rows)
+    blocks = bounds(*spans, rows, depth, key_rows)
     row = pl.BlockSpec((rows, HEAD), lambda i, *_: (i, 0))
     lane = pl.BlockSpec((1, 1, rows), lambda i, *_: (i, 0, 0))
     lanes = [v.reshape(count // rows, 1, rows) for v in by_lane + list(spans)]
@@ -654,7 +665,7 @@
     return pl.pallas_call(
         functools.partial(kernel, count=len(pieces), depth=depth, **more),
         grid_spec=pltpu.PrefetchScalarGridSpec(
-            num_scalar_prefetch=2,
+            num_scalar_prefetch=4,
             grid=(count // rows,),
             in_specs=[row] * len(by_row) + [lane] * len(lanes) + [row] * len(tail) + [whole_block(p) for p in pieces],
             out_specs=[row] * len(out_rows) + [lane] * out_lanes + [whole_block(g) for g in grads],
@@ -670,16 +681,16 @@
             transcendentals=count * LONGEST,
         ),
         name=name,
-    )(lo, hi, *by_row, *lanes, *tail, *pieces)
-
-
-def attend(queries, pieces, spans, rows=512, depth=1024):
+    )(*blocks, *by_row, *lanes, *tail, *pieces)
+
+
+def attend(queries, pieces, spans, rows=512, depth=512):
     return attention_call(
         attend_kernel, [queries], [], pieces, spans, [LOW, WIDE], 1, [], rows, depth, "attend"
     )
 
 
-def attend_back(queries, upstream, mixed, lse, tables, pieces, spans, rows=512, depth=1024):
+def attend_back(queries, upstream, mixed, lse, tables, pieces, spans, rows=512, depth=512):
     middle = len(pieces) // 2
     grads = [
         jax.ShapeDtypeStruct(p.shape, WIDE if j == middle else LOW) for j, p in enumerate(pieces)
@@ -697,7 +708,7 @@
         depth,
         "attend_back",
         tail=list(tables),
-        parts=2,
+        parts=1,
     )
 
 

time: 996 us -> 980 us (0.984)
  Pallas kernels: 395 us -> 358 us
  waiting for transfers between devices: 215 us -> 236 us
    pallas_call x2, Pallas kernels: 109 us -> 79.1 us  [attention_call(): pl.pallas_call(functools.partial(kernel, count=len(pieces), depth=depth,...]
    reduce_scatter x3, waiting for transfers between devices: 16.3 us -> 30.8 us  [group_total(): lax.psum_scatter(array, BOTH, scatter_dimension=0, axis_index_groups=over...]
  transfers between devices with their start and end apart: 27 -> 27, of which waited for: 15 -> 17; matrix products, arithmetic and copies ran while one was open for 26% -> 27% of each run, Pallas kernels for 37% -> 35%
where the time goes in v4:
time: 980 us; the launch traced here: 964 us
  Pallas kernels  358 us (37%)
  waiting for transfers between devices  236 us (24%)
  matrix products  142 us (14%)
  local copies, waits for them, and re-layouts  88.4 us (9%)
  other arithmetic  72.1 us (7%)
  starting transfers between devices  50.3 us (5%)
  between operations  17.6 us (2%)
    pallas_call x1, Pallas kernels, seq_total(): pl.pallas_call(functools.partial(seq_total_kernel, count=count, chunks=ch...  171 us
    dot_general x31, matrix products, dot(): return lax.dot_general(a, b, (dims, ((), ())), preferred_element_type=WIDE)  134 us
    pallas_call x2, Pallas kernels, attention_call(): pl.pallas_call(functools.partial(kernel, count=len(pieces), depth=depth,...  79.1 us
    all_to_all x3, waiting for transfers between devices, exchange(): return lax.all_to_all(array, BOTH, 0, 0, axis_index_groups=groups)  65.1 us
    ppermute x4, waiting for transfers between devices, seq_shift(): lax.ppermute(shard, 'seq', [(i, i + by) for i in range(count) if 0 <= i +...  63.6 us
    ppermute x6, waiting for transfers between devices, mp_shift(): lax.ppermute(shard, 'mp', [(i, (i + by) % count) for i in range(count)])  59.8 us
    unnamed x240, local copies, waits for them, and re-layouts  35.2 us
    pallas_call x2, Pallas kernels, total_over_all(): pl.pallas_call(functools.partial(total_kernel, seq_bits=seq_bits, mp_bits...  33.4 us
  transfers between devices with their start and end apart: 27, of which 17 were waited for; matrix products, arithmetic and copies ran while one was open for 27% of the time, Pallas kernels for 35%

profile of v4, /device:TPU:0, one launch (start us, length us, event | category | flops | bytes accessed | tf_op | source)
XLA Modules:
  0.0 963.8 jit_solution(4730182495784696596)
XLA Ops:
  44.3 7.7 fusion.64
  55.3 7.5 multiply_convert_fusion.5
  81.6 12.5 %collective-permute-done.1 = bf16[512,512]{1,0:T(8,128)(2,1)S(1)} collective-permute-done((bf16[512,512]{1,0:T(8,128)(2,1)S(1)}, bf16[512,512]{1,0:T(8,128)(2,1)S(1)}, u32[]{:S(2)}, u32[]{:S(2)}) %collective-permute-start.1) | collective-permute-done | bytes 524320 | tf_op jit(solution)/shard_map/ppermute | solution.py:43
  120.6 13.2 %all-gather.15.cloned.1.call-done.in_ref = bf16[4096,1024]{1,0:T(8,128)(2,1)} async-done(((bf16[512,1024]{1,0:T(8,128)(2,1)}), bf16[4096,1024]{1,0:T(8,128)(2,1)}) %all-gather.15.cloned.1.call-update) | async-done | bytes 8388624 | tf_op jit(solution)/shard_map/all_gather | solution.py:805
  143.2 6.3 project.1
  163.7 25.8 %collective-permute-done.2.rest_0_ = bf16[3072,256]{1,0:T(8,128)(2,1)} collective-permute-done((bf16[3072,256]{1,0:T(8,128)(2,1)}, bf16[3072,256]{1,0:T(8,128)(2,1)}, u32[]{:S(2)}, u32[]{:S(2)}) %collective-permute-start.2) | collective-permute-done | bytes 1572896 | tf_op jit(solution)/shard_map/ppermute | solution.py:52
  194.8 33.1 %attend.1 = (bf16[4096,128]{1,0:T(8,128)(2,1)}, f32[4096,128]{1,0:T(8,128)}, f32[8,1,512]{2,1,0:T(1,128)}) custom-call(s32[8]{0:T(128)} %get-tuple-element.188.lo_ref, s32[8]{0:T(128)} %get-tuple-element.186.inner_ref, s32[8]{0:T(128)} %get-tuple-element.185.outer_ref, s32[8]{0:T(128)} %get-tuple-element.187.hi_ref, bf16[4096,128]{1,0:T(8,128)(2,1)} %copy-done.10, ...), custom_call_target="tpu_custom_call" | custom-call | flops 47311749120 | bytes 16777216 | tf_op jit(solution)/shard_map/attend/pallas_call | solution.py:665
  231.6 6.1 fusion.89
  237.7 18.9 %all-to-all-done = bf16[8,512,128]{2,1,0:T(8,128)(2,1)S(1)} async-done(((bf16[8,512,128]{2,1,0:T(8,128)(2,1)}), bf16[8,512,128]{2,1,0:T(8,128)(2,1)S(1)}, u32[]{:S(2)}, u32[]{:S(2)}) %all-to-all-start) | async-done | bytes 1048608 | tf_op jit(solution)/shard_map/all_to_all | solution.py:910
  278.3 19.2 %total_over_all.2 = f32[16,128]{1,0:T(8,128)} custom-call(f32[16,128]{1,0:T(8,128)} %reshape.457.in_ref), custom_call_target="tpu_custom_call" | custom-call | tf_op jit(solution)/shard_map/total_over_all/pallas_call | solution.py:270
  306.9 11.3 %multiply_convert_fusion.1 = (bf16[512,4096]{1,0:T(8,128)(2,1)}, f32[512,4096]{1,0:T(8,128)}) fusion(bf16[512,1024]{1,0:T(8,128)(2,1)S(1)} %multiply_convert_fusion.12.refs_1_, bf16[4096,1024]{0,1:T(8,128)(2,1)} %all-gather.21.cloned.1.call-done), kind=kOutput, calls=%fused_computation.1 | convolution fusion | flops 4305453056 | bytes 22020096 | tf_op jit(solution)/shard_map/dot_general | solution.py:26
  318.2 9.7 %fusion.102 = (f32[512]{0:T(512)S(1)}, f32[512,1024]{1,0:T(8,128)S(1)}) fusion(f32[512,1024]{1,0:T(8,128)} %copy-done.22, bf16[512,4096]{1,0:T(8,128)(2,1)} %get-tuple-element.274.refs_2_, bf16[4096,1024]{1,0:T(8,128)(2,1)} %all-gather.23.cloned.1.call-done), kind=kOutput, calls=%fused_computation.307 | convolution fusion | flops 4296539648 | bytes 16779264 | tf_op jit(solution)/shard_map/dot_general | solution.py:26
  339.5 9.6 multiply_convert_fusion.refs_0_
  349.1 9.6 multiply_reduce_fusion.1
  365.1 15.1 %products.2 = bf16[8,1024,1024]{2,1,0:T(8,128)(2,1)} custom-call(bf16[512,4096]{1,0:T(8,128)(2,1)} %multiply_convert_fusion.refs_0_, bf16[512,1024]{1,0:T(8,128)(2,1)S(1)} %multiply_convert_fusion.12.refs_1_, bf16[512,4096]{1,0:T(8,128)(2,1)} %get-tuple-element.274.refs_2_, bf16[512,1024]{1,0:T(8,128)(2,1)S(1)} %get-tuple-element.178.refs_3_), custom_call_target="tpu_custom_call" | custom-call | flops 8589934592 | bytes 16777216 | tf_op jit(solution)/shard_map/products/pallas_call | solution.py:159
  380.8 14.1 %total_over_all.3 = f32[16,128]{1,0:T(8,128)} custom-call(f32[16,128]{1,0:T(8,128)} %reshape.461.in_ref), custom_call_target="tpu_custom_call" | custom-call | tf_op jit(solution)/shard_map/total_over_all/pallas_call | solution.py:270
  395.6 10.3 %fusion.27 = (f32[1024]{0:T(1024)}, f32[1024]{0:T(1024)}, f32[1024]{0:T(1024)}, f32[1024]{0:T(1024)}, f32[1024]{0:T(1024)}, /*index=5*/bf16[512,1024]{1,0:T(8,128)(2,1)S(1)}) fusion(f32[516,1024]{1,0:T(8,128)} %copy-done.11, pred[512]{0:T(512)(128)(4,1)S(1)} %get-tuple-element.259, pred[512]{0:T(512)(128)(4,1)S(1)} %get-tuple-element.258, ...), kind=kLoop, calls=%fused_computation.58 | loop fusion | flops 12053504 | bytes 15771648 | tf_op jit(solution)/shard_map/reduce_sum | solution.py:986
  433.2 15.8 %products.3 = bf16[8,768,1024]{2,1,0:T(8,128)(2,1)} custom-call(bf16[512,1024]{1,0:T(8,128)(2,1)S(1)} %multiply_convert_fusion.8.refs_0_, bf16[512,1024]{1,0:T(8,128)(2,1)S(1)} %multiply_convert_fusion.15.refs_1_.refs_3_, bf16[512,1024]{1,0:T(8,128)(2,1)S(1)} %get-tuple-element.174.refs_2_, bf16[512,1024]{1,0:T(8,128)(2,1)S(1)} %multiply_convert_fusion.15.refs_1_.refs_3_, ...), custom_call_target="tpu_custom_call" | custom-call | flops 6442450944 | bytes 12582912 | tf_op jit(solution)/shard_map/products/pallas_call | solution.py:159
  449.0 7.8 all-to-all-done.1
  456.9 46.1 %attend_back.1 = (bf16[4096,128]{1,0:T(8,128)(2,1)}, bf16[3072,256]{1,0:T(8,128)(2,1)}, f32[4096,256]{1,0:T(8,128)}, bf16[3072,256]{1,0:T(8,128)(2,1)}) custom-call(s32[8]{0:T(128)} %get-tuple-element.188.lo_ref, s32[8]{0:T(128)} %get-tuple-element.186.inner_ref, s32[8]{0:T(128)} %get-tuple-element.185.outer_ref, s32[8]{0:T(128)} %get-tuple-element.187.hi_ref, ...), custom_call_target="tpu_custom_call" | custom-call | flops 63082332160 | bytes 16777216 | tf_op jit(solution)/shard_map/attend_back/pallas_call | solution.py:665
  507.6 8.5 collective-permute-start.11
  516.1 31.2 %collective-permute-done.10.rest_0_ = bf16[3072,256]{1,0:T(8,128)(2,1)S(1)} collective-permute-done((bf16[3072,256]{1,0:T(8,128)(2,1)}, bf16[3072,256]{1,0:T(8,128)(2,1)S(1)}, u32[]{:S(2)}, u32[]{:S(2)}) %collective-permute-start.10) | collective-permute-done | bytes 1572896 | tf_op jit(solution)/shard_map/ppermute | solution.py:52
  548.6 8.9 gathered.1
  562.2 8.9 convolution_convert_fusion.5
  571.1 38.4 %all-to-all-done.2 = bf16[8,512,384]{2,1,0:T(8,128)(2,1)} async-done(((bf16[8,512,384]{2,1,0:T(8,128)(2,1)}), bf16[8,512,384]{2,1,0:T(8,128)(2,1)}, u32[]{:S(2)}, u32[]{:S(2)}) %all-to-all-start.2) | async-done | bytes 3145760 | tf_op jit(solution)/shard_map/all_to_all | solution.py:910
  610.7 7.2 fusion.48
  619.9 6.9 reduce-scatter.6.cloned.1.call-done
  633.8 23.8 %collective-permute-done.12 = bf16[512,1024]{1,0:T(8,128)(2,1)S(1)} collective-permute-done((bf16[512,1024]{1,0:T(8,128)(2,1)S(1)}, bf16[512,1024]{1,0:T(8,128)(2,1)S(1)}, u32[]{:S(2)}, u32[]{:S(2)}) %collective-permute-start.12) | collective-permute-done | bytes 1048608 | tf_op jit(solution)/shard_map/ppermute | solution.py:43
  657.6 6.9 multiply_convert_fusion.2
  672.9 19.9 %collective-permute-done.13 = bf16[512,1024]{1,0:T(8,128)(2,1)S(1)} collective-permute-done((bf16[512,1024]{1,0:T(8,128)(2,1)S(1)}, bf16[512,1024]{1,0:T(8,128)(2,1)S(1)}, u32[]{:S(2)}, u32[]{:S(2)}) %collective-permute-start.13) | collective-permute-done | bytes 1048608 | tf_op jit(solution)/shard_map/ppermute | solution.py:43
  697.8 20.5 %reduce-scatter.8.cloned.1.call-done = bf16[544,1024]{1,0:T(8,128)(2,1)} async-done(((bf16[2176,1024]{1,0:T(8,128)(2,1)}), bf16[544,1024]{1,0:T(8,128)(2,1)}) %reduce-scatter.8.cloned.1.call-update) | async-done | bytes 1114128 | tf_op jit(solution)/shard_map/reduce_scatter | solution.py:818
  738.4 170.8 %seq_total.1 = (f32[88,128]{1,0:T(8,128)}, bf16[1024,1024]{1,0:T(8,128)(2,1)}, bf16[1024,1024]{1,0:T(8,128)(2,1)}, bf16[1024,1024]{1,0:T(8,128)(2,1)}, bf16[2,10...) custom-call(f32[88,128]{1,0:T(8,128)} %reshape.468.small_ref, bf16[512,1024]{1,0:T(8,128)(2,1)} %fusion.18.refs_0_, ...), custom_call_target="tpu_custom_call" | custom-call | flops 99999997952 | bytes 33554432 | tf_op jit(solution)/shard_map/seq_total/pallas_call | solution.py:431
  (469 shorter events, 294.6 us)
Async XLA Ops:
  7.2 70.7 %copy-start = (bf16[1024,1024]{1,0:T(8,128)(2,1)S(1)}, bf16[1024,1024]{1,0:T(8,128)(2,1)}, u32[]{:S(2)}) copy-start(bf16[1024,1024]{1,0:T(8,128)(2,1)} %param.49) | copy-start | bytes 6291460
  7.2 99.2 %all-gather.17.cloned.1.call-start = ((), (), s32[]{:S(2)}) async-start(), calls=%async_computation.10 | async-start | bytes 4718592 | tf_op jit(solution)/shard_map/all_gather | solution.py:805
  13.7 120.2 %all-gather.15.cloned.1.call-start = ((), (), s32[]{:S(2)}) async-start(), calls=%async_computation.9 | async-start | bytes 9437184 | tf_op jit(solution)/shard_map/all_gather | solution.py:805
  27.4 39.1 %collective-permute-start = (bf16[512,1024]{1,0:T(8,128)(2,1)}, bf16[512,1024]{1,0:T(8,128)(2,1)}, u32[]{:S(2)}, u32[]{:S(2)}) collective-permute-start(bf16[512,1024]{1,0:T(8,128)(2,1)} %convolution_convert_fusion.3), channel_id=1, source_target_pairs={{0,1},{1,0},{2,3},{3,2},{4,5},{5,4},{6,7},{7,6},{8,9},{9,8},{10,11... | collective-permute-start | bytes 3145736 | tf_op jit(solution)/shard_map/ppermute | solution.py:43
  44.3 93.6 %copy-start.79 = (s32[4096]{0:T(1024)}, s32[4096]{0:T(1024)S(1)}, u32[]{:S(2)}) copy-start(s32[4096]{0:T(1024)S(1)} %get-tuple-element.240) | copy-start | bytes 49156
  55.3 82.8 %copy-start.6 = (bf16[1024,384]{1,0:T(8,128)(2,1)}, bf16[1024,384]{1,0:T(8,128)(2,1)S(1)}, u32[]{:S(2)}) copy-start(bf16[1024,384]{1,0:T(8,128)(2,1)S(1)} %pad_maximum_fusion.11.matrix_ref) | copy-start | bytes 2359300
  76.8 154.8 %all-gather.19.cloned.1.call-start = ((), (), s32[]{:S(2)}) async-start(), calls=%async_computation.11 | async-start | bytes 9437184 | tf_op jit(solution)/shard_map/all_gather | solution.py:805
  76.9 17.3 %collective-permute-start.1 = (bf16[512,512]{1,0:T(8,128)(2,1)S(1)}, bf16[512,512]{1,0:T(8,128)(2,1)S(1)}, u32[]{:S(2)}, u32[]{:S(2)}) collective-permute-start(bf16[512,512]{1,0:T(8,128)(2,1)S(1)} %copy-done.62), channel_id=1, source_target_pairs={{0,1},{1,0},{2,3},{3,2},{4,5},{5,4},{6,7},{7,6},{8,9},{9,8},{10,11... | collective-permute-start | bytes 1572872 | tf_op jit(solution)/shard_map/ppermute | solution.py:43
  135.2 171.7 %all-gather.21.cloned.1.call-start = ((), (), s32[]{:S(2)}) async-start(), calls=%async_computation.12 | async-start | bytes 9437184 | tf_op jit(solution)/shard_map/all_gather | solution.py:805
  135.8 182.5 %all-gather.23.cloned.1.call-start = ((), (), s32[]{:S(2)}) async-start(), calls=%async_computation.13 | async-start | bytes 9437184 | tf_op jit(solution)/shard_map/all_gather | solution.py:805
  136.4 95.0 %collective-permute-start.4 = (f32[7,512]{1,0:T(8,128)S(1)}, f32[7,512]{1,0:T(8,128)S(1)}, u32[]{:S(2)}, u32[]{:S(2)}) collective-permute-start(f32[7,512]{1,0:T(8,128)S(1)} %get-tuple-element.184), channel_id=1, source_target_pairs={{0,1},{1,0},{2,3},{3,2},{4,5},{5,4},{6,7},{7,6},{8,9},{9,8},{10,11... | collective-permute-start | bytes 43016 | tf_op jit(solution)/shard_map/ppermute | solution.py:43
  152.1 37.3 %collective-permute-start.2 = (bf16[3072,256]{1,0:T(8,128)(2,1)}, bf16[3072,256]{1,0:T(8,128)(2,1)}, u32[]{:S(2)}, u32[]{:S(2)}) collective-permute-start(bf16[3072,256]{1,0:T(8,128)(2,1)} %get-tuple-element.204), channel_id=1, source_target_pairs={{0,8},{2,10},{4,12},{6,14},{8,16},{10,18},{12,20},{14,22},{16,24},... | collective-permute-start | bytes 4718600 | tf_op jit(solution)/shard_map/ppermute | solution.py:52
  156.6 38.2 %collective-permute-start.3 = (bf16[3072,256]{1,0:T(8,128)(2,1)}, bf16[3072,256]{1,0:T(8,128)(2,1)}, u32[]{:S(2)}, u32[]{:S(2)}) collective-permute-start(bf16[3072,256]{1,0:T(8,128)(2,1)} %get-tuple-element.203), channel_id=1, source_target_pairs={{8,0},{10,2},{12,4},{14,6},{16,8},{18,10},{20,12},{22,14},{24,16},... | collective-permute-start | bytes 4718600 | tf_op jit(solution)/shard_map/ppermute | solution.py:52
  227.8 28.8 %all-to-all-start = ((bf16[8,512,128]{2,1,0:T(8,128)(2,1)}), bf16[8,512,128]{2,1,0:T(8,128)(2,1)S(1)}, u32[]{:S(2)}, u32[]{:S(2)}) async-start(bf16[8,512,128]{2,1,0:T(8,128)(2,1)} %bitcast.306), calls=%async_computation | async-start | bytes 2097152 | tf_op jit(solution)/shard_map/all_to_all | solution.py:910
  231.4 148.7 %all-gather.25.cloned.1.call-start = ((), (), s32[]{:S(2)}) async-start(), calls=%async_computation.14 | async-start | bytes 7077888 | tf_op jit(solution)/shard_map/all_gather | solution.py:805
  267.0 6.0 collective-permute-start.6
  268.3 5.9 collective-permute-start.5
  272.9 233.5 %reduce-scatter.4.cloned.1.call-start = ((), (), s32[]{:S(2)}) async-start(), calls=%async_computation.6 | async-start | bytes 18874368 | tf_op jit(solution)/shard_map/reduce_scatter | solution.py:818
  332.2 4.5 collective-permute-start.7
  405.9 6.0 collective-permute-start.9
  407.3 5.9 collective-permute-start.8
  426.6 30.3 %all-to-all-start.1 = ((bf16[8,512,128]{2,1,0:T(8,128)(2,1)}), bf16[8,512,128]{2,1,0:T(8,128)(2,1)}, u32[]{:S(2)}, u32[]{:S(2)}) async-start(bf16[8,512,128]{2,1,0:T(8,128)(2,1)} %bitcast.282), calls=%async_computation.1 | async-start | bytes 2097152 | tf_op jit(solution)/shard_map/all_to_all | solution.py:910
  430.8 196.0 %reduce-scatter.6.cloned.1.call-start = ((), (), s32[]{:S(2)}) async-start(), calls=%async_computation.7 | async-start | bytes 14155776 | tf_op jit(solution)/shard_map/reduce_scatter | solution.py:818
  506.3 41.0 %collective-permute-start.10 = (bf16[3072,256]{1,0:T(8,128)(2,1)}, bf16[3072,256]{1,0:T(8,128)(2,1)S(1)}, u32[]{:S(2)}, u32[]{:S(2)}) collective-permute-start(bf16[3072,256]{1,0:T(8,128)(2,1)} %get-tuple-element.115), channel_id=1, source_target_pairs={{8,0},{10,2},{12,4},{14,6},{16,8},{18,10},{20,12},{22,14},{24,16},... | collective-permute-start | bytes 4718600 | tf_op jit(solution)/shard_map/ppermute | solution.py:52
  507.6 41.0 %collective-permute-start.11 = (bf16[3072,256]{1,0:T(8,128)(2,1)}, bf16[3072,256]{1,0:T(8,128)(2,1)}, u32[]{:S(2)}, u32[]{:S(2)}) collective-permute-start(bf16[3072,256]{1,0:T(8,128)(2,1)} %get-tuple-element.116), channel_id=1, source_target_pairs={{0,8},{2,10},{4,12},{6,14},{8,16},{10,18},{12,20},{14,22},{16,24},... | collective-permute-start | bytes 4718600 | tf_op jit(solution)/shard_map/ppermute | solution.py:52
  557.6 51.9 %all-to-all-start.2 = ((bf16[8,512,384]{2,1,0:T(8,128)(2,1)}), bf16[8,512,384]{2,1,0:T(8,128)(2,1)}, u32[]{:S(2)}, u32[]{:S(2)}) async-start(bf16[8,512,384]{2,1,0:T(8,128)(2,1)} %bitcast.275), calls=%async_computation.3 | async-start | bytes 6291456 | tf_op jit(solution)/shard_map/all_to_all | solution.py:910
  562.1 48.6 %copy-start.17 = (f32[512,1024]{1,0:T(8,128)S(1)}, f32[512,1024]{1,0:T(8,128)}, u32[]{:S(2)}) copy-start(f32[512,1024]{1,0:T(8,128)} %multiply_add_fusion.7) | copy-start | bytes 6291460
  562.1 48.6 %copy-start.68 = (f32[512]{0:T(512)S(1)}, f32[512]{0:T(512)}, u32[]{:S(2)}) copy-start(f32[512]{0:T(512)} %copy-done.67) | copy-start | bytes 6148
  562.1 156.2 %reduce-scatter.8.cloned.1.call-start = ((), (), s32[]{:S(2)}) async-start(), calls=%async_computation.8 | async-start | bytes 5570560 | tf_op jit(solution)/shard_map/reduce_scatter | solution.py:818
  630.6 292.7 %all-gather.27.cloned.1.call-start = ((), (), s32[]{:S(2)}) async-start(), calls=%async_computation.15 | async-start | bytes 18939904 | tf_op jit(solution)/shard_map/all_gather | solution.py:1055
  632.4 25.2 %collective-permute-start.12 = (bf16[512,1024]{1,0:T(8,128)(2,1)S(1)}, bf16[512,1024]{1,0:T(8,128)(2,1)S(1)}, u32[]{:S(2)}, u32[]{:S(2)}) collective-permute-start(bf16[512,1024]{1,0:T(8,128)(2,1)S(1)} %multiply_convert_fusion.6), channel_id=1, source_target_pairs={{0,1},{1,0},{2,3},{3,2},{4,5},{5,4},{6,7},{7,6},{8,9},{9,8},{10,11... | collective-permute-start | bytes 3145736 | tf_op jit(solution)/shard_map/ppermute | solution.py:43
  668.3 24.5 %collective-permute-start.13 = (bf16[512,1024]{1,0:T(8,128)(2,1)S(1)}, bf16[512,1024]{1,0:T(8,128)(2,1)S(1)}, u32[]{:S(2)}, u32[]{:S(2)}) collective-permute-start(bf16[512,1024]{1,0:T(8,128)(2,1)S(1)} %convolution_convert_fusion.2), channel_id=1, source_target_pairs={{0,1},{1,0},{2,3},{3,2},{4,5},{5,4},{6,7},{7,6},{8,9},{9,8},{10,11... | collective-permute-start | bytes 3145736 | tf_op jit(solution)/shard_map/ppermute | solution.py:43
  (113 other events, 733.9 us)
Sparse Core Ops, SparseCore 0:
  13.8 51.4 all-gather.16
  76.9 56.8 all-gather.14
  136.3 54.3 all-gather.18
  193.0 67.2 all-gather.20
  262.0 54.4 all-gather.22
  318.2 45.5 all-gather.24
  380.3 126.0 reduce-scatter.3
  509.8 116.9 reduce-scatter.5
  630.7 87.5 reduce-scatter.7
  719.7 157.6 all-gather.26
